TPU v7x, 32 devices: a whole 2x2x4 slice. The times are simulated.
32 devices in a mesh: groups: 2 (over y), rows: 8 (over z, x), cols: 2 (over core).
Axes of the slice: x: 2, y: 2, z: 4, core: 2. Of those that a mesh axis runs over, the one named last changes fastest.
Arguments:
- snapshots: float32 [16, 24, 16, 256], P(('groups', 'rows'), None, None, 'cols'), parts along dimension 0, as said below
- labels: int32 [16, 24, 16], P(('groups', 'rows')), parts along dimension 0, may hold values from 0 to 7
- conductivity: float32 [16], P('groups'), parts along dimension 0, may hold values from 0.2 to 5
- pairing: int32 [6, 4, 128], replicated, may hold values from 0 to 127, each once within a row
Outputs:
- rotated: float32 [16, 24, 16, 256], P(('groups', 'rows'), None, None, 'cols'), parts along dimension 0
- sigma: float32 [512], P(('groups', 'cols')), parts along dimension 0
There are 2 independent parts, one for each index of `groups`. A program takes and returns all parts, laid end to end along the dimension named above; an argument that names none is the same for every part. Nothing has to cross between parts.
Inputs may be any that keep to these rules, and one draw needn't show every extreme that they name: `snapshots`: real-valued temperature deviations. `pairing`: each row along the last dimension is a permutation; entries 2 j and 2 j + 1 name the two columns of one plane rotation.
All inputs are finite; a program needn't handle non-finite values.
Results may differ from a plain program's by a relative error of at most 0.0003.
Values sent between devices are 32-bit elements; how exact they have to be, the bound alone decides.
No kernel may reach another device: no remote copies, remote signals or barrier semaphores. Data moves between devices by JAX's collectives and lax.ppermute only.
A program may use at most 64 MiB of HBM per device.

v0:
```python
import jax
import jax.numpy as jnp
from jax import lax
from jax.sharding import PartitionSpec as P

HIGHEST_PRECISION = lax.Precision.HIGHEST


def with_halo(cells, sides, width):
    for axis, dim in sides:
        count = lax.axis_size(axis)
        ends = count - 1
        head = lax.slice_in_dim(cells, 0, width, axis=dim)
        tail = lax.slice_in_dim(cells, cells.shape[dim] - width, cells.shape[dim], axis=dim)
        cells = jnp.concatenate(
            [
                lax.ppermute(tail, axis, [(i, (i + 1) % count) for i in range(ends)]),
                cells,
                lax.ppermute(head, axis, [((i + 1) % count, i) for i in range(ends)]),
            ],
            axis=dim,
        )
    return cells


def from_partner(value, axis, apart):
    mask = 2**apart
    pairs = [(source, source ^ mask) for source in range(lax.axis_size(axis))]
    return lax.ppermute(value, axis, pairs)


def contract_rows(left, right):
    return lax.dot_general(
        left,
        right,
        (((0,), (0,)), ((), ())),
        precision=HIGHEST_PRECISION,
        preferred_element_type=jnp.float32,
    )


def rotation_factor(gram_matrix, rounds_pairs):
    pair_width = gram_matrix.shape[0]
    column_ids = jnp.arange(pair_width, dtype=jnp.int32)
    accumulated = jnp.eye(pair_width, dtype=jnp.float32)
    for rotation_round in range(rounds_pairs.shape[0]):
        sel_first = (rounds_pairs[rotation_round, 0::2][:, None] == column_ids[None, :]).astype(
            jnp.float32
        )
        sel_second = (rounds_pairs[rotation_round, 1::2][:, None] == column_ids[None, :]).astype(
            jnp.float32
        )
        diagonal = jnp.diagonal(gram_matrix)
        g_first = jnp.dot(sel_first, diagonal, precision=HIGHEST_PRECISION)
        g_second = jnp.dot(sel_second, diagonal, precision=HIGHEST_PRECISION)
        coupling = jnp.sum(
            jnp.dot(sel_first, gram_matrix, precision=HIGHEST_PRECISION) * sel_second, axis=1
        )
        spread = g_first - g_second
        radius = jnp.sqrt(spread * spread + 4.0 * coupling * coupling)
        tangent = (
            -2.0
            * coupling
            * jnp.sign(spread)
            / (jnp.abs(spread) + radius + 1e-06 * (g_first + g_second + 1.0))
        )
        cosine = 1.0 / jnp.sqrt(1.0 + tangent * tangent)
        sine_term = cosine * tangent
        turn = contract_rows(sel_first * cosine[:, None], sel_first) + contract_rows(
            sel_second * cosine[:, None], sel_second
        )
        turn = (
            turn
            + contract_rows(sel_first * sine_term[:, None], sel_second)
            - contract_rows(sel_second * sine_term[:, None], sel_first)
        )
        gram_matrix = contract_rows(turn, jnp.dot(gram_matrix, turn, precision=HIGHEST_PRECISION))
        accumulated = jnp.dot(accumulated, turn, precision=HIGHEST_PRECISION)
    return (accumulated, gram_matrix)


def differences(values, axis_number):
    padding = [(0, 0)] * values.ndim
    padding[axis_number] = (1, 1)
    padded = jnp.pad(values, padding)
    length = values.shape[axis_number]
    upper_part = lax.slice_in_dim(padded, 2, length + 2, axis=axis_number)
    lower_part = lax.slice_in_dim(padded, 0, length, axis=axis_number)
    return 0.5 * (upper_part - lower_part)


def stencil(values, padded, weight):
    across = 0.5 * (padded[2:] - padded[:-2])
    return jnp.stack(
        [values, weight * across, weight * differences(values, 1), weight * differences(values, 2)]
    )


def shards(snapshots, labels, conductivity, pairing):
    pair_width = snapshots.shape[-1]
    half_width = pair_width // 2
    region_ids = jnp.arange(conductivity.shape[0], dtype=jnp.int32)
    onehot = (labels[..., None] == region_ids).astype(jnp.float32)
    weight = jnp.sqrt(jnp.sum(onehot * conductivity, axis=-1))[..., None]
    first_column = lax.axis_index("cols") == 0
    meetings = pairing.shape[0]
    padded = with_halo(snapshots, (("rows", 0),), 1)
    carried = stencil(snapshots, padded, weight)
    upper_block = carried[..., :half_width]
    lower_block = carried[..., half_width:]
    upper_gram = None
    lower_gram = None
    for meeting in range(meetings):
        pair_block = jnp.concatenate([upper_block, lower_block], axis=-1)
        flat_rows = pair_block.reshape(-1, pair_width)
        gram_matrix = lax.psum(contract_rows(flat_rows, flat_rows), "rows")
        factor, rotated_gram = rotation_factor(gram_matrix, pairing[meeting])
        pair_block = jnp.dot(
            pair_block.reshape(-1, pair_width), factor, precision=HIGHEST_PRECISION
        ).reshape(pair_block.shape)
        upper_block = pair_block[..., :half_width]
        lower_block = pair_block[..., half_width:]
        upper_gram = rotated_gram[:half_width, :half_width]
        lower_gram = rotated_gram[half_width:, half_width:]
        received_block, received_gram = from_partner((lower_block, lower_gram), "cols", 0)
        upper_block, lower_block = (
            jnp.where(first_column, upper_block, received_block),
            jnp.where(first_column, received_block, upper_block),
        )
        upper_gram, lower_gram = (
            jnp.where(first_column, upper_gram, received_gram),
            jnp.where(first_column, received_gram, upper_gram),
        )
    upper_block = upper_block[0]
    lower_block = lower_block[0]
    rotated = jnp.concatenate([upper_block, lower_block], axis=-1)
    sigma = jnp.concatenate(
        [jnp.sqrt(jnp.diagonal(upper_gram)), jnp.sqrt(jnp.diagonal(lower_gram))]
    )
    return (rotated, sigma)


def solution(mesh):
    placed = (
        P(("groups", "rows"), None, None, "cols"),
        P(("groups", "rows"), None, None),
        P("groups"),
        P(),
    )
    return jax.shard_map(
        shards,
        mesh=mesh,
        in_specs=placed,
        out_specs=(P(("groups", "rows"), None, None, "cols"), P(("groups", "cols"))),
        check_vma=False,
    )
```

profile of v0, /device:TPU:0, one launch (start us, length us, event | category | flops | bytes accessed | tf_op | source)
XLA Modules:
  0.0 583.9 jit_solution(8198916625920216826)
XLA Ops:
  9.5 5.5 collective-permute-start.1
  18.0 4.4 collective-permute-done.1
  22.4 2.1 convolution_bitcast_fusion.11
  24.7 69.7 %all-reduce.9.cloned.1.call-done = f32[128,128]{1,0:T(8,128)} async-done(((f32[128,128]{1,0:T(8,128)}), f32[128,128]{1,0:T(8,128)}) %all-reduce.9.cloned.1.call-update) | async-done | bytes 65552 | tf_op jit(solution)/shard_map/psum | solution.py:116
  94.4 1.9 gather_fusion
  112.6 2.3 collective-permute-done.2
  115.1 2.5 convolution_bitcast_fusion.10
  119.1 67.0 %all-reduce.11.cloned.1.call-done = f32[128,128]{1,0:T(8,128)} async-done(((f32[128,128]{1,0:T(8,128)}), f32[128,128]{1,0:T(8,128)}) %all-reduce.11.cloned.1.call-update) | async-done | bytes 65552 | tf_op jit(solution)/shard_map/psum | solution.py:116
  186.2 1.9 gather_fusion.4
  204.5 2.3 collective-permute-done.3
  206.9 2.5 convolution_bitcast_fusion.9
  211.1 66.9 %all-reduce.13.cloned.1.call-done = f32[128,128]{1,0:T(8,128)} async-done(((f32[128,128]{1,0:T(8,128)}), f32[128,128]{1,0:T(8,128)}) %all-reduce.13.cloned.1.call-update) | async-done | bytes 65552 | tf_op jit(solution)/shard_map/psum | solution.py:116
  278.0 1.9 gather_fusion.8
  296.3 2.3 collective-permute-done.4
  298.8 2.5 convolution_bitcast_fusion.8
  302.8 67.1 %all-reduce.15.cloned.1.call-done = f32[128,128]{1,0:T(8,128)} async-done(((f32[128,128]{1,0:T(8,128)}), f32[128,128]{1,0:T(8,128)}) %all-reduce.15.cloned.1.call-update) | async-done | bytes 65552 | tf_op jit(solution)/shard_map/psum | solution.py:116
  369.9 1.9 gather_fusion.12
  388.2 2.3 collective-permute-done.5
  390.6 2.5 convolution_bitcast_fusion.7
  394.4 67.3 %all-reduce.17.cloned.1.call-done = f32[128,128]{1,0:T(8,128)} async-done(((f32[128,128]{1,0:T(8,128)}), f32[128,128]{1,0:T(8,128)}) %all-reduce.17.cloned.1.call-update) | async-done | bytes 65552 | tf_op jit(solution)/shard_map/psum | solution.py:116
  461.7 1.9 gather_fusion.16
  482.7 2.5 convolution_bitcast_fusion.6
  485.3 68.5 %all-reduce.19.cloned.1.call-done = f32[128,128]{1,0:T(8,128)} async-done(((f32[128,128]{1,0:T(8,128)}), f32[128,128]{1,0:T(8,128)}) %all-reduce.19.cloned.1.call-update) | async-done | bytes 65552 | tf_op jit(solution)/shard_map/psum | solution.py:116
  553.8 1.9 gather_fusion.20
  (374 shorter events, 115.9 us)
Async XLA Ops:
  7.2 7.9 %copy-start.6 = (s32[6,4,128]{2,1,0:T(4,128)S(1)}, s32[6,4,128]{2,1,0:T(4,128)}, u32[]{:S(2)}) copy-start(s32[6,4,128]{2,1,0:T(4,128)} %param.7) | copy-start | bytes 36868
  7.2 87.2 %all-reduce.9.cloned.1.call-start = ((), (), s32[]{:S(2)}) async-start(), calls=%async_computation | async-start | bytes 131072 | tf_op jit(solution)/shard_map/psum | solution.py:116
  8.2 9.7 %collective-permute-start = (f32[1,24,16,128]{3,1,2,0:T(8,128)S(1)}, f32[1,24,16,128]{3,1,2,0:T(8,128)S(1)}, u32[]{:S(2)}, u32[]{:S(2)}) collective-permute-start(f32[1,24,16,128]{3,1,2,0:T(8,128)S(1)} %copy.77), channel_id=1, source_target_pairs={{2,0},{4,2},{6,4},{8,6},{10,8},{12,10},{14,12},{3,1},{5,3},{7,5},{... | collective-permute-start | bytes 589832 | tf_op jit(solution)/shard_map/ppermute | solution.py:19
  9.5 12.8 %collective-permute-start.1 = (f32[1,24,16,128]{3,1,2,0:T(8,128)S(1)}, f32[1,24,16,128]{3,1,2,0:T(8,128)S(1)}, u32[]{:S(2)}, u32[]{:S(2)}) collective-permute-start(f32[1,24,16,128]{3,1,2,0:T(8,128)S(1)} %copy.77), channel_id=1, source_target_pairs={{0,2},{2,4},{4,6},{6,8},{8,10},{10,12},{12,14},{1,3},{3,5},{5,7},{... | collective-permute-start | bytes 589832 | tf_op jit(solution)/shard_map/ppermute | solution.py:17
  15.2 1.1 copy-start.7
  16.3 0.7 copy-start.8
  24.6 161.6 %all-reduce.11.cloned.1.call-start = ((), (), s32[]{:S(2)}) async-start(), calls=%async_computation.1 | async-start | bytes 131072 | tf_op jit(solution)/shard_map/psum | solution.py:116
  96.3 0.8 copy-start.4
  112.5 2.3 collective-permute-start.2
  117.6 160.4 %all-reduce.13.cloned.1.call-start = ((), (), s32[]{:S(2)}) async-start(), calls=%async_computation.2 | async-start | bytes 131072 | tf_op jit(solution)/shard_map/psum | solution.py:116
  188.1 0.8 copy-start
  204.4 2.3 collective-permute-start.3
  209.4 160.4 %all-reduce.15.cloned.1.call-start = ((), (), s32[]{:S(2)}) async-start(), calls=%async_computation.3 | async-start | bytes 131072 | tf_op jit(solution)/shard_map/psum | solution.py:116
  280.0 0.8 copy-start.1
  296.2 2.3 collective-permute-start.4
  301.3 160.4 %all-reduce.17.cloned.1.call-start = ((), (), s32[]{:S(2)}) async-start(), calls=%async_computation.4 | async-start | bytes 131072 | tf_op jit(solution)/shard_map/psum | solution.py:116
  371.8 0.8 copy-start.2
  388.1 2.3 collective-permute-start.5
  393.1 160.7 %all-reduce.19.cloned.1.call-start = ((), (), s32[]{:S(2)}) async-start(), calls=%async_computation.5 | async-start | bytes 131072 | tf_op jit(solution)/shard_map/psum | solution.py:116
  463.7 0.8 copy-start.3
  480.2 2.3 collective-permute-start.6
  555.7 0.8 copy-start.5
  571.1 2.4 collective-permute-start.8
  572.9 2.8 collective-permute-start.7
Sparse Core Ops, SparseCore 0:
  24.7 69.6 all-reduce.8
  117.7 68.4 all-reduce.10
  209.5 68.4 all-reduce.12
  301.4 68.4 all-reduce.14
  393.2 68.4 all-reduce.16
  485.3 68.4 all-reduce.18
where the time goes:
time: 593 us; the launch traced here: 584 us
  waiting for transfers between devices  422 us (71%)
  matrix products  83.2 us (14%)
  local copies, waits for them, and re-layouts  51.1 us (9%)
  between operations  16.3 us (3%)
  starting transfers between devices  8.73 us (1%)
    psum x6, waiting for transfers between devices, shards(): gram_matrix = lax.psum(contract_rows(flat_rows, flat_rows), 'rows')  407 us
    dot_general x121, matrix products, contract_rows(): lax.dot_general(left, right, (((0,), (0,)), ((), ())), precision=HIGHEST_...  51.1 us
    gather x24, local copies, waits for them, and re-layouts, rotation_factor(): diagonal = jnp.diagonal(gram_matrix)  34.5 us
  transfers between devices with their start and end apart: 15, of which 13 were waited for; matrix products, arithmetic and copies ran while one was open for 2% of the time, Pallas kernels for 0%

commit v1 on v0

v1 whole, which is shorter than its diff:
```python
import functools

import jax
import jax.numpy as jnp
from jax import lax
from jax.experimental import pallas as pl
from jax.experimental.pallas import tpu as pltpu
from jax.sharding import PartitionSpec as P

HIGHEST = lax.Precision.HIGHEST
VMEM = pl.BlockSpec(memory_space=pltpu.VMEM)
SMEM = pl.BlockSpec(memory_space=pltpu.SMEM)


def dot(left, right, dims=((1,), (0,))):
    return lax.dot_general(
        left, right, (dims, ((), ())), precision=HIGHEST, preferred_element_type=jnp.float32
    )


def local_kernel(stride, own_ref, other_ref, coefs_ref, gram_ref, turned_ref):
    u = own_ref[...]
    rows = u.shape[0]
    coefs = jnp.concatenate([coefs_ref[g].T for g in range(coefs_ref.shape[0])], axis=0)
    applied = coefs[:, 0:1] * u
    for column, step in ((1, 2 * stride), (2, -2 * stride), (3, 2), (4, -2)):
        applied -= coefs[:, column : column + 1] * pltpu.roll(u, (-step) % rows, 0)
    width = u.shape[1]
    turned_ref[:width, :] = u.T
    turned_ref[width:, :] = other_ref[...].T
    gram_ref[...] = dot(turned_ref[...], applied)


def halo_kernel(side_ref, own_ref, halo_ref, coefs_ref, gram_ref, turned_ref, kept_ref, sent_ref):
    coefs = jnp.concatenate([coefs_ref[g].T for g in range(coefs_ref.shape[0])], axis=0)
    applied = coefs[:, 0:1] * own_ref[...] - coefs[:, 1:2] * halo_ref[...]
    gram = gram_ref[...] + dot(turned_ref[...], applied)
    width = own_ref.shape[1]
    half = width // 2
    first = side_ref[0] == 0
    own = gram[:width]
    cross = gram[width:]
    cross = 0.5 * jnp.where(first, cross.T, cross)
    kept_ref[:width, :] = 0.5 * (own + own.T)
    kept_ref[width:, :] = jnp.where(first, cross[:half], cross[half:])
    sent_ref[...] = jnp.where(first, cross[half:], cross[:half])


def lanes(values, index):
    return jnp.take_along_axis(
        values, jnp.broadcast_to(index, values.shape), axis=1, mode="promise_in_bounds"
    )


def rotation(diagonal, opposite, coupling, first):
    g_first = jnp.where(first, diagonal, opposite)
    g_second = jnp.where(first, opposite, diagonal)
    spread = g_first - g_second
    radius = jnp.sqrt(spread * spread + 4.0 * coupling * coupling)
    sign = jnp.where(spread > 0, 1.0, jnp.where(spread < 0, -1.0, 0.0))
    tangent = (
        -2.0 * coupling * sign / (jnp.abs(spread) + radius + 1e-06 * (g_first + g_second + 1.0))
    )
    cosine = 1.0 / jnp.sqrt(1.0 + tangent * tangent)
    sine = cosine * tangent
    return cosine[:1], jnp.where(first, -sine, sine)[:1]


def tournament_kernel(
    meets, turns, side_ref, mine_ref, theirs_ref, partner_ref, first_ref, own_ref, other_ref, rotated_ref, sigma_ref
):
    n = own_ref.shape[1]
    h = n // 2
    side = side_ref[0] == 0
    mine, theirs = mine_ref[...], theirs_ref[...]
    zero_side = jnp.where(side, mine, theirs)
    one_side = jnp.where(side, theirs, mine)
    cross = jnp.concatenate([zero_side[n:], one_side[n:]], axis=0)
    row = lax.broadcasted_iota(jnp.int32, (n, n), 0)
    col = lax.broadcasted_iota(jnp.int32, (n, n), 1)
    eye = row == col
    identity = jnp.where(eye, 1.0, 0.0)
    blank = jnp.zeros((n, h), jnp.float32)
    gram = jnp.concatenate(
        [
            jnp.concatenate([zero_side[:n], cross], axis=1),
            jnp.concatenate([cross.T, one_side[:n]], axis=1),
        ],
        axis=0,
    )
    total = None
    upper, lower = [0, 2], [1, 3]
    for meeting in range(meets):
        met = [gram[:n, :n], gram[n:, n:]]
        factor = [identity, identity]
        for turn in range(turns):
            index = meeting * turns + turn
            partner = partner_ref[index : index + 1, :]
            first = first_ref[index : index + 1, :] > 0
            paired = row == partner
            for d in range(2):
                held = met[d]
                diagonal = jnp.sum(jnp.where(eye, held, 0.0), axis=0, keepdims=True)
                coupling = jnp.sum(jnp.where(paired, held, 0.0), axis=0, keepdims=True)
                diagonal = jnp.broadcast_to(diagonal, (8, n))
                coupling = jnp.broadcast_to(coupling, (8, n))
                cosine, sine = rotation(diagonal, lanes(diagonal, partner), coupling, first)
                held = (held * cosine + lanes(held, partner) * sine).T
                met[d] = held * cosine + lanes(held, partner) * sine
                factor[d] = factor[d] * cosine + lanes(factor[d], partner) * sine
        blocks = {}
        for d in range(2):
            for block, part in ((upper[d], factor[d][:, :h]), (lower[d], factor[d][:, h:])):
                blocks[block] = jnp.concatenate([part, blank] if d == 0 else [blank, part], axis=0)
        if meeting == meets - 1:
            after = range(4)
            norms = {}
            for d in range(2):
                norm = jnp.sqrt(jnp.sum(jnp.where(eye, met[d], 0.0), axis=0, keepdims=True))
                norms[upper[d]], norms[lower[d]] = norm[:, :h], norm[:, h:]
        else:
            upper, lower = [upper[0], lower[0]], [lower[1], upper[1]]
            after = [upper[0], lower[0], upper[1], lower[1]]
        wide = jnp.concatenate([blocks[block] for block in after], axis=1)
        total = wide if total is None else dot(total, wide)
        if meeting < meets - 1:
            gram = dot(wide, dot(gram, wide), ((0,), (0,)))
    picked = jnp.where(side, total[:, :n], total[:, n:])
    near = jnp.where(side, picked[:n], picked[n:])
    far = jnp.where(side, picked[n:], picked[:n])
    rotated_ref[...] = dot(own_ref[...], near) + dot(other_ref[...], far)
    sigma_ref[...] = jnp.where(
        side,
        jnp.concatenate([norms[0], norms[1]], axis=1),
        jnp.concatenate([norms[2], norms[3]], axis=1),
    )


def partners(pairing):
    n = pairing.shape[-1]
    flat = pairing.reshape(-1, n)
    ids = jnp.arange(n, dtype=jnp.int32)
    opposite = flat.reshape(-1, n // 2, 2)[:, :, ::-1].reshape(-1, n)
    here = flat[:, :, None] == ids
    partner = jnp.sum(jnp.where(here, opposite[:, :, None], 0), axis=1)
    first = jnp.sum(jnp.where(here, (1 - (ids & 1))[None, :, None], 0), axis=1)
    return partner, first


def moved(values, dim, step):
    padding = [(0, 0)] * values.ndim
    padding[dim] = (0, step) if step > 0 else (-step, 0)
    start = max(step, 0)
    return lax.slice_in_dim(jnp.pad(values, padding), start, start + values.shape[dim], axis=dim)


def inside(shape, dim, step):
    place = lax.broadcasted_iota(jnp.int32, shape, dim) + step
    return ((place >= 0) & (place < shape[dim])).astype(jnp.float32)


def packed(arrays, width):
    flat = [array.reshape(-1, width) for array in arrays]
    flat += [jnp.zeros_like(flat[0])] * (8 - len(flat))
    return jnp.stack(flat, axis=1)


def shards(snapshots, labels, conductivity, pairing):
    planes, ny, nz, width = snapshots.shape
    cells = planes * ny * nz
    half = width // 2
    count = lax.axis_size("rows")
    own = snapshots.reshape(cells, width)
    halo = lax.ppermute(own, "rows", [(i + 2, i) for i in range(count - 2)])
    other = lax.ppermute(own, "cols", [(0, 1), (1, 0)])

    region_ids = jnp.arange(conductivity.shape[0], dtype=jnp.int32)
    squared = 0.25 * jnp.sum((labels[0][..., None] == region_ids) * conductivity, axis=-1)
    after = lax.ppermute(squared, "rows", [(i + 1, i) for i in range(count - 1)])
    before = lax.ppermute(squared, "rows", [(i, i + 1) for i in range(count - 1)])
    around = [moved(squared, dim, step) for dim in (0, 1) for step in (1, -1)]
    valid = [inside((ny, nz), dim, 2 * step) for dim in (0, 1) for step in (1, -1)]
    local_coefs = packed(
        [1.0 + sum(around)] + [value * keep for value, keep in zip(around, valid)], width
    )
    halo_coefs = packed([after + before, 2.0 * after], width)
    partner, first = partners(pairing)
    side = lax.axis_index("cols").astype(jnp.int32).reshape(1)

    gram, turned = pl.pallas_call(
        functools.partial(local_kernel, nz),
        out_shape=(
            jax.ShapeDtypeStruct((2 * width, width), jnp.float32),
            jax.ShapeDtypeStruct((2 * width, cells), jnp.float32),
        ),
        in_specs=[VMEM] * 3,
        out_specs=[VMEM] * 2,
        cost_estimate=pl.CostEstimate(flops=12 * cells * width * width, bytes_accessed=4 * 6 * cells * width, transcendentals=0),
    )(own, other, local_coefs)
    kept, sent = pl.pallas_call(
        halo_kernel,
        out_shape=(
            jax.ShapeDtypeStruct((width + half, width), jnp.float32),
            jax.ShapeDtypeStruct((half, width), jnp.float32),
        ),
        in_specs=[SMEM] + [VMEM] * 5,
        out_specs=[VMEM] * 2,
    )(side, own, halo, halo_coefs, gram, turned)
    received = lax.ppermute(sent, "cols", [(0, 1), (1, 0)])
    share = jnp.concatenate([kept[:width], kept[width:] + received], axis=0)
    apart = 1
    while apart < count:
        share = share + lax.ppermute(share, "rows", [(i, i ^ apart) for i in range(count)])
        apart *= 2
    theirs = lax.ppermute(share, "cols", [(0, 1), (1, 0)])
    rotated, sigma = pl.pallas_call(
        functools.partial(tournament_kernel, pairing.shape[0], pairing.shape[1]),
        out_shape=(
            jax.ShapeDtypeStruct((cells, width), jnp.float32),
            jax.ShapeDtypeStruct((1, width), jnp.float32),
        ),
        in_specs=[SMEM] + [VMEM] * 6,
        out_specs=[VMEM] * 2,
    )(side, share, theirs, partner, first, own, other)
    return rotated.reshape(snapshots.shape), sigma.reshape(width)


def solution(mesh):
    placed = (
        P(("groups", "rows"), None, None, "cols"),
        P(("groups", "rows"), None, None),
        P("groups"),
        P(),
    )
    return jax.shard_map(
        shards,
        mesh=mesh,
        in_specs=placed,
        out_specs=(P(("groups", "rows"), None, None, "cols"), P(("groups", "cols"))),
        check_vma=False,
    )
```

time: 593 us -> 58.5 us (0.10); the launches traced: 584 us -> 58.1 us
  waiting for transfers between devices: 422 us -> 11.5 us
  matrix products: 83.2 us -> 0 us
  local copies, waits for them, and re-layouts: 51.1 us -> 5.27 us
  Pallas kernels: 0 us -> 21 us
  between operations: 16.3 us -> 0.78 us
  starting transfers between devices: 8.73 us -> 15.1 us
    psum x6 -> x0, waiting for transfers between devices: 407 us -> none  [shards(): gram_matrix = lax.psum(contract_rows(flat_rows, flat_rows), 'rows')]
    dot_general x242 -> x0, matrix products: 83.2 us -> none  [the longest x121 51.1 us: contract_rows(): lax.dot_general(left, right, (((0,), (0,)), ((), ())), precision=HIGHEST_...]
    gather x26 -> x0, local copies, waits for them, and re-layouts: 36.1 us -> none  [the longest x24 34.5 us: rotation_factor(): diagonal = jnp.diagonal(gram_matrix)]
    pallas_call x0 -> x3, Pallas kernels: none -> 21 us  [the longest x1 15.6 us: shards(): pl.pallas_call(functools.partial(tournament_kernel, pairing.shape[0], pai...]
    slice x55 -> x1, local copies, waits for them, and re-layouts: 9.28 us -> 0.85 us  [shards(): share = jnp.concatenate([kept[:width], kept[width:] + received], axis=0)]
    ppermute x9, starting transfers between devices: 7.69 us -> 15.1 us  [the longest x3 6.9 us: shards(): lax.ppermute(share, 'rows', [(i, i ^ apart) for i in range(count)])]
  transfers between devices with their start and end apart: 15 -> 9, of which waited for: 13 -> 5; matrix products, arithmetic and copies ran while one was open for 2% -> 10% of each run, Pallas kernels for 0% -> 5%
where the time goes in v1:
time: 58.5 us; the launch traced here: 58.1 us
  Pallas kernels  21 us (36%)
  starting transfers between devices  15.1 us (26%)
  waiting for transfers between devices  11.5 us (20%)
  local copies, waits for them, and re-layouts  5.27 us (9%)
  other arithmetic  4.4 us (8%)
  between operations  0.78 us (1%)
    pallas_call x1, Pallas kernels, shards(): pl.pallas_call(functools.partial(tournament_kernel, pairing.shape[0], pai...  15.6 us
    ppermute x3, waiting for transfers between devices, shards(): lax.ppermute(share, 'rows', [(i, i ^ apart) for i in range(count)])  8.46 us
    ppermute x3, starting transfers between devices, shards(): lax.ppermute(share, 'rows', [(i, i ^ apart) for i in range(count)])  6.9 us
    ppermute x1, starting transfers between devices, shards(): lax.ppermute(squared, 'rows', [(i, i + 1) for i in range(count - 1)])  5.47 us
    pallas_call x1, Pallas kernels, shards(): pl.pallas_call(halo_kernel, out_shape=(jax.ShapeDtypeStruct((width + half...  2.76 us
    pallas_call x1, Pallas kernels, shards(): pl.pallas_call(functools.partial(local_kernel, nz), out_shape=(jax.ShapeD...  2.66 us
    ppermute x1, waiting for transfers between devices, shards(): halo = lax.ppermute(own, 'rows', [(i + 2, i) for i in range(count - 2)])  2.51 us
    unnamed x11, local copies, waits for them, and re-layouts  2.24 us
  transfers between devices with their start and end apart: 9, of which 5 were waited for; matrix products, arithmetic and copies ran while one was open for 10% of the time, Pallas kernels for 5%

profile of v1, /device:TPU:0, one launch (start us, length us, event | category | flops | bytes accessed | tf_op | source)
XLA Modules:
  0.0 58.1 jit_solution(17334628031152917582)
XLA Ops:
  0.6 0.8 %select_reduce_fusion.2 = f32[24,16]{0,1:T(8,128)S(1)} fusion(f32[8]{0:T(128)} %param.6, s32[24,16]{0,1:T(8,128)} %bitcast.16), kind=kLoop, calls=%fused_computation.4 | loop fusion | flops 8832 | bytes 3104 | tf_op jit(solution)/shard_map/reduce_sum | solution.py:178
  1.4 1.3 %collective-permute-start.1 = (f32[24,16]{0,1:T(8,128)S(1)}, f32[24,16]{0,1:T(8,128)S(1)}, u32[]{:S(2)}, u32[]{:S(2)}) collective-permute-start(f32[24,16]{0,1:T(8,128)S(1)} %broadcast_multiply_fusion.1), channel_id=1, source_target_pairs={{2,0},{4,2},{6,4},{8,6},{10,8},{12,10},{14,12},{3,1},{5,3},{7,5},{... | collective-permute-start | bytes 4616 | tf_op jit(solution)/shard_map/ppermute | solution.py:179
  2.7 5.5 %collective-permute-start.2 = (f32[24,16]{0,1:T(8,128)S(1)}, f32[24,16]{0,1:T(8,128)S(1)}, u32[]{:S(2)}, u32[]{:S(2)}) collective-permute-start(f32[24,16]{0,1:T(8,128)S(1)} %broadcast_multiply_fusion.1), channel_id=1, source_target_pairs={{0,2},{2,4},{4,6},{6,8},{8,10},{10,12},{12,14},{1,3},{3,5},{5,7},{... | collective-permute-start | bytes 4616 | tf_op jit(solution)/shard_map/ppermute | solution.py:180
  8.3 1.3 %collective-permute-start = (f32[384,128]{1,0:T(8,128)}, f32[384,128]{1,0:T(8,128)S(1)}, u32[]{:S(2)}, u32[]{:S(2)}) collective-permute-start(f32[384,128]{1,0:T(8,128)} %bitcast.10), channel_id=1, source_target_pairs={{4,0},{6,2},{8,4},{10,6},{12,8},{14,10},{5,1},{7,3},{9,5},{11,7},{... | collective-permute-start | bytes 589832 | tf_op jit(solution)/shard_map/ppermute | solution.py:174
  10.6 0.6 %stack.11.coefs_ref = f32[3,8,128]{2,1,0:T(8,128)} concatenate(f32[3,1,128]{2,1,0:T(1,128)S(1)} %stack_reshape.30, f32[3,1,128]{2,1,0:T(1,128)S(1)} %stack_reshape.31, f32[3,1,128]{2,1,0:T(1,128)S(1)} %stack_reshape.32, f32[3,1,128]{2,1,0:T(1,128)S(1)} %stack_reshape.33, f32[3,1,128]{2,1,0:T(1,128)S(1)} %stack_reshape.34, f32[3,1,128]{2,1,0:T(1,128)S(1)} %stack_broadcast_in_dim.3, ...), dimensions={1} | concatenate | bytes 24576 | tf_op jit(solution)/shard_map/stack | solution.py:165
  11.6 0.7 %maximum_maximum_fusion.coefs_ref = f32[3,8,128]{2,1,0:T(8,128)} fusion(f32[3,2,128]{2,1,0:T(2,128)S(1)} %broadcast.82, f32[3,1,128]{2,1,0:T(1,128)S(1)} %stack_reshape.29, f32[3,1,128]{2,1,0:T(1,128)S(1)} %stack_reshape.28, f32[8]{0:T(128)S(1)} %pad.25.clone), kind=kLoop, calls=%fused_computation.7 | loop fusion | flops 9216 | bytes 18464 | tf_op jit(solution)/shard_map/stack | solution.py:165
  12.2 0.7 %copy-done = f32[384,128]{1,0:T(8,128)} copy-done((f32[384,128]{1,0:T(8,128)}, f32[384,128]{1,0:T(8,128)S(1)}, u32[]{:S(2)}) %copy-start) | copy-done | bytes 196632
  12.9 2.7 %shard_map.59 = (f32[256,128]{1,0:T(8,128)}, f32[256,384]{1,0:T(8,128)}) custom-call(f32[384,128]{1,0:T(8,128)} %bitcast.11, f32[384,128]{1,0:T(8,128)} %copy-done, f32[3,8,128]{2,1,0:T(8,128)} %stack.11.coefs_ref), custom_call_target="tpu_custom_call" | custom-call | flops 75497472 | bytes 1179648 | tf_op jit(solution)/shard_map/pallas_call | solution.py:190
  15.6 2.5 %collective-permute-done.halo_ref = f32[384,128]{1,0:T(8,128)S(1)} collective-permute-done((f32[384,128]{1,0:T(8,128)}, f32[384,128]{1,0:T(8,128)S(1)}, u32[]{:S(2)}, u32[]{:S(2)}) %collective-permute-start) | collective-permute-done | bytes 196640 | tf_op jit(solution)/shard_map/ppermute | solution.py:174
  18.1 0.7 %copy-done.2 = f32[384,128]{1,0:T(8,128)} copy-done((f32[384,128]{1,0:T(8,128)}, f32[384,128]{1,0:T(8,128)S(1)}, u32[]{:S(2)}) %copy-start.2) | copy-done | bytes 196632
  18.8 2.8 %shard_map.60 = (f32[192,128]{1,0:T(8,128)}, f32[64,128]{1,0:T(8,128)}) custom-call(s32[1]{0:T(128)} %bitcast.side_ref, f32[384,128]{1,0:T(8,128)} %bitcast.12, f32[384,128]{1,0:T(8,128)} %copy-done.2, f32[3,8,128]{2,1,0:T(8,128)} %maximum_maximum_fusion.coefs_ref, f32[256,128]{1,0:T(8,128)} %get-tuple-element.8.gram_ref, f32[256,384]{1,0:T(8,128)} %get-tuple-element.9.turned_ref), custom_call_target="tpu_custom_call" | custom-call | tf_op jit(solution)/shard_map/pallas_call | solution.py:200
  21.5 0.9 %slice.22 = f32[128,128]{1,0:T(8,128)S(1)} slice(f32[192,128]{1,0:T(8,128)} %get-tuple-element.10), slice={[0:128], [0:128]} | slice | bytes 131072 | tf_op jit(solution)/shard_map/slice | solution.py:210
  22.4 0.6 collective-permute-done.4
  22.9 0.8 %slice_add_fusion = f32[64,128]{1,0:T(8,128)S(1)} fusion(f32[64,128]{1,0:T(8,128)S(1)} %collective-permute-done.4, f32[192,128]{1,0:T(8,128)} %get-tuple-element.10), kind=kLoop, calls=%fused_computation.6 | loop fusion | flops 8192 | bytes 98304 | tf_op jit(solution)/shard_map/add | solution.py:210
  23.7 2.6 %collective-permute-start.5 = (f32[192,128]{1,0:T(8,128)S(1)}, f32[192,128]{1,0:T(8,128)S(1)}, u32[]{:S(2)}, u32[]{:S(2)}) collective-permute-start(f32[192,128]{1,0:T(8,128)S(1)} %pad_maximum_fusion), channel_id=1, source_target_pairs={{0,2},{2,0},{4,6},{6,4},{8,10},{10,8},{12,14},{14,12},{1,3},{3,1},... | collective-permute-start | bytes 294920 | tf_op jit(solution)/shard_map/ppermute | solution.py:213
  26.3 3.1 %collective-permute-done.5 = f32[192,128]{1,0:T(8,128)S(1)} collective-permute-done((f32[192,128]{1,0:T(8,128)S(1)}, f32[192,128]{1,0:T(8,128)S(1)}, u32[]{:S(2)}, u32[]{:S(2)}) %collective-permute-start.5) | collective-permute-done | bytes 98336 | tf_op jit(solution)/shard_map/ppermute | solution.py:213
  29.5 1.6 %collective-permute-start.6 = (f32[192,128]{1,0:T(8,128)S(1)}, f32[192,128]{1,0:T(8,128)S(1)}, u32[]{:S(2)}, u32[]{:S(2)}) collective-permute-start(f32[192,128]{1,0:T(8,128)S(1)} %fusion.4), channel_id=1, source_target_pairs={{0,4},{2,6},{4,0},{6,2},{8,12},{10,14},{12,8},{14,10},{1,5},{3,7},... | collective-permute-start | bytes 294920 | tf_op jit(solution)/shard_map/ppermute | solution.py:213
  31.1 0.3 copy.31
  31.8 2.4 %collective-permute-done.6 = f32[192,128]{1,0:T(8,128)S(1)} collective-permute-done((f32[192,128]{1,0:T(8,128)S(1)}, f32[192,128]{1,0:T(8,128)S(1)}, u32[]{:S(2)}, u32[]{:S(2)}) %collective-permute-start.6) | collective-permute-done | bytes 98336 | tf_op jit(solution)/shard_map/ppermute | solution.py:213
  34.2 2.6 %collective-permute-start.7 = (f32[192,128]{1,0:T(8,128)S(1)}, f32[192,128]{1,0:T(8,128)S(1)}, u32[]{:S(2)}, u32[]{:S(2)}) collective-permute-start(f32[192,128]{1,0:T(8,128)S(1)} %add.66), channel_id=1, source_target_pairs={{0,8},{2,10},{4,12},{6,14},{8,0},{10,2},{12,4},{14,6},{1,9},{3,11}... | collective-permute-start | bytes 294920 | tf_op jit(solution)/shard_map/ppermute | solution.py:213
  36.8 2.9 %collective-permute-done.7 = f32[192,128]{1,0:T(8,128)S(1)} collective-permute-done((f32[192,128]{1,0:T(8,128)S(1)}, f32[192,128]{1,0:T(8,128)S(1)}, u32[]{:S(2)}, u32[]{:S(2)}) %collective-permute-start.7) | collective-permute-done | bytes 98336 | tf_op jit(solution)/shard_map/ppermute | solution.py:213
  39.9 2.0 %select_reduce_fusion = (s32[24,128]{1,0:T(8,128)}, s32[24,128]{1,0:T(8,128)}) fusion(s32[128]{0:T(128)S(1)} %and_subtract_fusion, s32[24,128]{1,0:T(8,128)S(1)} %bitcast.15, s32[24,128]{1,0:T(8,128)S(1)} %copy.32), kind=kLoop, calls=%fused_computation | loop fusion | flops 1959936 | bytes 49664 | tf_op jit(solution)/shard_map/reduce_sum | solution.py:146
  41.9 0.6 %copy-done.3 = f32[192,128]{1,0:T(8,128)} copy-done((f32[192,128]{1,0:T(8,128)}, f32[192,128]{1,0:T(8,128)S(1)}, u32[]{:S(2)}) %copy-start.3) | copy-done | bytes 98328
  42.5 15.6 %shard_map.61 = (f32[384,128]{1,0:T(8,128)}, f32[1,128]{1,0:T(1,128)}) custom-call(s32[1]{0:T(128)} %bitcast.side_ref, f32[192,128]{1,0:T(8,128)} %copy-done.1, f32[192,128]{1,0:T(8,128)} %copy-done.3, s32[24,128]{1,0:T(8,128)} %get-tuple-element.15.partner_ref, s32[24,128]{1,0:T(8,128)} %get-tuple-element.14.first_ref, f32[384,128]{1,0:T(8,128)} %bitcast.13, ...), custom_call_target="tpu_custom_call" | custom-call | tf_op jit(solution)/shard_map/pallas_call | solution.py:216
  (45 shorter events, 1.9 us)
Async XLA Ops:
  1.4 9.8 %collective-permute-start.1 = (f32[24,16]{0,1:T(8,128)S(1)}, f32[24,16]{0,1:T(8,128)S(1)}, u32[]{:S(2)}, u32[]{:S(2)}) collective-permute-start(f32[24,16]{0,1:T(8,128)S(1)} %broadcast_multiply_fusion.1), channel_id=1, source_target_pairs={{2,0},{4,2},{6,4},{8,6},{10,8},{12,10},{14,12},{3,1},{5,3},{7,5},{... | collective-permute-start | bytes 4616 | tf_op jit(solution)/shard_map/ppermute | solution.py:179
  2.7 8.5 %collective-permute-start.2 = (f32[24,16]{0,1:T(8,128)S(1)}, f32[24,16]{0,1:T(8,128)S(1)}, u32[]{:S(2)}, u32[]{:S(2)}) collective-permute-start(f32[24,16]{0,1:T(8,128)S(1)} %broadcast_multiply_fusion.1), channel_id=1, source_target_pairs={{0,2},{2,4},{4,6},{6,8},{8,10},{10,12},{12,14},{1,3},{3,5},{5,7},{... | collective-permute-start | bytes 4616 | tf_op jit(solution)/shard_map/ppermute | solution.py:180
  8.2 4.0 %collective-permute-start.3 = (f32[384,128]{1,0:T(8,128)}, f32[384,128]{1,0:T(8,128)S(1)}, u32[]{:S(2)}, u32[]{:S(2)}) collective-permute-start(f32[384,128]{1,0:T(8,128)} %bitcast.9), channel_id=1, source_target_pairs={{0,1},{1,0},{2,3},{3,2},{4,5},{5,4},{6,7},{7,6},{8,9},{9,8},{10,11... | collective-permute-start | bytes 589832 | tf_op jit(solution)/shard_map/ppermute | solution.py:175
  8.3 9.8 %collective-permute-start = (f32[384,128]{1,0:T(8,128)}, f32[384,128]{1,0:T(8,128)S(1)}, u32[]{:S(2)}, u32[]{:S(2)}) collective-permute-start(f32[384,128]{1,0:T(8,128)} %bitcast.10), channel_id=1, source_target_pairs={{4,0},{6,2},{8,4},{10,6},{12,8},{14,10},{5,1},{7,3},{9,5},{11,7},{... | collective-permute-start | bytes 589832 | tf_op jit(solution)/shard_map/ppermute | solution.py:174
  12.2 0.7 %copy-start = (f32[384,128]{1,0:T(8,128)}, f32[384,128]{1,0:T(8,128)S(1)}, u32[]{:S(2)}) copy-start(f32[384,128]{1,0:T(8,128)S(1)} %collective-permute-done.3.other_ref) | copy-start | bytes 589828
  18.1 0.7 %copy-start.2 = (f32[384,128]{1,0:T(8,128)}, f32[384,128]{1,0:T(8,128)S(1)}, u32[]{:S(2)}) copy-start(f32[384,128]{1,0:T(8,128)S(1)} %collective-permute-done.halo_ref) | copy-start | bytes 589828
  21.5 9.6 %copy-start.4 = (s32[6,4,128]{2,1,0:T(4,128)S(1)}, s32[6,4,128]{2,1,0:T(4,128)}, u32[]{:S(2)}) copy-start(s32[6,4,128]{2,1,0:T(4,128)} %param.7) | copy-start | bytes 36868
  21.5 1.4 %collective-permute-start.4 = (f32[64,128]{1,0:T(8,128)}, f32[64,128]{1,0:T(8,128)S(1)}, u32[]{:S(2)}, u32[]{:S(2)}) collective-permute-start(f32[64,128]{1,0:T(8,128)} %get-tuple-element.11), channel_id=1, source_target_pairs={{0,1},{1,0},{2,3},{3,2},{4,5},{5,4},{6,7},{7,6},{8,9},{9,8},{10,11... | collective-permute-start | bytes 98312 | tf_op jit(solution)/shard_map/ppermute | solution.py:209
  23.7 5.7 %collective-permute-start.5 = (f32[192,128]{1,0:T(8,128)S(1)}, f32[192,128]{1,0:T(8,128)S(1)}, u32[]{:S(2)}, u32[]{:S(2)}) collective-permute-start(f32[192,128]{1,0:T(8,128)S(1)} %pad_maximum_fusion), channel_id=1, source_target_pairs={{0,2},{2,0},{4,6},{6,4},{8,10},{10,8},{12,14},{14,12},{1,3},{3,1},... | collective-permute-start | bytes 294920 | tf_op jit(solution)/shard_map/ppermute | solution.py:213
  29.5 4.7 %collective-permute-start.6 = (f32[192,128]{1,0:T(8,128)S(1)}, f32[192,128]{1,0:T(8,128)S(1)}, u32[]{:S(2)}, u32[]{:S(2)}) collective-permute-start(f32[192,128]{1,0:T(8,128)S(1)} %fusion.4), channel_id=1, source_target_pairs={{0,4},{2,6},{4,0},{6,2},{8,12},{10,14},{12,8},{14,10},{1,5},{3,7},... | collective-permute-start | bytes 294920 | tf_op jit(solution)/shard_map/ppermute | solution.py:213
  34.2 5.6 %collective-permute-start.7 = (f32[192,128]{1,0:T(8,128)S(1)}, f32[192,128]{1,0:T(8,128)S(1)}, u32[]{:S(2)}, u32[]{:S(2)}) collective-permute-start(f32[192,128]{1,0:T(8,128)S(1)} %add.66), channel_id=1, source_target_pairs={{0,8},{2,10},{4,12},{6,14},{8,0},{10,2},{12,4},{14,6},{1,9},{3,11}... | collective-permute-start | bytes 294920 | tf_op jit(solution)/shard_map/ppermute | solution.py:213
  39.8 2.1 %copy-start.1 = (f32[192,128]{1,0:T(8,128)}, f32[192,128]{1,0:T(8,128)S(1)}, u32[]{:S(2)}) copy-start(f32[192,128]{1,0:T(8,128)S(1)} %add.67.mine_ref) | copy-start | bytes 294916
  39.8 2.1 %collective-permute-start.8 = (f32[192,128]{1,0:T(8,128)S(1)}, f32[192,128]{1,0:T(8,128)S(1)}, u32[]{:S(2)}, u32[]{:S(2)}) collective-permute-start(f32[192,128]{1,0:T(8,128)S(1)} %add.67.mine_ref), channel_id=1, source_target_pairs={{0,1},{1,0},{2,3},{3,2},{4,5},{5,4},{6,7},{7,6},{8,9},{9,8},{10,11... | collective-permute-start | bytes 294920 | tf_op jit(solution)/shard_map/ppermute | solution.py:215
  41.9 0.6 %copy-start.3 = (f32[192,128]{1,0:T(8,128)}, f32[192,128]{1,0:T(8,128)S(1)}, u32[]{:S(2)}) copy-start(f32[192,128]{1,0:T(8,128)S(1)} %collective-permute-done.8.theirs_ref) | copy-start | bytes 294916

commit v2 on v1

v2 whole, which is shorter than its diff:
```python
import functools

import jax
import jax.numpy as jnp
from jax import lax
from jax.experimental import pallas as pl
from jax.experimental.pallas import tpu as pltpu
from jax.sharding import PartitionSpec as P

HIGHEST = lax.Precision.HIGHEST
PARAMS = pltpu.CompilerParams(vmem_limit_bytes=16 * 2**20)
VMEM = pl.BlockSpec(memory_space=pltpu.VMEM)
SMEM = pl.BlockSpec(memory_space=pltpu.SMEM)


def dot(left, right, dims=((1,), (0,))):
    return lax.dot_general(
        left, right, (dims, ((), ())), precision=HIGHEST, preferred_element_type=jnp.float32
    )


def lanes(values, index):
    return jnp.take_along_axis(
        values, jnp.broadcast_to(index, values.shape), axis=1, mode="promise_in_bounds"
    )


def code_kernel(pairing_ref, code_ref):
    meets, turns, n = pairing_ref.shape
    pairs = jnp.concatenate([pairing_ref[m] for m in range(meets)], axis=0)
    place = lax.broadcasted_iota(jnp.int32, pairs.shape, 1)
    told = lanes(pairs, place ^ 1) + jnp.where(place % 2 == 0, n, 0)
    pairs = pairs.astype(jnp.float32).T
    told = told.astype(jnp.float32).T
    col = lax.broadcasted_iota(jnp.int32, (n, n), 1).astype(jnp.float32)
    rows = []
    for index in range(meets * turns):
        here = pairs[:, index : index + 1] == col
        rows.append(jnp.sum(jnp.where(here, told[:, index : index + 1], 0.0), axis=0, keepdims=True))
    code_ref[...] = jnp.concatenate(rows, axis=0).astype(jnp.int32)


def quarter_squares(labels, conductivity_ref):
    labels = labels.T
    squares = jnp.zeros(labels.shape, jnp.float32)
    for region in range(conductivity_ref.shape[0]):
        squares = jnp.where(labels == region, conductivity_ref[region], squares)
    return 0.25 * squares


def local_kernel(conductivity_ref, own_ref, other_ref, labels_ref, gram_ref, turned_ref, applied_ref):
    ny, nz, width = own_ref.shape
    squares = quarter_squares(labels_ref[...], conductivity_ref)
    z = lax.broadcasted_iota(jnp.int32, (nz, ny), 0)
    above = jnp.where(z < nz - 1, pltpu.roll(squares, nz - 1, 0), 0.0)
    below = jnp.where(z > 0, pltpu.roll(squares, 1, 0), 0.0)
    inner = 1.0 + above + below
    above = jnp.where(z < nz - 2, above, 0.0)
    below = jnp.where(z > 1, below, 0.0)
    for y in range(ny):
        u = own_ref[y]
        scale = inner[:, y : y + 1]
        if y > 0:
            scale += squares[:, y - 1 : y]
        if y < ny - 1:
            scale += squares[:, y + 1 : y + 2]
        total = scale * u
        if y > 1:
            total -= squares[:, y - 1 : y] * own_ref[y - 2]
        if y < ny - 2:
            total -= squares[:, y + 1 : y + 2] * own_ref[y + 2]
        total -= above[:, y : y + 1] * pltpu.roll(u, nz - 2, 0)
        total -= below[:, y : y + 1] * pltpu.roll(u, 2, 0)
        applied_ref[y * nz : (y + 1) * nz, :] = total
    turned_ref[:width, :] = own_ref[...].reshape(ny * nz, width).T
    turned_ref[width:, :] = other_ref[...].reshape(ny * nz, width).T
    gram_ref[...] = dot(turned_ref[...], applied_ref[...])


def halo_kernel(
    place_ref, conductivity_ref, own_ref, halo_ref, after_ref, before_ref, gram_ref, turned_ref,
    kept_ref, sent_ref, applied_ref,
):
    ny, nz, width = own_ref.shape
    after = quarter_squares(after_ref[...], conductivity_ref)
    before = quarter_squares(before_ref[...], conductivity_ref)
    after = jnp.where(place_ref[1] < place_ref[2] - 1, after, 0.0)
    before = jnp.where(place_ref[1] > 0, before, 0.0)
    for y in range(ny):
        ahead = after[:, y : y + 1]
        applied_ref[y * nz : (y + 1) * nz, :] = (ahead + before[:, y : y + 1]) * own_ref[y] - (
            2.0 * ahead
        ) * halo_ref[y]
    gram = gram_ref[...] + dot(turned_ref[...], applied_ref[...])
    half = width // 2
    first = place_ref[0] == 0
    own = gram[:width]
    cross = gram[width:]
    cross = 0.5 * jnp.where(first, cross.T, cross)
    kept_ref[:width, :] = 0.5 * (own + own.T)
    kept_ref[width:, :] = jnp.where(first, cross[:half], cross[half:])
    sent_ref[...] = jnp.where(first, cross[half:], cross[:half])


def rotation(diagonal, opposite, coupling, first):
    g_first = jnp.where(first, diagonal, opposite)
    g_second = jnp.where(first, opposite, diagonal)
    spread = g_first - g_second
    radius = jnp.sqrt(spread * spread + 4.0 * coupling * coupling)
    sign = jnp.where(spread > 0, 1.0, jnp.where(spread < 0, -1.0, 0.0))
    tangent = (
        -2.0 * coupling * sign / (jnp.abs(spread) + radius + 1e-06 * (g_first + g_second + 1.0))
    )
    cosine = 1.0 / jnp.sqrt(1.0 + tangent * tangent)
    sine = cosine * tangent
    return cosine[:1], jnp.where(first, -sine, sine)[:1]


def tournament_kernel(
    meets, turns, place_ref, mine_ref, theirs_ref, code_ref, own_ref, other_ref, rotated_ref, sigma_ref
):
    n = own_ref.shape[2]
    h = n // 2
    side = place_ref[0] == 0
    mine, theirs = mine_ref[...], theirs_ref[...]
    zero_side = jnp.where(side, mine, theirs)
    one_side = jnp.where(side, theirs, mine)
    cross = jnp.concatenate([zero_side[n:], one_side[n:]], axis=0)
    row = lax.broadcasted_iota(jnp.int32, (n, n), 0)
    col = lax.broadcasted_iota(jnp.int32, (n, n), 1)
    eye = row == col
    identity = jnp.where(eye, 1.0, 0.0)
    blank = jnp.zeros((n, h), jnp.float32)
    gram = jnp.concatenate(
        [
            jnp.concatenate([zero_side[:n], cross], axis=1),
            jnp.concatenate([cross.T, one_side[:n]], axis=1),
        ],
        axis=0,
    )
    total = None
    upper, lower = [0, 2], [1, 3]
    for meeting in range(meets):
        met = [gram[:n, :n], gram[n:, n:]]
        factor = [identity, identity]
        for turn in range(turns):
            index = meeting * turns + turn
            told = code_ref[index : index + 1, :]
            partner = told % n
            first = told >= n
            paired = row == partner
            for d in range(2):
                held = met[d]
                diagonal = jnp.sum(jnp.where(eye, held, 0.0), axis=0, keepdims=True)
                coupling = jnp.sum(jnp.where(paired, held, 0.0), axis=0, keepdims=True)
                diagonal = jnp.broadcast_to(diagonal, (8, n))
                coupling = jnp.broadcast_to(coupling, (8, n))
                cosine, sine = rotation(diagonal, lanes(diagonal, partner), coupling, first)
                held = (held * cosine + lanes(held, partner) * sine).T
                met[d] = held * cosine + lanes(held, partner) * sine
                factor[d] = factor[d] * cosine + lanes(factor[d], partner) * sine
        blocks = {}
        for d in range(2):
            for block, part in ((upper[d], factor[d][:, :h]), (lower[d], factor[d][:, h:])):
                blocks[block] = jnp.concatenate([part, blank] if d == 0 else [blank, part], axis=0)
        if meeting == meets - 1:
            after = range(4)
            norms = {}
            for d in range(2):
                norm = jnp.sqrt(jnp.sum(jnp.where(eye, met[d], 0.0), axis=0, keepdims=True))
                norms[upper[d]], norms[lower[d]] = norm[:, :h], norm[:, h:]
        else:
            upper, lower = [upper[0], lower[0]], [lower[1], upper[1]]
            after = [upper[0], lower[0], upper[1], lower[1]]
        wide = jnp.concatenate([blocks[block] for block in after], axis=1)
        total = wide if total is None else dot(total, wide)
        if meeting < meets - 1:
            gram = dot(wide, dot(gram, wide), ((0,), (0,)))
    picked = jnp.where(side, total[:, :n], total[:, n:])
    near = jnp.where(side, picked[:n], picked[n:])
    far = jnp.where(side, picked[n:], picked[:n])
    flat = (-1, n)
    rotated = dot(own_ref[...].reshape(flat), near) + dot(other_ref[...].reshape(flat), far)
    rotated_ref[...] = rotated.reshape(rotated_ref.shape)
    sigma_ref[...] = jnp.where(
        side,
        jnp.concatenate([norms[0], norms[1]], axis=1),
        jnp.concatenate([norms[2], norms[3]], axis=1),
    )


def shards(snapshots, labels, conductivity, pairing):
    planes, ny, nz, width = snapshots.shape
    cells = planes * ny * nz
    half = width // 2
    count = lax.axis_size("rows")
    swap = [(0, 1), (1, 0)]
    own = snapshots[0]
    labels = labels[0]
    halo = lax.ppermute(own, "rows", [(i + 2, i) for i in range(count - 2)])
    other = lax.ppermute(own, "cols", swap)
    after = lax.ppermute(labels, "rows", [(i + 1, i) for i in range(count - 1)])
    before = lax.ppermute(labels, "rows", [(i, i + 1) for i in range(count - 1)])
    place = jnp.stack(
        [lax.axis_index("cols"), lax.axis_index("rows"), jnp.asarray(count, jnp.int32)]
    ).astype(jnp.int32)

    code = pl.pallas_call(
        code_kernel,
        out_shape=jax.ShapeDtypeStruct((pairing.shape[0] * pairing.shape[1], width), jnp.int32),
        in_specs=[VMEM],
        out_specs=VMEM,
        compiler_params=PARAMS,
    )(pairing)
    gram, turned = pl.pallas_call(
        local_kernel,
        out_shape=(
            jax.ShapeDtypeStruct((2 * width, width), jnp.float32),
            jax.ShapeDtypeStruct((2 * width, cells), jnp.float32),
        ),
        in_specs=[SMEM] + [VMEM] * 3,
        out_specs=[VMEM] * 2,
        scratch_shapes=[pltpu.VMEM((cells, width), jnp.float32)],
        compiler_params=PARAMS,
    )(conductivity, own, other, labels)
    kept, sent = pl.pallas_call(
        halo_kernel,
        out_shape=(
            jax.ShapeDtypeStruct((width + half, width), jnp.float32),
            jax.ShapeDtypeStruct((half, width), jnp.float32),
        ),
        in_specs=[SMEM] * 2 + [VMEM] * 6,
        out_specs=[VMEM] * 2,
        scratch_shapes=[pltpu.VMEM((cells, width), jnp.float32)],
        compiler_params=PARAMS,
    )(place, conductivity, own, halo, after, before, gram, turned)
    received = lax.ppermute(sent, "cols", swap)
    share = jnp.concatenate([kept[:width], kept[width:] + received], axis=0)
    apart = 1
    while apart < count:
        share = share + lax.ppermute(share, "rows", [(i, i ^ apart) for i in range(count)])
        apart *= 2
    theirs = lax.ppermute(share, "cols", swap)
    rotated, sigma = pl.pallas_call(
        functools.partial(tournament_kernel, pairing.shape[0], pairing.shape[1]),
        out_shape=(
            jax.ShapeDtypeStruct((ny, nz, width), jnp.float32),
            jax.ShapeDtypeStruct((1, width), jnp.float32),
        ),
        in_specs=[SMEM] + [VMEM] * 5,
        out_specs=[VMEM] * 2,
        compiler_params=PARAMS,
    )(place, share, theirs, code, own, other)
    return rotated.reshape(snapshots.shape), sigma.reshape(width)


def solution(mesh):
    placed = (
        P(("groups", "rows"), None, None, "cols"),
        P(("groups", "rows"), None, None),
        P("groups"),
        P(),
    )
    return jax.shard_map(
        shards,
        mesh=mesh,
        in_specs=placed,
        out_specs=(P(("groups", "rows"), None, None, "cols"), P(("groups", "cols"))),
        check_vma=False,
    )
```

time: 58.5 us -> 49.5 us (0.85)
  other arithmetic: 4.4 us -> 0.13 us
  local copies, waits for them, and re-layouts: 5.27 us -> 2.28 us
  starting transfers between devices: 15.1 us -> 17.4 us
  Pallas kernels: 21 us -> 18.9 us
  waiting for transfers between devices: 11.5 us -> 9.55 us
    reduce_sum x2 -> x0, other arithmetic: 2.8 us -> none  [the longest x1 1.99 us: partners(): first = jnp.sum(jnp.where(here, (1 - (ids & 1))[None, :, None], 0), axis=1)]
    ppermute x1, waiting for transfers between devices: 2.51 us -> 0.01 us  [shards(): halo = lax.ppermute(own, 'rows', [(i + 2, i) for i in range(count - 2)])]
    ppermute x3, starting transfers between devices: 6.9 us -> 8.94 us  [shards(): lax.ppermute(share, 'rows', [(i, i ^ apart) for i in range(count)])]
    another operation x13 -> x0, local copies, waits for them, and re-layouts: 1.47 us -> none  [the longest x11 1.29 us: packed(): return jnp.stack(flat, axis=1)]
    pallas_call x1, Pallas kernels: 2.76 us -> 1.33 us  [shards(): pl.pallas_call(halo_kernel, out_shape=(jax.ShapeDtypeStruct((width + half...]
    slice x1, local copies, waits for them, and re-layouts: 0.85 us -> 0.01 us  [shards(): share = jnp.concatenate([kept[:width], kept[width:] + received], axis=0)]
    add x1, other arithmetic: 0.77 us -> 0.01 us  [shards(): share = jnp.concatenate([kept[:width], kept[width:] + received], axis=0)]
    ppermute x5, waiting for transfers between devices: 0.57 us -> 1.22 us  [the longest x1 1 us: shards(): received = lax.ppermute(sent, 'cols', swap)]
  transfers between devices with their start and end apart: 9 -> 9, of which waited for: 5 -> 5; matrix products, arithmetic and copies ran while one was open for 10% -> 2% of each run, Pallas kernels for 5% -> 5%
where the time goes in v2:
time: 49.5 us; the launch traced here: 49 us
  Pallas kernels  18.9 us (38%)
  starting transfers between devices  17.4 us (35%)
  waiting for transfers between devices  9.55 us (19%)
  local copies, waits for them, and re-layouts  2.28 us (5%)
  between operations  0.76 us (2%)
    pallas_call x1, Pallas kernels, shards(): pl.pallas_call(functools.partial(tournament_kernel, pairing.shape[0], pai...  15 us
    ppermute x3, starting transfers between devices, shards(): lax.ppermute(share, 'rows', [(i, i ^ apart) for i in range(count)])  8.94 us
    ppermute x3, waiting for transfers between devices, shards(): lax.ppermute(share, 'rows', [(i, i ^ apart) for i in range(count)])  8.33 us
    ppermute x1, starting transfers between devices, shards(): lax.ppermute(labels, 'rows', [(i, i + 1) for i in range(count - 1)])  5.05 us
    unnamed x9, local copies, waits for them, and re-layouts  2.28 us
    pallas_call x1, Pallas kernels, shards(): pl.pallas_call(local_kernel, out_shape=(jax.ShapeDtypeStruct((2 * width,...  1.48 us
    pallas_call x1, Pallas kernels, shards(): pl.pallas_call(halo_kernel, out_shape=(jax.ShapeDtypeStruct((width + half...  1.33 us
    ppermute x1, starting transfers between devices, shards(): after = lax.ppermute(labels, 'rows', [(i + 1, i) for i in range(count - 1)])  1.28 us
  transfers between devices with their start and end apart: 9, of which 5 were waited for; matrix products, arithmetic and copies ran while one was open for 2% of the time, Pallas kernels for 5%

profile of v2, /device:TPU:0, one launch (start us, length us, event | category | flops | bytes accessed | tf_op | source)
XLA Modules:
  0.0 49.0 jit_solution(6513184972813933221)
XLA Ops:
  0.6 0.5 %collective-permute-start.3 = (f32[24,16,128]{2,1,0:T(8,128)}, f32[24,16,128]{2,1,0:T(8,128)S(1)}, u32[]{:S(2)}, u32[]{:S(2)}) collective-permute-start(f32[24,16,128]{2,1,0:T(8,128)} %bitcast.6), channel_id=1, source_target_pairs={{0,1},{1,0},{2,3},{3,2},{4,5},{5,4},{6,7},{7,6},{8,9},{9,8},{10,11... | collective-permute-start | bytes 589832 | tf_op jit(solution)/shard_map/ppermute | solution.py:201
  1.1 1.3 %collective-permute-start = (f32[24,16,128]{2,1,0:T(8,128)}, f32[24,16,128]{2,1,0:T(8,128)S(1)}, u32[]{:S(2)}, u32[]{:S(2)}) collective-permute-start(f32[24,16,128]{2,1,0:T(8,128)} %bitcast.7), channel_id=1, source_target_pairs={{4,0},{6,2},{8,4},{10,6},{12,8},{14,10},{5,1},{7,3},{9,5},{11,7},{... | collective-permute-start | bytes 589832 | tf_op jit(solution)/shard_map/ppermute | solution.py:200
  2.4 0.8 %copy.6 = s32[1,24,16]{2,1,0:T(8,128)S(1)} copy(s32[1,24,16]{1,2,0:T(8,128)} %param.5) | data formatting | bytes 3072 | tf_op args[1]
  3.2 1.3 %collective-permute-start.1 = (s32[24,16]{1,0:T(8,128)S(1)}, s32[24,16]{1,0:T(8,128)S(1)}, u32[]{:S(2)}, u32[]{:S(2)}) collective-permute-start(s32[24,16]{1,0:T(8,128)S(1)} %bitcast.11), channel_id=1, source_target_pairs={{2,0},{4,2},{6,4},{8,6},{10,8},{12,10},{14,12},{3,1},{5,3},{7,5},{... | collective-permute-start | bytes 4616 | tf_op jit(solution)/shard_map/ppermute | solution.py:202
  4.5 5.0 %collective-permute-start.2 = (s32[24,16]{1,0:T(8,128)S(1)}, s32[24,16]{1,0:T(8,128)S(1)}, u32[]{:S(2)}, u32[]{:S(2)}) collective-permute-start(s32[24,16]{1,0:T(8,128)S(1)} %bitcast.12), channel_id=1, source_target_pairs={{0,2},{2,4},{4,6},{6,8},{8,10},{10,12},{12,14},{1,3},{3,5},{5,7},{... | collective-permute-start | bytes 4616 | tf_op jit(solution)/shard_map/ppermute | solution.py:203
  9.6 0.0 copy-start.3
  9.6 0.1 pad_add_fusion.place_ref
  9.6 0.6 %copy-done.3 = f32[8]{0:T(128)S(1)} copy-done((f32[8]{0:T(128)S(1)}, f32[8]{0:T(128)}, u32[]{:S(2)}) %copy-start.3) | copy-done | bytes 56
  10.2 0.9 %copy-done = f32[1,24,16,128]{3,2,1,0:T(8,128)S(1)} copy-done((f32[1,24,16,128]{3,2,1,0:T(8,128)S(1)}, f32[1,24,16,128]{3,2,1,0:T(8,128)}, u32[]{:S(2)}) %copy-start) | copy-done | bytes 196632
  11.1 1.5 %shard_map.59 = (f32[256,128]{1,0:T(8,128)S(1)}, f32[256,384]{1,0:T(8,128)S(1)}) custom-call(f32[8]{0:T(128)S(1)} %copy-done.3, f32[24,16,128]{2,1,0:T(8,128)S(1)} %bitcast.8, f32[24,16,128]{2,1,0:T(8,128)S(1)} %collective-permute-done.3.other_ref, s32[24,16]{1,0:T(8,128)S(1)} %bitcast.13), custom_call_target="tpu_custom_call" | custom-call | tf_op jit(solution)/shard_map/pallas_call | solution.py:215
  12.7 1.3 %shard_map.60 = (f32[192,128]{1,0:T(8,128)S(1)}, f32[64,128]{1,0:T(8,128)S(1)}) custom-call(s32[3]{0:T(128)S(1)} %pad_add_fusion.place_ref, f32[8]{0:T(128)S(1)} %copy-done.3, f32[24,16,128]{2,1,0:T(8,128)S(1)} %bitcast.9, f32[24,16,128]{2,1,0:T(8,128)S(1)} %collective-permute-done.halo_ref, s32[24,16]{1,0:T(8,128)S(1)} %collective-permute-done.1.after_ref, ...), custom_call_target="tpu_custom_call" | custom-call | tf_op jit(solution)/shard_map/pallas_call | solution.py:226
  14.0 0.3 collective-permute-start.4
  14.3 1.0 %collective-permute-done.4 = f32[64,128]{1,0:T(8,128)S(1)} collective-permute-done((f32[64,128]{1,0:T(8,128)S(1)}, f32[64,128]{1,0:T(8,128)S(1)}, u32[]{:S(2)}, u32[]{:S(2)}) %collective-permute-start.4) | collective-permute-done | bytes 32800 | tf_op jit(solution)/shard_map/ppermute | solution.py:237
  15.3 3.0 %collective-permute-start.5 = (f32[192,128]{1,0:T(8,128)S(1)}, f32[192,128]{1,0:T(8,128)S(1)}, u32[]{:S(2)}, u32[]{:S(2)}) collective-permute-start(f32[192,128]{1,0:T(8,128)S(1)} %pad_maximum_fusion), channel_id=1, source_target_pairs={{0,2},{2,0},{4,6},{6,4},{8,10},{10,8},{12,14},{14,12},{1,3},{3,1},... | collective-permute-start | bytes 294920 | tf_op jit(solution)/shard_map/ppermute | solution.py:241
  18.3 3.1 %collective-permute-done.5 = f32[192,128]{1,0:T(8,128)S(1)} collective-permute-done((f32[192,128]{1,0:T(8,128)S(1)}, f32[192,128]{1,0:T(8,128)S(1)}, u32[]{:S(2)}, u32[]{:S(2)}) %collective-permute-start.5) | collective-permute-done | bytes 98336 | tf_op jit(solution)/shard_map/ppermute | solution.py:241
  21.4 2.7 %collective-permute-start.6 = (f32[192,128]{1,0:T(8,128)S(1)}, f32[192,128]{1,0:T(8,128)S(1)}, u32[]{:S(2)}, u32[]{:S(2)}) collective-permute-start(f32[192,128]{1,0:T(8,128)S(1)} %fusion), channel_id=1, source_target_pairs={{0,4},{2,6},{4,0},{6,2},{8,12},{10,14},{12,8},{14,10},{1,5},{3,7},... | collective-permute-start | bytes 294920 | tf_op jit(solution)/shard_map/ppermute | solution.py:241
  24.1 2.6 %collective-permute-done.6 = f32[192,128]{1,0:T(8,128)S(1)} collective-permute-done((f32[192,128]{1,0:T(8,128)S(1)}, f32[192,128]{1,0:T(8,128)S(1)}, u32[]{:S(2)}, u32[]{:S(2)}) %collective-permute-start.6) | collective-permute-done | bytes 98336 | tf_op jit(solution)/shard_map/ppermute | solution.py:241
  26.7 0.0 copy-start.2
  26.8 3.3 %collective-permute-start.7 = (f32[192,128]{1,0:T(8,128)S(1)}, f32[192,128]{1,0:T(8,128)S(1)}, u32[]{:S(2)}, u32[]{:S(2)}) collective-permute-start(f32[192,128]{1,0:T(8,128)S(1)} %add.14), channel_id=1, source_target_pairs={{0,8},{2,10},{4,12},{6,14},{8,0},{10,2},{12,4},{14,6},{1,9},{3,11}... | collective-permute-start | bytes 294920 | tf_op jit(solution)/shard_map/ppermute | solution.py:241
  30.0 2.6 %collective-permute-done.7 = f32[192,128]{1,0:T(8,128)S(1)} collective-permute-done((f32[192,128]{1,0:T(8,128)S(1)}, f32[192,128]{1,0:T(8,128)S(1)}, u32[]{:S(2)}, u32[]{:S(2)}) %collective-permute-start.7) | collective-permute-done | bytes 98336 | tf_op jit(solution)/shard_map/ppermute | solution.py:241
  32.6 0.1 collective-permute-start.8
  32.7 1.1 %shard_map.61.code_ref = s32[24,128]{1,0:T(8,128)S(1)} custom-call(s32[6,4,128]{2,1,0:T(4,128)S(1)} %copy-done.2), custom_call_target="tpu_custom_call" | custom-call | tf_op jit(solution)/shard_map/pallas_call | solution.py:208
  33.8 0.2 collective-permute-done.8.theirs_ref
  34.0 15.0 %shard_map.62 = (f32[24,16,128]{2,1,0:T(8,128)}, f32[1,128]{1,0:T(1,128)}) custom-call(s32[3]{0:T(128)S(1)} %pad_add_fusion.place_ref, f32[192,128]{1,0:T(8,128)S(1)} %add.15.mine_ref, f32[192,128]{1,0:T(8,128)S(1)} %collective-permute-done.8.theirs_ref, s32[24,128]{1,0:T(8,128)S(1)} %shard_map.61.code_ref, f32[24,16,128]{2,1,0:T(8,128)S(1)} %bitcast.10, ...), custom_call_target="tpu_custom_call" | custom-call | tf_op jit(solution)/shard_map/pallas_call | solution.py:244
  (14 shorter events, 0.1 us)
Async XLA Ops:
  0.6 9.0 %collective-permute-start.3 = (f32[24,16,128]{2,1,0:T(8,128)}, f32[24,16,128]{2,1,0:T(8,128)S(1)}, u32[]{:S(2)}, u32[]{:S(2)}) collective-permute-start(f32[24,16,128]{2,1,0:T(8,128)} %bitcast.6), channel_id=1, source_target_pairs={{0,1},{1,0},{2,3},{3,2},{4,5},{5,4},{6,7},{7,6},{8,9},{9,8},{10,11... | collective-permute-start | bytes 589832 | tf_op jit(solution)/shard_map/ppermute | solution.py:201
  1.1 11.5 %collective-permute-start = (f32[24,16,128]{2,1,0:T(8,128)}, f32[24,16,128]{2,1,0:T(8,128)S(1)}, u32[]{:S(2)}, u32[]{:S(2)}) collective-permute-start(f32[24,16,128]{2,1,0:T(8,128)} %bitcast.7), channel_id=1, source_target_pairs={{4,0},{6,2},{8,4},{10,6},{12,8},{14,10},{5,1},{7,3},{9,5},{11,7},{... | collective-permute-start | bytes 589832 | tf_op jit(solution)/shard_map/ppermute | solution.py:200
  3.2 9.4 %collective-permute-start.1 = (s32[24,16]{1,0:T(8,128)S(1)}, s32[24,16]{1,0:T(8,128)S(1)}, u32[]{:S(2)}, u32[]{:S(2)}) collective-permute-start(s32[24,16]{1,0:T(8,128)S(1)} %bitcast.11), channel_id=1, source_target_pairs={{2,0},{4,2},{6,4},{8,6},{10,8},{12,10},{14,12},{3,1},{5,3},{7,5},{... | collective-permute-start | bytes 4616 | tf_op jit(solution)/shard_map/ppermute | solution.py:202
  4.5 8.1 %collective-permute-start.2 = (s32[24,16]{1,0:T(8,128)S(1)}, s32[24,16]{1,0:T(8,128)S(1)}, u32[]{:S(2)}, u32[]{:S(2)}) collective-permute-start(s32[24,16]{1,0:T(8,128)S(1)} %bitcast.12), channel_id=1, source_target_pairs={{0,2},{2,4},{4,6},{6,8},{8,10},{10,12},{12,14},{1,3},{3,5},{5,7},{... | collective-permute-start | bytes 4616 | tf_op jit(solution)/shard_map/ppermute | solution.py:203
  9.6 0.7 %copy-start.3 = (f32[8]{0:T(128)S(1)}, f32[8]{0:T(128)}, u32[]{:S(2)}) copy-start(f32[8]{0:T(128)} %conductivity_ref.3) | copy-start | bytes 100
  10.2 0.9 %copy-start = (f32[1,24,16,128]{3,2,1,0:T(8,128)S(1)}, f32[1,24,16,128]{3,2,1,0:T(8,128)}, u32[]{:S(2)}) copy-start(f32[1,24,16,128]{3,2,1,0:T(8,128)} %param.4) | copy-start | bytes 589828
  14.0 1.3 %collective-permute-start.4 = (f32[64,128]{1,0:T(8,128)S(1)}, f32[64,128]{1,0:T(8,128)S(1)}, u32[]{:S(2)}, u32[]{:S(2)}) collective-permute-start(f32[64,128]{1,0:T(8,128)S(1)} %get-tuple-element.11), channel_id=1, source_target_pairs={{0,1},{1,0},{2,3},{3,2},{4,5},{5,4},{6,7},{7,6},{8,9},{9,8},{10,11... | collective-permute-start | bytes 98312 | tf_op jit(solution)/shard_map/ppermute | solution.py:237
  15.3 6.1 %collective-permute-start.5 = (f32[192,128]{1,0:T(8,128)S(1)}, f32[192,128]{1,0:T(8,128)S(1)}, u32[]{:S(2)}, u32[]{:S(2)}) collective-permute-start(f32[192,128]{1,0:T(8,128)S(1)} %pad_maximum_fusion), channel_id=1, source_target_pairs={{0,2},{2,0},{4,6},{6,4},{8,10},{10,8},{12,14},{14,12},{1,3},{3,1},... | collective-permute-start | bytes 294920 | tf_op jit(solution)/shard_map/ppermute | solution.py:241
  21.4 5.3 %collective-permute-start.6 = (f32[192,128]{1,0:T(8,128)S(1)}, f32[192,128]{1,0:T(8,128)S(1)}, u32[]{:S(2)}, u32[]{:S(2)}) collective-permute-start(f32[192,128]{1,0:T(8,128)S(1)} %fusion), channel_id=1, source_target_pairs={{0,4},{2,6},{4,0},{6,2},{8,12},{10,14},{12,8},{14,10},{1,5},{3,7},... | collective-permute-start | bytes 294920 | tf_op jit(solution)/shard_map/ppermute | solution.py:241
  26.7 6.0 %copy-start.2 = (s32[6,4,128]{2,1,0:T(4,128)S(1)}, s32[6,4,128]{2,1,0:T(4,128)}, u32[]{:S(2)}) copy-start(s32[6,4,128]{2,1,0:T(4,128)} %pairing_ref.1) | copy-start | bytes 36868
  26.7 7.2 %copy-start.1 = (f32[1,24,16,128]{3,2,1,0:T(8,128)S(1)}, f32[1,24,16,128]{3,2,1,0:T(8,128)}, u32[]{:S(2)}) copy-start(f32[1,24,16,128]{3,2,1,0:T(8,128)} %param.4) | copy-start | bytes 589828
  26.8 5.9 %collective-permute-start.7 = (f32[192,128]{1,0:T(8,128)S(1)}, f32[192,128]{1,0:T(8,128)S(1)}, u32[]{:S(2)}, u32[]{:S(2)}) collective-permute-start(f32[192,128]{1,0:T(8,128)S(1)} %add.14), channel_id=1, source_target_pairs={{0,8},{2,10},{4,12},{6,14},{8,0},{10,2},{12,4},{14,6},{1,9},{3,11}... | collective-permute-start | bytes 294920 | tf_op jit(solution)/shard_map/ppermute | solution.py:241
  32.6 1.4 %collective-permute-start.8 = (f32[192,128]{1,0:T(8,128)S(1)}, f32[192,128]{1,0:T(8,128)S(1)}, u32[]{:S(2)}, u32[]{:S(2)}) collective-permute-start(f32[192,128]{1,0:T(8,128)S(1)} %add.15.mine_ref), channel_id=1, source_target_pairs={{0,1},{1,0},{2,3},{3,2},{4,5},{5,4},{6,7},{7,6},{8,9},{9,8},{10,11... | collective-permute-start | bytes 294920 | tf_op jit(solution)/shard_map/ppermute | solution.py:243

commit v3 on v2

--- a/solution.py
+++ b/solution.py
@@ -102,18 +102,46 @@
     sent_ref[...] = jnp.where(first, cross[half:], cross[:half])
 
 
+def split(values, count):
+    parts = []
+    for index in range(count):
+        part = values.astype(jnp.bfloat16)
+        parts.append(part)
+        if index < count - 1:
+            values = values - part.astype(jnp.float32)
+    return parts
+
+
+TWO = ((0, 0), (0, 1), (1, 0))
+THREE = TWO + ((0, 2), (1, 1), (2, 0))
+
+
+def long_dot(left, right, terms):
+    count = 1 + max(i for i, _ in terms)
+    left, right = split(left, count), split(right, count)
+    return jnp.dot(
+        jnp.concatenate([left[i] for i, _ in terms], axis=1),
+        jnp.concatenate([right[j] for _, j in terms], axis=0),
+        preferred_element_type=jnp.float32,
+    )
+
+
+def column_sums(values):
+    return jnp.broadcast_to(jnp.sum(values, axis=0, keepdims=True), (8, values.shape[1]))
+
+
 def rotation(diagonal, opposite, coupling, first):
     g_first = jnp.where(first, diagonal, opposite)
     g_second = jnp.where(first, opposite, diagonal)
     spread = g_first - g_second
     radius = jnp.sqrt(spread * spread + 4.0 * coupling * coupling)
-    sign = jnp.where(spread > 0, 1.0, jnp.where(spread < 0, -1.0, 0.0))
-    tangent = (
-        -2.0 * coupling * sign / (jnp.abs(spread) + radius + 1e-06 * (g_first + g_second + 1.0))
-    )
-    cosine = 1.0 / jnp.sqrt(1.0 + tangent * tangent)
+    turned = jnp.where(spread > 0, -2.0, jnp.where(spread < 0, 2.0, 0.0)) * coupling
+    tangent = turned * pl.reciprocal(
+        jnp.abs(spread) + radius + 1e-06 * (g_first + g_second + 1.0), approx=False
+    )
+    cosine = lax.rsqrt(1.0 + tangent * tangent)
     sine = cosine * tangent
-    return cosine[:1], jnp.where(first, -sine, sine)[:1]
+    return cosine, jnp.where(first, -sine, sine)
 
 
 def tournament_kernel(
@@ -125,63 +153,108 @@
     mine, theirs = mine_ref[...], theirs_ref[...]
     zero_side = jnp.where(side, mine, theirs)
     one_side = jnp.where(side, theirs, mine)
-    cross = jnp.concatenate([zero_side[n:], one_side[n:]], axis=0)
+    eye = lax.broadcasted_iota(jnp.int32, (n, n), 0) == lax.broadcasted_iota(jnp.int32, (n, n), 1)
     row = lax.broadcasted_iota(jnp.int32, (n, n), 0)
-    col = lax.broadcasted_iota(jnp.int32, (n, n), 1)
-    eye = row == col
-    identity = jnp.where(eye, 1.0, 0.0)
-    blank = jnp.zeros((n, h), jnp.float32)
-    gram = jnp.concatenate(
-        [
-            jnp.concatenate([zero_side[:n], cross], axis=1),
-            jnp.concatenate([cross.T, one_side[:n]], axis=1),
-        ],
-        axis=0,
-    )
+    blank = jnp.zeros((n, n), jnp.float32)
+    low_half = lax.broadcasted_iota(jnp.int32, (h, n), 1) < h
+    low = lax.broadcasted_iota(jnp.int32, (2 * n, n), 1) < h
+
+    cross01 = jnp.concatenate([zero_side[n:], one_side[n:]], axis=0)
+    near = [zero_side[:n], one_side[:n]]
+    cross = [cross01.T, cross01]
     total = None
+    slots = [[0, 1], [2, 3]]
     upper, lower = [0, 2], [1, 3]
     for meeting in range(meets):
-        met = [gram[:n, :n], gram[n:, n:]]
-        factor = [identity, identity]
+        last = meeting == meets - 1
+        uppers = {frozenset((upper[d], lower[d])): upper[d] for d in range(2)}
+        swapped = [uppers[frozenset(slots[d])] != slots[d][0] for d in range(2)]
+        factor = [None, None]
+        diagonal = [column_sums(jnp.where(eye, near[d], 0.0)) for d in range(2)]
         for turn in range(turns):
             index = meeting * turns + turn
             told = code_ref[index : index + 1, :]
-            partner = told % n
-            first = told >= n
-            paired = row == partner
+            other_way = pltpu.roll(jnp.broadcast_to(told, (8, n)), h, 1)[:1]
             for d in range(2):
-                held = met[d]
-                diagonal = jnp.sum(jnp.where(eye, held, 0.0), axis=0, keepdims=True)
-                coupling = jnp.sum(jnp.where(paired, held, 0.0), axis=0, keepdims=True)
-                diagonal = jnp.broadcast_to(diagonal, (8, n))
-                coupling = jnp.broadcast_to(coupling, (8, n))
-                cosine, sine = rotation(diagonal, lanes(diagonal, partner), coupling, first)
-                held = (held * cosine + lanes(held, partner) * sine).T
-                met[d] = held * cosine + lanes(held, partner) * sine
-                factor[d] = factor[d] * cosine + lanes(factor[d], partner) * sine
-        blocks = {}
-        for d in range(2):
-            for block, part in ((upper[d], factor[d][:, :h]), (lower[d], factor[d][:, h:])):
-                blocks[block] = jnp.concatenate([part, blank] if d == 0 else [blank, part], axis=0)
-        if meeting == meets - 1:
-            after = range(4)
-            norms = {}
-            for d in range(2):
-                norm = jnp.sqrt(jnp.sum(jnp.where(eye, met[d], 0.0), axis=0, keepdims=True))
-                norms[upper[d]], norms[lower[d]] = norm[:, :h], norm[:, h:]
+                partner = (other_way % n) ^ h if swapped[d] else told % n
+                first = (other_way if swapped[d] else told) >= n
+                if turn == 0:
+                    paired = row == partner
+                    coupling = column_sums(jnp.where(paired, near[d], 0.0))
+                else:
+                    opposite = lanes(factor[d], partner)
+                    coupling = column_sums(opposite * near[d])
+                across = lanes(diagonal[d], partner)
+                cosine, sine = rotation(diagonal[d], across, coupling, first)
+                diagonal[d] = (
+                    cosine * cosine * diagonal[d] + 2.0 * cosine * sine * coupling + sine * sine * across
+                )
+                cosine, sine = cosine[:1], sine[:1]
+                if turn == 0:
+                    factor[d] = jnp.where(eye, cosine, jnp.where(paired, sine, 0.0))
+                else:
+                    factor[d] = factor[d] * cosine + opposite * sine
+                if not last or turn < turns - 1:
+                    near[d] = near[d] * cosine + lanes(near[d], partner) * sine
+                if not last:
+                    cross[d] = cross[d] * cosine + lanes(cross[d], partner) * sine
+        if last:
+            break
+        if total is None:
+            total = [
+                jnp.concatenate([factor[0], blank], axis=0),
+                jnp.concatenate([blank, factor[1]], axis=0),
+            ]
         else:
-            upper, lower = [upper[0], lower[0]], [lower[1], upper[1]]
-            after = [upper[0], lower[0], upper[1], lower[1]]
-        wide = jnp.concatenate([blocks[block] for block in after], axis=1)
-        total = wide if total is None else dot(total, wide)
-        if meeting < meets - 1:
-            gram = dot(wide, dot(gram, wide), ((0,), (0,)))
-    picked = jnp.where(side, total[:, :n], total[:, n:])
-    near = jnp.where(side, picked[:n], picked[n:])
-    far = jnp.where(side, picked[n:], picked[:n])
-    flat = (-1, n)
-    rotated = dot(own_ref[...].reshape(flat), near) + dot(other_ref[...].reshape(flat), far)
-    rotated_ref[...] = rotated.reshape(rotated_ref.shape)
+            total = [long_dot(total[d], factor[d], TWO) for d in range(2)]
+        top = long_dot(factor[0].T, jnp.concatenate([near[0], cross[1]], axis=1), THREE)
+        bottom = long_dot(factor[1].T, jnp.concatenate([cross[0], near[1]], axis=1), THREE)
+        g00, g01, g10, g11 = top[:, :n], top[:, n:], bottom[:, :n], bottom[:, n:]
+        upper, lower = [upper[0], lower[0]], [lower[1], upper[1]]
+        meets_next = [frozenset((upper[d], lower[d])) for d in range(2)]
+        if frozenset((slots[0][0], slots[1][1])) not in meets_next:
+            slots[1] = slots[1][::-1]
+            g01, g11 = pltpu.roll(g01, h, 1), pltpu.roll(g11, h, 1)
+            g10 = jnp.concatenate([g10[h:], g10[:h]], axis=0)
+            g11 = jnp.concatenate([g11[h:], g11[:h]], axis=0)
+            total[1] = pltpu.roll(total[1], h, 1)
+        slots = [[slots[0][0], slots[1][1]], [slots[1][0], slots[0][1]]]
+
+        def mixed(first, second, third, fourth):
+            return jnp.concatenate(
+                [
+                    jnp.where(low_half, first[:h], second[:h]),
+                    jnp.where(low_half, third[h:], fourth[h:]),
+                ],
+                axis=0,
+            )
+
+        near = [mixed(g00, g01, g10, g11), mixed(g11, g10, g01, g00)]
+        cross = [mixed(g10, g11, g00, g01), mixed(g01, g00, g11, g10)]
+        total = [jnp.where(low, total[0], total[1]), jnp.where(low, total[1], total[0])]
+
+    flat = jnp.concatenate(
+        [own_ref[...].reshape(-1, n), other_ref[...].reshape(-1, n)], axis=1
+    )
+    both = jnp.concatenate(total, axis=1)
+    both = jnp.concatenate(
+        [jnp.where(side, both[:n], both[n:]), jnp.where(side, both[n:], both[:n])], axis=0
+    )
+    before_last = long_dot(flat, both, TWO)
+    gap = jnp.zeros((n, h), jnp.float32)
+    blocks, norms = {}, {}
+    for d in range(2):
+        norm = jnp.sqrt(diagonal[d][:1])
+        for i in range(2):
+            part = factor[d][:, i * h : (i + 1) * h]
+            blocks[slots[d][i]] = jnp.concatenate([part, gap] if d == 0 else [gap, part], axis=0)
+            norms[slots[d][i]] = norm[:, i * h : (i + 1) * h]
+    picked = jnp.where(
+        side,
+        jnp.concatenate([blocks[0], blocks[1]], axis=1),
+        jnp.concatenate([blocks[2], blocks[3]], axis=1),
+    )
+    rotated_ref[...] = long_dot(before_last, picked, TWO).reshape(rotated_ref.shape)
     sigma_ref[...] = jnp.where(
         side,
         jnp.concatenate([norms[0], norms[1]], axis=1),

time: 49.5 us -> 42.5 us (0.86)
  Pallas kernels: 18.9 us -> 11.8 us
    pallas_call x1, Pallas kernels: 15 us -> 7.96 us  [shards(): pl.pallas_call(functools.partial(tournament_kernel, pairing.shape[0], pai...]
  transfers between devices with their start and end apart: 9 -> 9, of which waited for: 5 -> 5; matrix products, arithmetic and copies ran while one was open for 2% -> 2% of each run, Pallas kernels for 5% -> 6%
where the time goes in v3:
time: 42.5 us; the launch traced here: 42 us
  starting transfers between devices  17.4 us (41%)
  Pallas kernels  11.8 us (28%)
  waiting for transfers between devices  9.55 us (22%)
  local copies, waits for them, and re-layouts  2.28 us (5%)
  between operations  0.76 us (2%)
    ppermute x3, starting transfers between devices, shards(): lax.ppermute(share, 'rows', [(i, i ^ apart) for i in range(count)])  8.94 us
    ppermute x3, waiting for transfers between devices, shards(): lax.ppermute(share, 'rows', [(i, i ^ apart) for i in range(count)])  8.33 us
    pallas_call x1, Pallas kernels, shards(): pl.pallas_call(functools.partial(tournament_kernel, pairing.shape[0], pai...  7.96 us
    ppermute x1, starting transfers between devices, shards(): lax.ppermute(labels, 'rows', [(i, i + 1) for i in range(count - 1)])  5.05 us
    unnamed x9, local copies, waits for them, and re-layouts  2.28 us
    pallas_call x1, Pallas kernels, shards(): pl.pallas_call(local_kernel, out_shape=(jax.ShapeDtypeStruct((2 * width,...  1.48 us
    pallas_call x1, Pallas kernels, shards(): pl.pallas_call(halo_kernel, out_shape=(jax.ShapeDtypeStruct((width + half...  1.33 us
    ppermute x1, starting transfers between devices, shards(): after = lax.ppermute(labels, 'rows', [(i + 1, i) for i in range(count - 1)])  1.28 us
  transfers between devices with their start and end apart: 9, of which 5 were waited for; matrix products, arithmetic and copies ran while one was open for 2% of the time, Pallas kernels for 6%

profile of v3, /device:TPU:0, one launch (start us, length us, event | category | flops | bytes accessed | tf_op | source)
XLA Modules:
  0.0 42.0 jit_solution(5355435596788401046)
XLA Ops:
  0.6 0.5 %collective-permute-start.3 = (f32[24,16,128]{2,1,0:T(8,128)}, f32[24,16,128]{2,1,0:T(8,128)S(1)}, u32[]{:S(2)}, u32[]{:S(2)}) collective-permute-start(f32[24,16,128]{2,1,0:T(8,128)} %bitcast.6), channel_id=1, source_target_pairs={{0,1},{1,0},{2,3},{3,2},{4,5},{5,4},{6,7},{7,6},{8,9},{9,8},{10,11... | collective-permute-start | bytes 589832 | tf_op jit(solution)/shard_map/ppermute | solution.py:274
  1.1 1.3 %collective-permute-start = (f32[24,16,128]{2,1,0:T(8,128)}, f32[24,16,128]{2,1,0:T(8,128)S(1)}, u32[]{:S(2)}, u32[]{:S(2)}) collective-permute-start(f32[24,16,128]{2,1,0:T(8,128)} %bitcast.7), channel_id=1, source_target_pairs={{4,0},{6,2},{8,4},{10,6},{12,8},{14,10},{5,1},{7,3},{9,5},{11,7},{... | collective-permute-start | bytes 589832 | tf_op jit(solution)/shard_map/ppermute | solution.py:273
  2.4 0.8 %copy.6 = s32[1,24,16]{2,1,0:T(8,128)S(1)} copy(s32[1,24,16]{1,2,0:T(8,128)} %param.5) | data formatting | bytes 3072 | tf_op args[1]
  3.2 1.3 %collective-permute-start.1 = (s32[24,16]{1,0:T(8,128)S(1)}, s32[24,16]{1,0:T(8,128)S(1)}, u32[]{:S(2)}, u32[]{:S(2)}) collective-permute-start(s32[24,16]{1,0:T(8,128)S(1)} %bitcast.11), channel_id=1, source_target_pairs={{2,0},{4,2},{6,4},{8,6},{10,8},{12,10},{14,12},{3,1},{5,3},{7,5},{... | collective-permute-start | bytes 4616 | tf_op jit(solution)/shard_map/ppermute | solution.py:275
  4.5 5.0 %collective-permute-start.2 = (s32[24,16]{1,0:T(8,128)S(1)}, s32[24,16]{1,0:T(8,128)S(1)}, u32[]{:S(2)}, u32[]{:S(2)}) collective-permute-start(s32[24,16]{1,0:T(8,128)S(1)} %bitcast.12), channel_id=1, source_target_pairs={{0,2},{2,4},{4,6},{6,8},{8,10},{10,12},{12,14},{1,3},{3,5},{5,7},{... | collective-permute-start | bytes 4616 | tf_op jit(solution)/shard_map/ppermute | solution.py:276
  9.6 0.1 pad_add_fusion.place_ref
  9.6 0.6 %copy-done.3 = f32[8]{0:T(128)S(1)} copy-done((f32[8]{0:T(128)S(1)}, f32[8]{0:T(128)}, u32[]{:S(2)}) %copy-start.3) | copy-done | bytes 56
  10.2 0.9 %copy-done = f32[1,24,16,128]{3,2,1,0:T(8,128)S(1)} copy-done((f32[1,24,16,128]{3,2,1,0:T(8,128)S(1)}, f32[1,24,16,128]{3,2,1,0:T(8,128)}, u32[]{:S(2)}) %copy-start) | copy-done | bytes 196632
  11.1 1.5 %shard_map.59 = (f32[256,128]{1,0:T(8,128)S(1)}, f32[256,384]{1,0:T(8,128)S(1)}) custom-call(f32[8]{0:T(128)S(1)} %copy-done.3, f32[24,16,128]{2,1,0:T(8,128)S(1)} %bitcast.8, f32[24,16,128]{2,1,0:T(8,128)S(1)} %collective-permute-done.3.other_ref, s32[24,16]{1,0:T(8,128)S(1)} %bitcast.13), custom_call_target="tpu_custom_call" | custom-call | tf_op jit(solution)/shard_map/pallas_call | solution.py:288
  12.7 1.3 %shard_map.60 = (f32[192,128]{1,0:T(8,128)S(1)}, f32[64,128]{1,0:T(8,128)S(1)}) custom-call(s32[3]{0:T(128)S(1)} %pad_add_fusion.place_ref, f32[8]{0:T(128)S(1)} %copy-done.3, f32[24,16,128]{2,1,0:T(8,128)S(1)} %bitcast.9, f32[24,16,128]{2,1,0:T(8,128)S(1)} %collective-permute-done.halo_ref, s32[24,16]{1,0:T(8,128)S(1)} %collective-permute-done.1.after_ref, ...), custom_call_target="tpu_custom_call" | custom-call | tf_op jit(solution)/shard_map/pallas_call | solution.py:299
  14.0 0.3 collective-permute-start.4
  14.3 1.0 %collective-permute-done.4 = f32[64,128]{1,0:T(8,128)S(1)} collective-permute-done((f32[64,128]{1,0:T(8,128)S(1)}, f32[64,128]{1,0:T(8,128)S(1)}, u32[]{:S(2)}, u32[]{:S(2)}) %collective-permute-start.4) | collective-permute-done | bytes 32800 | tf_op jit(solution)/shard_map/ppermute | solution.py:310
  15.3 3.0 %collective-permute-start.5 = (f32[192,128]{1,0:T(8,128)S(1)}, f32[192,128]{1,0:T(8,128)S(1)}, u32[]{:S(2)}, u32[]{:S(2)}) collective-permute-start(f32[192,128]{1,0:T(8,128)S(1)} %pad_maximum_fusion), channel_id=1, source_target_pairs={{0,2},{2,0},{4,6},{6,4},{8,10},{10,8},{12,14},{14,12},{1,3},{3,1},... | collective-permute-start | bytes 294920 | tf_op jit(solution)/shard_map/ppermute | solution.py:314
  18.3 3.1 %collective-permute-done.5 = f32[192,128]{1,0:T(8,128)S(1)} collective-permute-done((f32[192,128]{1,0:T(8,128)S(1)}, f32[192,128]{1,0:T(8,128)S(1)}, u32[]{:S(2)}, u32[]{:S(2)}) %collective-permute-start.5) | collective-permute-done | bytes 98336 | tf_op jit(solution)/shard_map/ppermute | solution.py:314
  21.4 2.7 %collective-permute-start.6 = (f32[192,128]{1,0:T(8,128)S(1)}, f32[192,128]{1,0:T(8,128)S(1)}, u32[]{:S(2)}, u32[]{:S(2)}) collective-permute-start(f32[192,128]{1,0:T(8,128)S(1)} %fusion), channel_id=1, source_target_pairs={{0,4},{2,6},{4,0},{6,2},{8,12},{10,14},{12,8},{14,10},{1,5},{3,7},... | collective-permute-start | bytes 294920 | tf_op jit(solution)/shard_map/ppermute | solution.py:314
  24.1 2.6 %collective-permute-done.6 = f32[192,128]{1,0:T(8,128)S(1)} collective-permute-done((f32[192,128]{1,0:T(8,128)S(1)}, f32[192,128]{1,0:T(8,128)S(1)}, u32[]{:S(2)}, u32[]{:S(2)}) %collective-permute-start.6) | collective-permute-done | bytes 98336 | tf_op jit(solution)/shard_map/ppermute | solution.py:314
  26.7 0.0 copy-start.2
  26.7 0.0 copy-start.1
  26.8 3.3 %collective-permute-start.7 = (f32[192,128]{1,0:T(8,128)S(1)}, f32[192,128]{1,0:T(8,128)S(1)}, u32[]{:S(2)}, u32[]{:S(2)}) collective-permute-start(f32[192,128]{1,0:T(8,128)S(1)} %add.14), channel_id=1, source_target_pairs={{0,8},{2,10},{4,12},{6,14},{8,0},{10,2},{12,4},{14,6},{1,9},{3,11}... | collective-permute-start | bytes 294920 | tf_op jit(solution)/shard_map/ppermute | solution.py:314
  30.0 2.6 %collective-permute-done.7 = f32[192,128]{1,0:T(8,128)S(1)} collective-permute-done((f32[192,128]{1,0:T(8,128)S(1)}, f32[192,128]{1,0:T(8,128)S(1)}, u32[]{:S(2)}, u32[]{:S(2)}) %collective-permute-start.7) | collective-permute-done | bytes 98336 | tf_op jit(solution)/shard_map/ppermute | solution.py:314
  32.6 0.1 collective-permute-start.8
  32.7 1.1 %shard_map.61.code_ref = s32[24,128]{1,0:T(8,128)S(1)} custom-call(s32[6,4,128]{2,1,0:T(4,128)S(1)} %copy-done.2), custom_call_target="tpu_custom_call" | custom-call | tf_op jit(solution)/shard_map/pallas_call | solution.py:281
  33.8 0.2 collective-permute-done.8.theirs_ref
  34.0 8.0 %shard_map.62 = (f32[24,16,128]{2,1,0:T(8,128)}, f32[1,128]{1,0:T(1,128)}) custom-call(s32[3]{0:T(128)S(1)} %pad_add_fusion.place_ref, f32[192,128]{1,0:T(8,128)S(1)} %add.15.mine_ref, f32[192,128]{1,0:T(8,128)S(1)} %collective-permute-done.8.theirs_ref, s32[24,128]{1,0:T(8,128)S(1)} %shard_map.61.code_ref, f32[24,16,128]{2,1,0:T(8,128)S(1)} %bitcast.10, ...), custom_call_target="tpu_custom_call" | custom-call | tf_op jit(solution)/shard_map/pallas_call | solution.py:317
  (14 shorter events, 0.1 us)
Async XLA Ops:
  0.6 9.0 %collective-permute-start.3 = (f32[24,16,128]{2,1,0:T(8,128)}, f32[24,16,128]{2,1,0:T(8,128)S(1)}, u32[]{:S(2)}, u32[]{:S(2)}) collective-permute-start(f32[24,16,128]{2,1,0:T(8,128)} %bitcast.6), channel_id=1, source_target_pairs={{0,1},{1,0},{2,3},{3,2},{4,5},{5,4},{6,7},{7,6},{8,9},{9,8},{10,11... | collective-permute-start | bytes 589832 | tf_op jit(solution)/shard_map/ppermute | solution.py:274
  1.1 11.5 %collective-permute-start = (f32[24,16,128]{2,1,0:T(8,128)}, f32[24,16,128]{2,1,0:T(8,128)S(1)}, u32[]{:S(2)}, u32[]{:S(2)}) collective-permute-start(f32[24,16,128]{2,1,0:T(8,128)} %bitcast.7), channel_id=1, source_target_pairs={{4,0},{6,2},{8,4},{10,6},{12,8},{14,10},{5,1},{7,3},{9,5},{11,7},{... | collective-permute-start | bytes 589832 | tf_op jit(solution)/shard_map/ppermute | solution.py:273
  3.2 9.4 %collective-permute-start.1 = (s32[24,16]{1,0:T(8,128)S(1)}, s32[24,16]{1,0:T(8,128)S(1)}, u32[]{:S(2)}, u32[]{:S(2)}) collective-permute-start(s32[24,16]{1,0:T(8,128)S(1)} %bitcast.11), channel_id=1, source_target_pairs={{2,0},{4,2},{6,4},{8,6},{10,8},{12,10},{14,12},{3,1},{5,3},{7,5},{... | collective-permute-start | bytes 4616 | tf_op jit(solution)/shard_map/ppermute | solution.py:275
  4.5 8.1 %collective-permute-start.2 = (s32[24,16]{1,0:T(8,128)S(1)}, s32[24,16]{1,0:T(8,128)S(1)}, u32[]{:S(2)}, u32[]{:S(2)}) collective-permute-start(s32[24,16]{1,0:T(8,128)S(1)} %bitcast.12), channel_id=1, source_target_pairs={{0,2},{2,4},{4,6},{6,8},{8,10},{10,12},{12,14},{1,3},{3,5},{5,7},{... | collective-permute-start | bytes 4616 | tf_op jit(solution)/shard_map/ppermute | solution.py:276
  9.6 0.7 %copy-start.3 = (f32[8]{0:T(128)S(1)}, f32[8]{0:T(128)}, u32[]{:S(2)}) copy-start(f32[8]{0:T(128)} %conductivity_ref.3) | copy-start | bytes 100
  10.2 0.9 %copy-start = (f32[1,24,16,128]{3,2,1,0:T(8,128)S(1)}, f32[1,24,16,128]{3,2,1,0:T(8,128)}, u32[]{:S(2)}) copy-start(f32[1,24,16,128]{3,2,1,0:T(8,128)} %param.4) | copy-start | bytes 589828
  14.0 1.3 %collective-permute-start.4 = (f32[64,128]{1,0:T(8,128)S(1)}, f32[64,128]{1,0:T(8,128)S(1)}, u32[]{:S(2)}, u32[]{:S(2)}) collective-permute-start(f32[64,128]{1,0:T(8,128)S(1)} %get-tuple-element.11), channel_id=1, source_target_pairs={{0,1},{1,0},{2,3},{3,2},{4,5},{5,4},{6,7},{7,6},{8,9},{9,8},{10,11... | collective-permute-start | bytes 98312 | tf_op jit(solution)/shard_map/ppermute | solution.py:310
  15.3 6.1 %collective-permute-start.5 = (f32[192,128]{1,0:T(8,128)S(1)}, f32[192,128]{1,0:T(8,128)S(1)}, u32[]{:S(2)}, u32[]{:S(2)}) collective-permute-start(f32[192,128]{1,0:T(8,128)S(1)} %pad_maximum_fusion), channel_id=1, source_target_pairs={{0,2},{2,0},{4,6},{6,4},{8,10},{10,8},{12,14},{14,12},{1,3},{3,1},... | collective-permute-start | bytes 294920 | tf_op jit(solution)/shard_map/ppermute | solution.py:314
  21.4 5.3 %collective-permute-start.6 = (f32[192,128]{1,0:T(8,128)S(1)}, f32[192,128]{1,0:T(8,128)S(1)}, u32[]{:S(2)}, u32[]{:S(2)}) collective-permute-start(f32[192,128]{1,0:T(8,128)S(1)} %fusion), channel_id=1, source_target_pairs={{0,4},{2,6},{4,0},{6,2},{8,12},{10,14},{12,8},{14,10},{1,5},{3,7},... | collective-permute-start | bytes 294920 | tf_op jit(solution)/shard_map/ppermute | solution.py:314
  26.7 6.0 %copy-start.2 = (s32[6,4,128]{2,1,0:T(4,128)S(1)}, s32[6,4,128]{2,1,0:T(4,128)}, u32[]{:S(2)}) copy-start(s32[6,4,128]{2,1,0:T(4,128)} %pairing_ref.1) | copy-start | bytes 36868
  26.7 7.2 %copy-start.1 = (f32[1,24,16,128]{3,2,1,0:T(8,128)S(1)}, f32[1,24,16,128]{3,2,1,0:T(8,128)}, u32[]{:S(2)}) copy-start(f32[1,24,16,128]{3,2,1,0:T(8,128)} %param.4) | copy-start | bytes 589828
  26.8 5.9 %collective-permute-start.7 = (f32[192,128]{1,0:T(8,128)S(1)}, f32[192,128]{1,0:T(8,128)S(1)}, u32[]{:S(2)}, u32[]{:S(2)}) collective-permute-start(f32[192,128]{1,0:T(8,128)S(1)} %add.14), channel_id=1, source_target_pairs={{0,8},{2,10},{4,12},{6,14},{8,0},{10,2},{12,4},{14,6},{1,9},{3,11}... | collective-permute-start | bytes 294920 | tf_op jit(solution)/shard_map/ppermute | solution.py:314
  32.6 1.4 %collective-permute-start.8 = (f32[192,128]{1,0:T(8,128)S(1)}, f32[192,128]{1,0:T(8,128)S(1)}, u32[]{:S(2)}, u32[]{:S(2)}) collective-permute-start(f32[192,128]{1,0:T(8,128)S(1)} %add.15.mine_ref), channel_id=1, source_target_pairs={{0,1},{1,0},{2,3},{3,2},{4,5},{5,4},{6,7},{7,6},{8,9},{9,8},{10,11... | collective-permute-start | bytes 294920 | tf_op jit(solution)/shard_map/ppermute | solution.py:316

commit v4 on v3

--- a/solution.py
+++ b/solution.py
@@ -7,16 +7,10 @@
 from jax.experimental.pallas import tpu as pltpu
 from jax.sharding import PartitionSpec as P
 
-HIGHEST = lax.Precision.HIGHEST
 PARAMS = pltpu.CompilerParams(vmem_limit_bytes=16 * 2**20)
+HBM = pl.BlockSpec(memory_space=pltpu.HBM)
 VMEM = pl.BlockSpec(memory_space=pltpu.VMEM)
 SMEM = pl.BlockSpec(memory_space=pltpu.SMEM)
-
-
-def dot(left, right, dims=((1,), (0,))):
-    return lax.dot_general(
-        left, right, (dims, ((), ())), precision=HIGHEST, preferred_element_type=jnp.float32
-    )
 
 
 def lanes(values, index):
@@ -40,17 +34,66 @@
     code_ref[...] = jnp.concatenate(rows, axis=0).astype(jnp.int32)
 
 
-def quarter_squares(labels, conductivity_ref):
-    labels = labels.T
+def split(values, count):
+    parts = []
+    for index in range(count):
+        part = values.astype(jnp.bfloat16)
+        parts.append(part)
+        if index < count - 1:
+            values = values - part.astype(jnp.float32)
+    return parts
+
+
+TWO = ((0, 0), (0, 1), (1, 0))
+THREE = TWO + ((0, 2), (1, 1), (2, 0))
+
+
+def long_dot(left, right, terms):
+    count = 1 + max(i for i, _ in terms)
+    left, right = split(left, count), split(right, count)
+    return jnp.dot(
+        laid(left, terms, 0, 1), laid(right, terms, 1, 0), preferred_element_type=jnp.float32
+    )
+
+
+def laid(parts, terms, side, axis):
+    return jnp.concatenate([parts[term[side]] for term in terms], axis=axis)
+
+
+def column_sums(values):
+    return jnp.broadcast_to(jnp.sum(values, axis=0, keepdims=True), (8, values.shape[1]))
+
+
+def quarter_squares(labels, table):
     squares = jnp.zeros(labels.shape, jnp.float32)
-    for region in range(conductivity_ref.shape[0]):
-        squares = jnp.where(labels == region, conductivity_ref[region], squares)
-    return 0.25 * squares
-
-
-def local_kernel(conductivity_ref, own_ref, other_ref, labels_ref, gram_ref, turned_ref, applied_ref):
+    for region in range(table.shape[0]):
+        squares = jnp.where(labels == region, table[region : region + 1, : labels.shape[1]], squares)
+    return squares
+
+
+def local_kernel(
+    conductivity_ref, own_hbm_ref, labels_hbm_ref, other_ref,
+    gram_ref, turned_ref, own_ref, table_ref,
+    applied_ref, labels_ref, regions_ref, sems,
+):
     ny, nz, width = own_ref.shape
-    squares = quarter_squares(labels_ref[...], conductivity_ref)
+    cells = ny * nz
+    fetches = [
+        pltpu.make_async_copy(source, target, sems.at[index])
+        for index, (source, target) in enumerate(
+            ((own_hbm_ref, own_ref), (labels_hbm_ref, labels_ref), (conductivity_ref, regions_ref))
+        )
+    ]
+    for fetch in fetches:
+        fetch.start()
+    turned_ref[width:, :] = laid(split(other_ref[...].reshape(cells, width).T, 3), THREE, 0, 1)
+    for fetch in fetches:
+        fetch.wait()
+    table_ref[...] = jnp.concatenate(
+        [jnp.full((1, width), 0.25 * regions_ref[region]) for region in range(table_ref.shape[0])],
+        axis=0,
+    )
+    squares = quarter_squares(labels_ref[...], table_ref[...])
     z = lax.broadcasted_iota(jnp.int32, (nz, ny), 0)
     above = jnp.where(z < nz - 1, pltpu.roll(squares, nz - 1, 0), 0.0)
     below = jnp.where(z > 0, pltpu.roll(squares, 1, 0), 0.0)
@@ -72,18 +115,23 @@
         total -= above[:, y : y + 1] * pltpu.roll(u, nz - 2, 0)
         total -= below[:, y : y + 1] * pltpu.roll(u, 2, 0)
         applied_ref[y * nz : (y + 1) * nz, :] = total
-    turned_ref[:width, :] = own_ref[...].reshape(ny * nz, width).T
-    turned_ref[width:, :] = other_ref[...].reshape(ny * nz, width).T
-    gram_ref[...] = dot(turned_ref[...], applied_ref[...])
+    turned_ref[:width, :] = laid(split(own_ref[...].reshape(cells, width).T, 3), THREE, 0, 1)
+    gram_ref[...] = jnp.dot(
+        turned_ref[...],
+        laid(split(applied_ref[...], 3), THREE, 1, 0),
+        preferred_element_type=jnp.float32,
+    )
 
 
 def halo_kernel(
-    place_ref, conductivity_ref, own_ref, halo_ref, after_ref, before_ref, gram_ref, turned_ref,
+    place_ref, table_ref, own_ref, halo_ref, mine_ref, theirs_ref, gram_ref, turned_ref,
     kept_ref, sent_ref, applied_ref,
 ):
     ny, nz, width = own_ref.shape
-    after = quarter_squares(after_ref[...], conductivity_ref)
-    before = quarter_squares(before_ref[...], conductivity_ref)
+    mine = quarter_squares(mine_ref[...], table_ref[...])
+    theirs = quarter_squares(theirs_ref[...], table_ref[...])
+    after = jnp.where(place_ref[0] == 0, mine, theirs)
+    before = jnp.where(place_ref[0] == 0, theirs, mine)
     after = jnp.where(place_ref[1] < place_ref[2] - 1, after, 0.0)
     before = jnp.where(place_ref[1] > 0, before, 0.0)
     for y in range(ny):
@@ -91,43 +139,47 @@
         applied_ref[y * nz : (y + 1) * nz, :] = (ahead + before[:, y : y + 1]) * own_ref[y] - (
             2.0 * ahead
         ) * halo_ref[y]
-    gram = gram_ref[...] + dot(turned_ref[...], applied_ref[...])
+    gram = gram_ref[...] + jnp.dot(
+        turned_ref[...],
+        laid(split(applied_ref[...], 3), THREE, 1, 0),
+        preferred_element_type=jnp.float32,
+    )
     half = width // 2
     first = place_ref[0] == 0
     own = gram[:width]
     cross = gram[width:]
     cross = 0.5 * jnp.where(first, cross.T, cross)
-    kept_ref[:width, :] = 0.5 * (own + own.T)
-    kept_ref[width:, :] = jnp.where(first, cross[:half], cross[half:])
+    own = 0.5 * (own + own.T)
+    row = lax.broadcasted_iota(jnp.int32, (half, width), 0)
+    col = lax.broadcasted_iota(jnp.int32, (half, width), 1)
+    kept_ref[:half, :] = jnp.where(
+        (col >= row), own[:half], pltpu.roll(own[half:], half, 1)
+    )
+    kept_ref[half : half + 8, :] = column_sums(
+        jnp.where(
+            lax.broadcasted_iota(jnp.int32, (width, width), 0)
+            == lax.broadcasted_iota(jnp.int32, (width, width), 1),
+            own,
+            0.0,
+        )
+    )
+    kept_ref[half + 8 :, :] = jnp.where(first, cross[:half], cross[half:])
     sent_ref[...] = jnp.where(first, cross[half:], cross[:half])
 
 
-def split(values, count):
-    parts = []
-    for index in range(count):
-        part = values.astype(jnp.bfloat16)
-        parts.append(part)
-        if index < count - 1:
-            values = values - part.astype(jnp.float32)
-    return parts
-
-
-TWO = ((0, 0), (0, 1), (1, 0))
-THREE = TWO + ((0, 2), (1, 1), (2, 0))
-
-
-def long_dot(left, right, terms):
-    count = 1 + max(i for i, _ in terms)
-    left, right = split(left, count), split(right, count)
-    return jnp.dot(
-        jnp.concatenate([left[i] for i, _ in terms], axis=1),
-        jnp.concatenate([right[j] for _, j in terms], axis=0),
-        preferred_element_type=jnp.float32,
-    )
-
-
-def column_sums(values):
-    return jnp.broadcast_to(jnp.sum(values, axis=0, keepdims=True), (8, values.shape[1]))
+def unpacked(share):
+    n = share.shape[1]
+    h = n // 2
+    top = share[:h]
+    row = lax.broadcasted_iota(jnp.int32, (h, n), 0)
+    col = lax.broadcasted_iota(jnp.int32, (h, n), 1)
+    mirror = top.T
+    wide = jnp.concatenate([mirror[:h], mirror[:h]], axis=1)
+    first = jnp.where(col >= row, top, wide)
+    second = jnp.where(col - h < row, pltpu.roll(top, h, 1), wide)
+    second = jnp.where(col - h == row, share[h : h + 1], second)
+    tall = jnp.concatenate([mirror[h:], mirror[h:]], axis=1)
+    return jnp.concatenate([first, jnp.where(col < h, tall, second)], axis=0)
 
 
 def rotation(diagonal, opposite, coupling, first):
@@ -159,8 +211,8 @@
     low_half = lax.broadcasted_iota(jnp.int32, (h, n), 1) < h
     low = lax.broadcasted_iota(jnp.int32, (2 * n, n), 1) < h
 
-    cross01 = jnp.concatenate([zero_side[n:], one_side[n:]], axis=0)
-    near = [zero_side[:n], one_side[:n]]
+    cross01 = jnp.concatenate([zero_side[h + 8 :], one_side[h + 8 :]], axis=0)
+    near = [unpacked(zero_side), unpacked(one_side)]
     cross = [cross01.T, cross01]
     total = None
     slots = [[0, 1], [2, 3]]
@@ -269,11 +321,9 @@
     count = lax.axis_size("rows")
     swap = [(0, 1), (1, 0)]
     own = snapshots[0]
-    labels = labels[0]
+    labels = labels[0].T
     halo = lax.ppermute(own, "rows", [(i + 2, i) for i in range(count - 2)])
     other = lax.ppermute(own, "cols", swap)
-    after = lax.ppermute(labels, "rows", [(i + 1, i) for i in range(count - 1)])
-    before = lax.ppermute(labels, "rows", [(i, i + 1) for i in range(count - 1)])
     place = jnp.stack(
         [lax.axis_index("cols"), lax.axis_index("rows"), jnp.asarray(count, jnp.int32)]
     ).astype(jnp.int32)
@@ -285,30 +335,45 @@
         out_specs=VMEM,
         compiler_params=PARAMS,
     )(pairing)
-    gram, turned = pl.pallas_call(
+    beside = lax.ppermute(
+        labels,
+        ("rows", "cols"),
+        [(2 * (i + 1), 2 * i) for i in range(count - 1)]
+        + [(2 * i + 1, 2 * (i + 1) + 1) for i in range(count - 1)],
+    )
+    gram, turned, own, table = pl.pallas_call(
         local_kernel,
         out_shape=(
             jax.ShapeDtypeStruct((2 * width, width), jnp.float32),
-            jax.ShapeDtypeStruct((2 * width, cells), jnp.float32),
+            jax.ShapeDtypeStruct((2 * width, len(THREE) * cells), jnp.bfloat16),
+            jax.ShapeDtypeStruct((ny, nz, width), jnp.float32),
+            jax.ShapeDtypeStruct((conductivity.shape[0], width), jnp.float32),
         ),
-        in_specs=[SMEM] + [VMEM] * 3,
+        in_specs=[HBM] * 3 + [VMEM],
+        out_specs=[VMEM] * 4,
+        scratch_shapes=[
+            pltpu.VMEM((cells, width), jnp.float32),
+            pltpu.VMEM(labels.shape, jnp.int32),
+            pltpu.SMEM(conductivity.shape, jnp.float32),
+            pltpu.SemaphoreType.DMA((3,)),
+        ],
+        compiler_params=PARAMS,
+    )(conductivity, own, labels, other)
+    beside, table = lax.optimization_barrier((beside, table))
+    across = lax.ppermute(beside, "cols", swap)
+    kept, sent = pl.pallas_call(
+        halo_kernel,
+        out_shape=(
+            jax.ShapeDtypeStruct((width + 8, width), jnp.float32),
+            jax.ShapeDtypeStruct((half, width), jnp.float32),
+        ),
+        in_specs=[SMEM] + [VMEM] * 7,
         out_specs=[VMEM] * 2,
         scratch_shapes=[pltpu.VMEM((cells, width), jnp.float32)],
         compiler_params=PARAMS,
-    )(conductivity, own, other, labels)
-    kept, sent = pl.pallas_call(
-        halo_kernel,
-        out_shape=(
-            jax.ShapeDtypeStruct((width + half, width), jnp.float32),
-            jax.ShapeDtypeStruct((half, width), jnp.float32),
-        ),
-        in_specs=[SMEM] * 2 + [VMEM] * 6,
-        out_specs=[VMEM] * 2,
-        scratch_shapes=[pltpu.VMEM((cells, width), jnp.float32)],
-        compiler_params=PARAMS,
-    )(place, conductivity, own, halo, after, before, gram, turned)
+    )(place, table, own, halo, beside, across, gram, turned)
     received = lax.ppermute(sent, "cols", swap)
-    share = jnp.concatenate([kept[:width], kept[width:] + received], axis=0)
+    share = jnp.concatenate([kept[: half + 8], kept[half + 8 :] + received], axis=0)
     apart = 1
     while apart < count:
         share = share + lax.ppermute(share, "rows", [(i, i ^ apart) for i in range(count)])

time: 42.5 us -> 39.2 us (0.922)
  starting transfers between devices: 17.4 us -> 13.5 us
  waiting for transfers between devices: 9.55 us -> 10.1 us
    ppermute x2, starting transfers between devices: 6.33 us -> 3.75 us  [the longest x1 2.46 us: shards(): across = lax.ppermute(beside, 'cols', swap)]
    ppermute x2, waiting for transfers between devices: 0.01 us -> 1.53 us  [the longest x1 0.95 us: shards(): lax.ppermute(labels, ('rows', 'cols'), [(2 * (i + 1), 2 * i) for i in ran...]
    ppermute x3, starting transfers between devices: 8.94 us -> 7.43 us  [shards(): lax.ppermute(share, 'rows', [(i, i ^ apart) for i in range(count)])]
    ppermute x3, waiting for transfers between devices: 8.33 us -> 7.36 us  [shards(): lax.ppermute(share, 'rows', [(i, i ^ apart) for i in range(count)])]
    unnamed x9 -> x8, local copies, waits for them, and re-layouts: 2.28 us -> 2.27 us
  transfers between devices with their start and end apart: 9 -> 9, of which waited for: 5 -> 8; matrix products, arithmetic and copies ran while one was open for 2% -> 0% of each run, Pallas kernels for 6% -> 7%
where the time goes in v4:
time: 39.2 us; the launch traced here: 38.9 us
  starting transfers between devices  13.5 us (34%)
  Pallas kernels  12.2 us (31%)
  waiting for transfers between devices  10.1 us (26%)
  local copies, waits for them, and re-layouts  2.28 us (6%)
  between operations  0.72 us (2%)
    pallas_call x1, Pallas kernels, shards(): pl.pallas_call(functools.partial(tournament_kernel, pairing.shape[0], pai...  8.19 us
    ppermute x3, starting transfers between devices, shards(): lax.ppermute(share, 'rows', [(i, i ^ apart) for i in range(count)])  7.43 us
    ppermute x3, waiting for transfers between devices, shards(): lax.ppermute(share, 'rows', [(i, i ^ apart) for i in range(count)])  7.36 us
    ppermute x1, starting transfers between devices, shards(): across = lax.ppermute(beside, 'cols', swap)  2.46 us
    unnamed x8, local copies, waits for them, and re-layouts  2.27 us
    pallas_call x1, Pallas kernels, shards(): pl.pallas_call(local_kernel, out_shape=(jax.ShapeDtypeStruct((2 * width,...  1.7 us
    ppermute x1, starting transfers between devices, shards(): lax.ppermute(labels, ('rows', 'cols'), [(2 * (i + 1), 2 * i) for i in ran...  1.29 us
    pallas_call x1, Pallas kernels, shards(): pl.pallas_call(halo_kernel, out_shape=(jax.ShapeDtypeStruct((width + 8, w...  1.28 us
  transfers between devices with their start and end apart: 9, of which 8 were waited for; matrix products, arithmetic and copies ran while one was open for 0% of the time, Pallas kernels for 7%

profile of v4, /device:TPU:0, one launch (start us, length us, event | category | flops | bytes accessed | tf_op | source)
XLA Modules:
  0.0 38.9 jit_solution(2526524110011179877)
XLA Ops:
  0.6 0.5 %collective-permute-start.1 = (f32[24,16,128]{2,1,0:T(8,128)}, f32[24,16,128]{2,1,0:T(8,128)S(1)}, u32[]{:S(2)}, u32[]{:S(2)}) collective-permute-start(f32[24,16,128]{2,1,0:T(8,128)} %bitcast.8), channel_id=1, source_target_pairs={{0,1},{1,0},{2,3},{3,2},{4,5},{5,4},{6,7},{7,6},{8,9},{9,8},{10,11... | collective-permute-start | bytes 589832 | tf_op jit(solution)/shard_map/ppermute | solution.py:326
  1.1 1.3 %collective-permute-start.2 = (f32[24,16,128]{2,1,0:T(8,128)}, f32[24,16,128]{2,1,0:T(8,128)S(1)}, u32[]{:S(2)}, u32[]{:S(2)}) collective-permute-start(f32[24,16,128]{2,1,0:T(8,128)} %bitcast.9), channel_id=1, source_target_pairs={{4,0},{6,2},{8,4},{10,6},{12,8},{14,10},{5,1},{7,3},{9,5},{11,7},{... | collective-permute-start | bytes 589832 | tf_op jit(solution)/shard_map/ppermute | solution.py:325
  2.4 1.3 %collective-permute-start = (s32[16,24]{1,0:T(8,128)}, s32[16,24]{1,0:T(8,128)S(1)}, u32[]{:S(2)}, u32[]{:S(2)}) collective-permute-start(s32[16,24]{1,0:T(8,128)} %bitcast.11), channel_id=1, source_target_pairs={{2,0},{4,2},{6,4},{8,6},{10,8},{12,10},{14,12},{1,3},{3,5},{5,7},{... | collective-permute-start | bytes 4616 | tf_op jit(solution)/shard_map/ppermute | solution.py:338
  3.8 0.9 %copy-done = f32[1,24,16,128]{3,2,1,0:T(8,128)S(1)} copy-done((f32[1,24,16,128]{3,2,1,0:T(8,128)S(1)}, f32[1,24,16,128]{3,2,1,0:T(8,128)}, u32[]{:S(2)}) %copy-start) | copy-done | bytes 196632
  4.7 0.7 %copy-done.2 = s32[1,24,16]{1,2,0:T(8,128)S(1)} copy-done((s32[1,24,16]{1,2,0:T(8,128)S(1)}, s32[1,24,16]{1,2,0:T(8,128)}, u32[]{:S(2)}) %copy-start.2) | copy-done | bytes 1560
  5.4 0.7 %copy-done.3 = f32[8]{0:T(128)S(1)} copy-done((f32[8]{0:T(128)S(1)}, f32[8]{0:T(128)}, u32[]{:S(2)}) %copy-start.3) | copy-done | bytes 56
  6.0 1.7 %shard_map.59 = (f32[256,128]{1,0:T(8,128)S(1)}, bf16[256,2304]{1,0:T(8,128)(2,1)S(1)}, f32[24,16,128]{2,1,0:T(8,128)S(1)}, f32[8,128]{1,0:T(8,128)S(1)}) custom-call(f32[8]{0:T(128)S(1)} %copy-done.3, f32[24,16,128]{2,1,0:T(8,128)S(1)} %bitcast.10, s32[16,24]{1,0:T(8,128)S(1)} %bitcast.12, f32[24,16,128]{2,1,0:T(8,128)S(1)} %collective-permute-done.1.other_ref), custom_call_target="tpu_custom_call" | custom-call | tf_op jit(solution)/shard_map/pallas_call | solution.py:344
  7.7 0.9 %collective-permute-done.mine_ref = s32[16,24]{1,0:T(8,128)S(1)} collective-permute-done((s32[16,24]{1,0:T(8,128)}, s32[16,24]{1,0:T(8,128)S(1)}, u32[]{:S(2)}, u32[]{:S(2)}) %collective-permute-start) | collective-permute-done | bytes 1568 | tf_op jit(solution)/shard_map/ppermute | solution.py:338
  8.7 2.5 %collective-permute-start.3 = (s32[16,24]{1,0:T(8,128)S(1)}, s32[16,24]{1,0:T(8,128)S(1)}, u32[]{:S(2)}, u32[]{:S(2)}) collective-permute-start(s32[16,24]{1,0:T(8,128)S(1)} %collective-permute-done.mine_ref), channel_id=1, source_target_pairs={{0,1},{1,0},{2,3},{3,2},{4,5},{5,4},{6,7},{7,6},{8,9},{9,8},{10,11... | collective-permute-start | bytes 4616 | tf_op jit(solution)/shard_map/ppermute | solution.py:363
  11.1 0.1 pad_add_fusion.place_ref
  11.2 0.2 collective-permute-done.2.halo_ref
  11.4 0.6 %collective-permute-done.3.theirs_ref = s32[16,24]{1,0:T(8,128)S(1)} collective-permute-done((s32[16,24]{1,0:T(8,128)S(1)}, s32[16,24]{1,0:T(8,128)S(1)}, u32[]{:S(2)}, u32[]{:S(2)}) %collective-permute-start.3) | collective-permute-done | bytes 1568 | tf_op jit(solution)/shard_map/ppermute | solution.py:363
  12.0 1.3 %shard_map.60 = (f32[136,128]{1,0:T(8,128)S(1)}, f32[64,128]{1,0:T(8,128)S(1)}) custom-call(s32[3]{0:T(128)S(1)} %pad_add_fusion.place_ref, f32[8,128]{1,0:T(8,128)S(1)} %get-tuple-element.13.table_ref, f32[24,16,128]{2,1,0:T(8,128)S(1)} %get-tuple-element.14.own_ref, f32[24,16,128]{2,1,0:T(8,128)S(1)} %collective-permute-done.2.halo_ref, ...), custom_call_target="tpu_custom_call" | custom-call | tf_op jit(solution)/shard_map/pallas_call | solution.py:364
  13.3 0.4 %collective-permute-start.4 = (f32[64,128]{1,0:T(8,128)S(1)}, f32[64,128]{1,0:T(8,128)S(1)}, u32[]{:S(2)}, u32[]{:S(2)}) collective-permute-start(f32[64,128]{1,0:T(8,128)S(1)} %get-tuple-element.19), channel_id=1, source_target_pairs={{0,1},{1,0},{2,3},{3,2},{4,5},{5,4},{6,7},{7,6},{8,9},{9,8},{10,11... | collective-permute-start | bytes 98312 | tf_op jit(solution)/shard_map/ppermute | solution.py:375
  13.7 0.9 %collective-permute-done.4 = f32[64,128]{1,0:T(8,128)S(1)} collective-permute-done((f32[64,128]{1,0:T(8,128)S(1)}, f32[64,128]{1,0:T(8,128)S(1)}, u32[]{:S(2)}, u32[]{:S(2)}) %collective-permute-start.4) | collective-permute-done | bytes 32800 | tf_op jit(solution)/shard_map/ppermute | solution.py:375
  14.6 2.2 %collective-permute-start.5 = (f32[136,128]{1,0:T(8,128)S(1)}, f32[136,128]{1,0:T(8,128)S(1)}, u32[]{:S(2)}, u32[]{:S(2)}) collective-permute-start(f32[136,128]{1,0:T(8,128)S(1)} %pad_maximum_fusion), channel_id=1, source_target_pairs={{0,2},{2,0},{4,6},{6,4},{8,10},{10,8},{12,14},{14,12},{1,3},{3,1},... | collective-permute-start | bytes 208904 | tf_op jit(solution)/shard_map/ppermute | solution.py:379
  16.8 2.7 %collective-permute-done.5 = f32[136,128]{1,0:T(8,128)S(1)} collective-permute-done((f32[136,128]{1,0:T(8,128)S(1)}, f32[136,128]{1,0:T(8,128)S(1)}, u32[]{:S(2)}, u32[]{:S(2)}) %collective-permute-start.5) | collective-permute-done | bytes 69664 | tf_op jit(solution)/shard_map/ppermute | solution.py:379
  19.5 2.0 %collective-permute-start.6 = (f32[136,128]{1,0:T(8,128)S(1)}, f32[136,128]{1,0:T(8,128)S(1)}, u32[]{:S(2)}, u32[]{:S(2)}) collective-permute-start(f32[136,128]{1,0:T(8,128)S(1)} %fusion), channel_id=1, source_target_pairs={{0,4},{2,6},{4,0},{6,2},{8,12},{10,14},{12,8},{14,10},{1,5},{3,7},... | collective-permute-start | bytes 208904 | tf_op jit(solution)/shard_map/ppermute | solution.py:379
  21.5 2.4 %collective-permute-done.6 = f32[136,128]{1,0:T(8,128)S(1)} collective-permute-done((f32[136,128]{1,0:T(8,128)S(1)}, f32[136,128]{1,0:T(8,128)S(1)}, u32[]{:S(2)}, u32[]{:S(2)}) %collective-permute-start.6) | collective-permute-done | bytes 69664 | tf_op jit(solution)/shard_map/ppermute | solution.py:379
  23.9 3.2 %collective-permute-start.7 = (f32[136,128]{1,0:T(8,128)S(1)}, f32[136,128]{1,0:T(8,128)S(1)}, u32[]{:S(2)}, u32[]{:S(2)}) collective-permute-start(f32[136,128]{1,0:T(8,128)S(1)} %add.14), channel_id=1, source_target_pairs={{0,8},{2,10},{4,12},{6,14},{8,0},{10,2},{12,4},{14,6},{1,9},{3,11}... | collective-permute-start | bytes 208904 | tf_op jit(solution)/shard_map/ppermute | solution.py:379
  27.1 2.3 %collective-permute-done.7 = f32[136,128]{1,0:T(8,128)S(1)} collective-permute-done((f32[136,128]{1,0:T(8,128)S(1)}, f32[136,128]{1,0:T(8,128)S(1)}, u32[]{:S(2)}, u32[]{:S(2)}) %collective-permute-start.7) | collective-permute-done | bytes 69664 | tf_op jit(solution)/shard_map/ppermute | solution.py:379
  29.5 1.1 %shard_map.61.code_ref = s32[24,128]{1,0:T(8,128)S(1)} custom-call(s32[6,4,128]{2,1,0:T(4,128)S(1)} %copy-done.1), custom_call_target="tpu_custom_call" | custom-call | tf_op jit(solution)/shard_map/pallas_call | solution.py:331
  30.5 0.2 collective-permute-done.8.theirs_ref
  30.7 8.2 %shard_map.62 = (f32[24,16,128]{2,1,0:T(8,128)}, f32[1,128]{1,0:T(1,128)}) custom-call(s32[3]{0:T(128)S(1)} %pad_add_fusion.place_ref, f32[136,128]{1,0:T(8,128)S(1)} %add.15.mine_ref, f32[136,128]{1,0:T(8,128)S(1)} %collective-permute-done.8.theirs_ref, s32[24,128]{1,0:T(8,128)S(1)} %shard_map.61.code_ref, f32[24,16,128]{2,1,0:T(8,128)S(1)} %get-tuple-element.14.own_ref, ...), custom_call_target="tpu_custom_call" | custom-call | tf_op jit(solution)/shard_map/pallas_call | solution.py:382
  (13 shorter events, 0.1 us)
Async XLA Ops:
  0.6 3.1 %collective-permute-start.1 = (f32[24,16,128]{2,1,0:T(8,128)}, f32[24,16,128]{2,1,0:T(8,128)S(1)}, u32[]{:S(2)}, u32[]{:S(2)}) collective-permute-start(f32[24,16,128]{2,1,0:T(8,128)} %bitcast.8), channel_id=1, source_target_pairs={{0,1},{1,0},{2,3},{3,2},{4,5},{5,4},{6,7},{7,6},{8,9},{9,8},{10,11... | collective-permute-start | bytes 589832 | tf_op jit(solution)/shard_map/ppermute | solution.py:326
  1.1 10.2 %collective-permute-start.2 = (f32[24,16,128]{2,1,0:T(8,128)}, f32[24,16,128]{2,1,0:T(8,128)S(1)}, u32[]{:S(2)}, u32[]{:S(2)}) collective-permute-start(f32[24,16,128]{2,1,0:T(8,128)} %bitcast.9), channel_id=1, source_target_pairs={{4,0},{6,2},{8,4},{10,6},{12,8},{14,10},{5,1},{7,3},{9,5},{11,7},{... | collective-permute-start | bytes 589832 | tf_op jit(solution)/shard_map/ppermute | solution.py:325
  2.4 6.3 %collective-permute-start = (s32[16,24]{1,0:T(8,128)}, s32[16,24]{1,0:T(8,128)S(1)}, u32[]{:S(2)}, u32[]{:S(2)}) collective-permute-start(s32[16,24]{1,0:T(8,128)} %bitcast.11), channel_id=1, source_target_pairs={{2,0},{4,2},{6,4},{8,6},{10,8},{12,10},{14,12},{1,3},{3,5},{5,7},{... | collective-permute-start | bytes 4616 | tf_op jit(solution)/shard_map/ppermute | solution.py:338
  3.8 0.9 %copy-start = (f32[1,24,16,128]{3,2,1,0:T(8,128)S(1)}, f32[1,24,16,128]{3,2,1,0:T(8,128)}, u32[]{:S(2)}) copy-start(f32[1,24,16,128]{3,2,1,0:T(8,128)} %param.4) | copy-start | bytes 589828
  4.7 0.7 %copy-start.2 = (s32[1,24,16]{1,2,0:T(8,128)S(1)}, s32[1,24,16]{1,2,0:T(8,128)}, u32[]{:S(2)}) copy-start(s32[1,24,16]{1,2,0:T(8,128)} %param.5) | copy-start | bytes 4612
  5.4 0.7 %copy-start.3 = (f32[8]{0:T(128)S(1)}, f32[8]{0:T(128)}, u32[]{:S(2)}) copy-start(f32[8]{0:T(128)} %conductivity_ref.1) | copy-start | bytes 100
  8.7 3.3 %collective-permute-start.3 = (s32[16,24]{1,0:T(8,128)S(1)}, s32[16,24]{1,0:T(8,128)S(1)}, u32[]{:S(2)}, u32[]{:S(2)}) collective-permute-start(s32[16,24]{1,0:T(8,128)S(1)} %collective-permute-done.mine_ref), channel_id=1, source_target_pairs={{0,1},{1,0},{2,3},{3,2},{4,5},{5,4},{6,7},{7,6},{8,9},{9,8},{10,11... | collective-permute-start | bytes 4616 | tf_op jit(solution)/shard_map/ppermute | solution.py:363
  12.0 17.5 %copy-start.1 = (s32[6,4,128]{2,1,0:T(4,128)S(1)}, s32[6,4,128]{2,1,0:T(4,128)}, u32[]{:S(2)}) copy-start(s32[6,4,128]{2,1,0:T(4,128)} %pairing_ref.1) | copy-start | bytes 36868
  13.3 1.3 %collective-permute-start.4 = (f32[64,128]{1,0:T(8,128)S(1)}, f32[64,128]{1,0:T(8,128)S(1)}, u32[]{:S(2)}, u32[]{:S(2)}) collective-permute-start(f32[64,128]{1,0:T(8,128)S(1)} %get-tuple-element.19), channel_id=1, source_target_pairs={{0,1},{1,0},{2,3},{3,2},{4,5},{5,4},{6,7},{7,6},{8,9},{9,8},{10,11... | collective-permute-start | bytes 98312 | tf_op jit(solution)/shard_map/ppermute | solution.py:375
  14.6 4.9 %collective-permute-start.5 = (f32[136,128]{1,0:T(8,128)S(1)}, f32[136,128]{1,0:T(8,128)S(1)}, u32[]{:S(2)}, u32[]{:S(2)}) collective-permute-start(f32[136,128]{1,0:T(8,128)S(1)} %pad_maximum_fusion), channel_id=1, source_target_pairs={{0,2},{2,0},{4,6},{6,4},{8,10},{10,8},{12,14},{14,12},{1,3},{3,1},... | collective-permute-start | bytes 208904 | tf_op jit(solution)/shard_map/ppermute | solution.py:379
  19.5 4.4 %collective-permute-start.6 = (f32[136,128]{1,0:T(8,128)S(1)}, f32[136,128]{1,0:T(8,128)S(1)}, u32[]{:S(2)}, u32[]{:S(2)}) collective-permute-start(f32[136,128]{1,0:T(8,128)S(1)} %fusion), channel_id=1, source_target_pairs={{0,4},{2,6},{4,0},{6,2},{8,12},{10,14},{12,8},{14,10},{1,5},{3,7},... | collective-permute-start | bytes 208904 | tf_op jit(solution)/shard_map/ppermute | solution.py:379
  23.9 5.5 %collective-permute-start.7 = (f32[136,128]{1,0:T(8,128)S(1)}, f32[136,128]{1,0:T(8,128)S(1)}, u32[]{:S(2)}, u32[]{:S(2)}) collective-permute-start(f32[136,128]{1,0:T(8,128)S(1)} %add.14), channel_id=1, source_target_pairs={{0,8},{2,10},{4,12},{6,14},{8,0},{10,2},{12,4},{14,6},{1,9},{3,11}... | collective-permute-start | bytes 208904 | tf_op jit(solution)/shard_map/ppermute | solution.py:379
  29.4 1.3 %collective-permute-start.8 = (f32[136,128]{1,0:T(8,128)S(1)}, f32[136,128]{1,0:T(8,128)S(1)}, u32[]{:S(2)}, u32[]{:S(2)}) collective-permute-start(f32[136,128]{1,0:T(8,128)S(1)} %add.15.mine_ref), channel_id=1, source_target_pairs={{0,1},{1,0},{2,3},{3,2},{4,5},{5,4},{6,7},{7,6},{8,9},{9,8},{10,11... | collective-permute-start | bytes 208904 | tf_op jit(solution)/shard_map/ppermute | solution.py:381

commit v5 on v4

--- a/solution.py
+++ b/solution.py
@@ -206,14 +206,16 @@
     zero_side = jnp.where(side, mine, theirs)
     one_side = jnp.where(side, theirs, mine)
     eye = lax.broadcasted_iota(jnp.int32, (n, n), 0) == lax.broadcasted_iota(jnp.int32, (n, n), 1)
-    row = lax.broadcasted_iota(jnp.int32, (n, n), 0)
     blank = jnp.zeros((n, n), jnp.float32)
     low_half = lax.broadcasted_iota(jnp.int32, (h, n), 1) < h
     low = lax.broadcasted_iota(jnp.int32, (2 * n, n), 1) < h
 
-    cross01 = jnp.concatenate([zero_side[h + 8 :], one_side[h + 8 :]], axis=0)
+    tiles = range(n // 8)
+    rows = [lax.broadcasted_iota(jnp.int32, (8, n), 0) + 8 * i for i in tiles]
+    cols = lax.broadcasted_iota(jnp.int32, (8, n), 1)
     near = [unpacked(zero_side), unpacked(one_side)]
-    cross = [cross01.T, cross01]
+    cross = jnp.concatenate([zero_side[h + 8 :], one_side[h + 8 :]], axis=0)
+    diagonal = [column_sums(jnp.where(eye, near[d], 0.0)) for d in range(2)]
     total = None
     slots = [[0, 1], [2, 3]]
     upper, lower = [0, 2], [1, 3]
@@ -222,34 +224,44 @@
         uppers = {frozenset((upper[d], lower[d])): upper[d] for d in range(2)}
         swapped = [uppers[frozenset(slots[d])] != slots[d][0] for d in range(2)]
         factor = [None, None]
-        diagonal = [column_sums(jnp.where(eye, near[d], 0.0)) for d in range(2)]
+        near = [[near[d][8 * i : 8 * i + 8] for i in tiles] for d in range(2)]
+        cross = [cross[8 * i : 8 * i + 8] for i in tiles]
         for turn in range(turns):
             index = meeting * turns + turn
-            told = code_ref[index : index + 1, :]
-            other_way = pltpu.roll(jnp.broadcast_to(told, (8, n)), h, 1)[:1]
+            told = jnp.broadcast_to(code_ref[index : index + 1, :], (8, n))
+            other_way = pltpu.roll(told, h, 1)
             for d in range(2):
                 partner = (other_way % n) ^ h if swapped[d] else told % n
                 first = (other_way if swapped[d] else told) >= n
                 if turn == 0:
-                    paired = row == partner
-                    coupling = column_sums(jnp.where(paired, near[d], 0.0))
+                    coupling = [
+                        jnp.where(rows[i] == partner, near[d][i], 0.0) for i in tiles
+                    ]
                 else:
-                    opposite = lanes(factor[d], partner)
-                    coupling = column_sums(opposite * near[d])
+                    opposite = [lanes(part, partner) for part in factor[d]]
+                    coupling = [left * right for left, right in zip(opposite, near[d])]
+                while len(coupling) > 1:
+                    coupling = [a + b for a, b in zip(coupling[::2], coupling[1::2])]
+                coupling = column_sums(coupling[0])
                 across = lanes(diagonal[d], partner)
                 cosine, sine = rotation(diagonal[d], across, coupling, first)
                 diagonal[d] = (
                     cosine * cosine * diagonal[d] + 2.0 * cosine * sine * coupling + sine * sine * across
                 )
-                cosine, sine = cosine[:1], sine[:1]
                 if turn == 0:
-                    factor[d] = jnp.where(eye, cosine, jnp.where(paired, sine, 0.0))
+                    factor[d] = [
+                        jnp.where(rows[i] == cols, cosine, jnp.where(rows[i] == partner, sine, 0.0))
+                        for i in tiles
+                    ]
                 else:
-                    factor[d] = factor[d] * cosine + opposite * sine
+                    factor[d] = [
+                        part * cosine + away * sine for part, away in zip(factor[d], opposite)
+                    ]
                 if not last or turn < turns - 1:
-                    near[d] = near[d] * cosine + lanes(near[d], partner) * sine
-                if not last:
-                    cross[d] = cross[d] * cosine + lanes(cross[d], partner) * sine
+                    near[d] = [part * cosine + lanes(part, partner) * sine for part in near[d]]
+                if not last and d == 1:
+                    cross = [part * cosine + lanes(part, partner) * sine for part in cross]
+        factor = [jnp.concatenate(factor[d], axis=0) for d in range(2)]
         if last:
             break
         if total is None:
@@ -259,9 +271,12 @@
             ]
         else:
             total = [long_dot(total[d], factor[d], TWO) for d in range(2)]
-        top = long_dot(factor[0].T, jnp.concatenate([near[0], cross[1]], axis=1), THREE)
-        bottom = long_dot(factor[1].T, jnp.concatenate([cross[0], near[1]], axis=1), THREE)
-        g00, g01, g10, g11 = top[:, :n], top[:, n:], bottom[:, :n], bottom[:, n:]
+        near = [jnp.concatenate(near[d], axis=0) for d in range(2)]
+        cross = jnp.concatenate(cross, axis=0)
+        top = long_dot(factor[0].T, jnp.concatenate([near[0], cross], axis=1), THREE)
+        g00, g01 = top[:, :n], top[:, n:]
+        g11 = long_dot(factor[1].T, near[1], THREE)
+        g10 = g01.T
         upper, lower = [upper[0], lower[0]], [lower[1], upper[1]]
         meets_next = [frozenset((upper[d], lower[d])) for d in range(2)]
         if frozenset((slots[0][0], slots[1][1])) not in meets_next:
@@ -270,6 +285,7 @@
             g10 = jnp.concatenate([g10[h:], g10[:h]], axis=0)
             g11 = jnp.concatenate([g11[h:], g11[:h]], axis=0)
             total[1] = pltpu.roll(total[1], h, 1)
+            diagonal[1] = pltpu.roll(diagonal[1], h, 1)
         slots = [[slots[0][0], slots[1][1]], [slots[1][0], slots[0][1]]]
 
         def mixed(first, second, third, fourth):
@@ -282,7 +298,11 @@
             )
 
         near = [mixed(g00, g01, g10, g11), mixed(g11, g10, g01, g00)]
-        cross = [mixed(g10, g11, g00, g01), mixed(g01, g00, g11, g10)]
+        cross = mixed(g01, g00, g11, g10)
+        diagonal = [
+            jnp.where(cols < h, diagonal[0], diagonal[1]),
+            jnp.where(cols < h, diagonal[1], diagonal[0]),
+        ]
         total = [jnp.where(low, total[0], total[1]), jnp.where(low, total[1], total[0])]
 
     flat = jnp.concatenate(
@@ -358,7 +378,7 @@
             pltpu.SemaphoreType.DMA((3,)),
         ],
         compiler_params=PARAMS,
-    )(conductivity, own, labels, other)
+    )(*[pltpu.with_memory_space_constraint(value, pltpu.HBM) for value in (conductivity, own, labels)], other)
     beside, table = lax.optimization_barrier((beside, table))
     across = lax.ppermute(beside, "cols", swap)
     kept, sent = pl.pallas_call(

time: 39.2 us -> 38.2 us (0.974)
  waiting for transfers between devices: 10.1 us -> 14.2 us
  starting transfers between devices: 13.5 us -> 11 us
  local copies, waits for them, and re-layouts: 2.28 us -> 0.01 us
    unnamed x8 -> x2, local copies, waits for them, and re-layouts: 2.27 us -> 0.01 us
    ppermute x1, starting transfers between devices: 2.46 us -> 0.35 us  [shards(): across = lax.ppermute(beside, 'cols', swap)]
    ppermute x1, waiting for transfers between devices: 0.17 us -> 2.28 us  [shards(): halo = lax.ppermute(own, 'rows', [(i + 2, i) for i in range(count - 2)])]
    ppermute x1, waiting for transfers between devices: 0.95 us -> 3.05 us  [shards(): lax.ppermute(labels, ('rows', 'cols'), [(2 * (i + 1), 2 * i) for i in ran...]
    ppermute x1, waiting for transfers between devices: 0.58 us -> 0.01 us  [shards(): across = lax.ppermute(beside, 'cols', swap)]
    pallas_call x1, Pallas kernels: 8.19 us -> 7.68 us  [shards(): pl.pallas_call(functools.partial(tournament_kernel, pairing.shape[0], pai...]
  transfers between devices with their start and end apart: 9 -> 9, of which waited for: 8 -> 7; matrix products, arithmetic and copies ran while one was open for 0% -> 0% of each run, Pallas kernels for 7% -> 8%
where the time goes in v5:
time: 38.2 us; the launch traced here: 38 us
  waiting for transfers between devices  14.2 us (37%)
  Pallas kernels  11.9 us (31%)
  starting transfers between devices  11 us (29%)
  between operations  0.73 us (2%)
    pallas_call x1, Pallas kernels, shards(): pl.pallas_call(functools.partial(tournament_kernel, pairing.shape[0], pai...  7.68 us
    ppermute x3, waiting for transfers between devices, shards(): lax.ppermute(share, 'rows', [(i, i ^ apart) for i in range(count)])  7.55 us
    ppermute x3, starting transfers between devices, shards(): lax.ppermute(share, 'rows', [(i, i ^ apart) for i in range(count)])  7.4 us
    ppermute x1, waiting for transfers between devices, shards(): lax.ppermute(labels, ('rows', 'cols'), [(2 * (i + 1), 2 * i) for i in ran...  3.05 us
    ppermute x1, waiting for transfers between devices, shards(): halo = lax.ppermute(own, 'rows', [(i + 2, i) for i in range(count - 2)])  2.28 us
    pallas_call x1, Pallas kernels, shards(): pl.pallas_call(local_kernel, out_shape=(jax.ShapeDtypeStruct((2 * width,...  1.88 us
    ppermute x1, starting transfers between devices, shards(): lax.ppermute(labels, ('rows', 'cols'), [(2 * (i + 1), 2 * i) for i in ran...  1.29 us
    pallas_call x1, Pallas kernels, shards(): pl.pallas_call(halo_kernel, out_shape=(jax.ShapeDtypeStruct((width + 8, w...  1.29 us
  transfers between devices with their start and end apart: 9, of which 7 were waited for; matrix products, arithmetic and copies ran while one was open for 0% of the time, Pallas kernels for 8%

profile of v5, /device:TPU:0, one launch (start us, length us, event | category | flops | bytes accessed | tf_op | source)
XLA Modules:
  0.0 38.0 jit_solution(12148341992500004411)
XLA Ops:
  0.6 0.5 %collective-permute-start.1 = (f32[24,16,128]{2,1,0:T(8,128)}, f32[24,16,128]{2,1,0:T(8,128)S(1)}, u32[]{:S(2)}, u32[]{:S(2)}) collective-permute-start(f32[24,16,128]{2,1,0:T(8,128)} %bitcast.8), channel_id=1, source_target_pairs={{0,1},{1,0},{2,3},{3,2},{4,5},{5,4},{6,7},{7,6},{8,9},{9,8},{10,11... | collective-permute-start | bytes 589832 | tf_op jit(solution)/shard_map/ppermute | solution.py:346
  1.1 1.3 %collective-permute-start.2 = (f32[24,16,128]{2,1,0:T(8,128)}, f32[24,16,128]{2,1,0:T(8,128)S(1)}, u32[]{:S(2)}, u32[]{:S(2)}) collective-permute-start(f32[24,16,128]{2,1,0:T(8,128)} %bitcast.9), channel_id=1, source_target_pairs={{4,0},{6,2},{8,4},{10,6},{12,8},{14,10},{5,1},{7,3},{9,5},{11,7},{... | collective-permute-start | bytes 589832 | tf_op jit(solution)/shard_map/ppermute | solution.py:345
  2.4 1.3 %collective-permute-start = (s32[16,24]{1,0:T(8,128)}, s32[16,24]{1,0:T(8,128)S(1)}, u32[]{:S(2)}, u32[]{:S(2)}) collective-permute-start(s32[16,24]{1,0:T(8,128)} %bitcast.11), channel_id=1, source_target_pairs={{2,0},{4,2},{6,4},{8,6},{10,8},{12,10},{14,12},{1,3},{3,5},{5,7},{... | collective-permute-start | bytes 4616 | tf_op jit(solution)/shard_map/ppermute | solution.py:358
  3.7 0.0 collective-permute-done.1.other_ref
  3.8 1.9 %shard_map.59 = (f32[256,128]{1,0:T(8,128)S(1)}, bf16[256,2304]{1,0:T(8,128)(2,1)S(1)}, f32[24,16,128]{2,1,0:T(8,128)S(1)}, f32[8,128]{1,0:T(8,128)S(1)}) custom-call(f32[8]{0:T(128)} %conductivity_ref.1, f32[24,16,128]{2,1,0:T(8,128)} %bitcast.10, s32[16,24]{1,0:T(8,128)} %bitcast.12, f32[24,16,128]{2,1,0:T(8,128)S(1)} %collective-permute-done.1.other_ref), custom_call_target="tpu_custom_call" | custom-call | tf_op jit(solution)/shard_map/pallas_call | solution.py:364
  5.6 3.1 %collective-permute-done.mine_ref = s32[16,24]{1,0:T(8,128)S(1)} collective-permute-done((s32[16,24]{1,0:T(8,128)}, s32[16,24]{1,0:T(8,128)S(1)}, u32[]{:S(2)}, u32[]{:S(2)}) %collective-permute-start) | collective-permute-done | bytes 1568 | tf_op jit(solution)/shard_map/ppermute | solution.py:358
  8.7 0.3 collective-permute-start.3
  9.0 0.1 pad_add_fusion.place_ref
  9.1 2.3 %collective-permute-done.2.halo_ref = f32[24,16,128]{2,1,0:T(8,128)S(1)} collective-permute-done((f32[24,16,128]{2,1,0:T(8,128)}, f32[24,16,128]{2,1,0:T(8,128)S(1)}, u32[]{:S(2)}, u32[]{:S(2)}) %collective-permute-start.2) | collective-permute-done | bytes 196640 | tf_op jit(solution)/shard_map/ppermute | solution.py:345
  11.4 0.0 collective-permute-done.3.theirs_ref
  11.4 1.3 %shard_map.60 = (f32[136,128]{1,0:T(8,128)S(1)}, f32[64,128]{1,0:T(8,128)S(1)}) custom-call(s32[3]{0:T(128)S(1)} %pad_add_fusion.place_ref, f32[8,128]{1,0:T(8,128)S(1)} %get-tuple-element.13.table_ref, f32[24,16,128]{2,1,0:T(8,128)S(1)} %get-tuple-element.14.own_ref, f32[24,16,128]{2,1,0:T(8,128)S(1)} %collective-permute-done.2.halo_ref, ...), custom_call_target="tpu_custom_call" | custom-call | tf_op jit(solution)/shard_map/pallas_call | solution.py:384
  12.7 0.1 collective-permute-start.4
  12.8 1.2 %collective-permute-done.4 = f32[64,128]{1,0:T(8,128)S(1)} collective-permute-done((f32[64,128]{1,0:T(8,128)S(1)}, f32[64,128]{1,0:T(8,128)S(1)}, u32[]{:S(2)}, u32[]{:S(2)}) %collective-permute-start.4) | collective-permute-done | bytes 32800 | tf_op jit(solution)/shard_map/ppermute | solution.py:395
  14.0 2.8 %collective-permute-start.5 = (f32[136,128]{1,0:T(8,128)S(1)}, f32[136,128]{1,0:T(8,128)S(1)}, u32[]{:S(2)}, u32[]{:S(2)}) collective-permute-start(f32[136,128]{1,0:T(8,128)S(1)} %pad_maximum_fusion), channel_id=1, source_target_pairs={{0,2},{2,0},{4,6},{6,4},{8,10},{10,8},{12,14},{14,12},{1,3},{3,1},... | collective-permute-start | bytes 208904 | tf_op jit(solution)/shard_map/ppermute | solution.py:399
  16.8 2.5 %collective-permute-done.5 = f32[136,128]{1,0:T(8,128)S(1)} collective-permute-done((f32[136,128]{1,0:T(8,128)S(1)}, f32[136,128]{1,0:T(8,128)S(1)}, u32[]{:S(2)}, u32[]{:S(2)}) %collective-permute-start.5) | collective-permute-done | bytes 69664 | tf_op jit(solution)/shard_map/ppermute | solution.py:399
  19.3 1.8 %collective-permute-start.6 = (f32[136,128]{1,0:T(8,128)S(1)}, f32[136,128]{1,0:T(8,128)S(1)}, u32[]{:S(2)}, u32[]{:S(2)}) collective-permute-start(f32[136,128]{1,0:T(8,128)S(1)} %fusion), channel_id=1, source_target_pairs={{0,4},{2,6},{4,0},{6,2},{8,12},{10,14},{12,8},{14,10},{1,5},{3,7},... | collective-permute-start | bytes 208904 | tf_op jit(solution)/shard_map/ppermute | solution.py:399
  21.1 2.6 %collective-permute-done.6 = f32[136,128]{1,0:T(8,128)S(1)} collective-permute-done((f32[136,128]{1,0:T(8,128)S(1)}, f32[136,128]{1,0:T(8,128)S(1)}, u32[]{:S(2)}, u32[]{:S(2)}) %collective-permute-start.6) | collective-permute-done | bytes 69664 | tf_op jit(solution)/shard_map/ppermute | solution.py:399
  23.7 2.8 %collective-permute-start.7 = (f32[136,128]{1,0:T(8,128)S(1)}, f32[136,128]{1,0:T(8,128)S(1)}, u32[]{:S(2)}, u32[]{:S(2)}) collective-permute-start(f32[136,128]{1,0:T(8,128)S(1)} %add.14), channel_id=1, source_target_pairs={{0,8},{2,10},{4,12},{6,14},{8,0},{10,2},{12,4},{14,6},{1,9},{3,11}... | collective-permute-start | bytes 208904 | tf_op jit(solution)/shard_map/ppermute | solution.py:399
  26.5 2.5 %collective-permute-done.7 = f32[136,128]{1,0:T(8,128)S(1)} collective-permute-done((f32[136,128]{1,0:T(8,128)S(1)}, f32[136,128]{1,0:T(8,128)S(1)}, u32[]{:S(2)}, u32[]{:S(2)}) %collective-permute-start.7) | collective-permute-done | bytes 69664 | tf_op jit(solution)/shard_map/ppermute | solution.py:399
  29.0 0.1 collective-permute-start.8
  29.0 0.0 copy-done
  29.1 1.1 %shard_map.61.code_ref = s32[24,128]{1,0:T(8,128)S(1)} custom-call(s32[6,4,128]{2,1,0:T(4,128)S(1)} %copy-done), custom_call_target="tpu_custom_call" | custom-call | tf_op jit(solution)/shard_map/pallas_call | solution.py:351
  30.1 0.2 collective-permute-done.8.theirs_ref
  30.3 7.7 %shard_map.62 = (f32[24,16,128]{2,1,0:T(8,128)}, f32[1,128]{1,0:T(1,128)}) custom-call(s32[3]{0:T(128)S(1)} %pad_add_fusion.place_ref, f32[136,128]{1,0:T(8,128)S(1)} %add.15.mine_ref, f32[136,128]{1,0:T(8,128)S(1)} %collective-permute-done.8.theirs_ref, s32[24,128]{1,0:T(8,128)S(1)} %shard_map.61.code_ref, f32[24,16,128]{2,1,0:T(8,128)S(1)} %get-tuple-element.14.own_ref, ...), custom_call_target="tpu_custom_call" | custom-call | tf_op jit(solution)/shard_map/pallas_call | solution.py:402
  (7 shorter events, 0.1 us)
Async XLA Ops:
  0.6 3.1 %collective-permute-start.1 = (f32[24,16,128]{2,1,0:T(8,128)}, f32[24,16,128]{2,1,0:T(8,128)S(1)}, u32[]{:S(2)}, u32[]{:S(2)}) collective-permute-start(f32[24,16,128]{2,1,0:T(8,128)} %bitcast.8), channel_id=1, source_target_pairs={{0,1},{1,0},{2,3},{3,2},{4,5},{5,4},{6,7},{7,6},{8,9},{9,8},{10,11... | collective-permute-start | bytes 589832 | tf_op jit(solution)/shard_map/ppermute | solution.py:346
  1.1 10.2 %collective-permute-start.2 = (f32[24,16,128]{2,1,0:T(8,128)}, f32[24,16,128]{2,1,0:T(8,128)S(1)}, u32[]{:S(2)}, u32[]{:S(2)}) collective-permute-start(f32[24,16,128]{2,1,0:T(8,128)} %bitcast.9), channel_id=1, source_target_pairs={{4,0},{6,2},{8,4},{10,6},{12,8},{14,10},{5,1},{7,3},{9,5},{11,7},{... | collective-permute-start | bytes 589832 | tf_op jit(solution)/shard_map/ppermute | solution.py:345
  2.4 6.3 %collective-permute-start = (s32[16,24]{1,0:T(8,128)}, s32[16,24]{1,0:T(8,128)S(1)}, u32[]{:S(2)}, u32[]{:S(2)}) collective-permute-start(s32[16,24]{1,0:T(8,128)} %bitcast.11), channel_id=1, source_target_pairs={{2,0},{4,2},{6,4},{8,6},{10,8},{12,10},{14,12},{1,3},{3,5},{5,7},{... | collective-permute-start | bytes 4616 | tf_op jit(solution)/shard_map/ppermute | solution.py:358
  8.7 2.7 %collective-permute-start.3 = (s32[16,24]{1,0:T(8,128)S(1)}, s32[16,24]{1,0:T(8,128)S(1)}, u32[]{:S(2)}, u32[]{:S(2)}) collective-permute-start(s32[16,24]{1,0:T(8,128)S(1)} %collective-permute-done.mine_ref), channel_id=1, source_target_pairs={{0,1},{1,0},{2,3},{3,2},{4,5},{5,4},{6,7},{7,6},{8,9},{9,8},{10,11... | collective-permute-start | bytes 4616 | tf_op jit(solution)/shard_map/ppermute | solution.py:383
  11.4 17.7 %copy-start = (s32[6,4,128]{2,1,0:T(4,128)S(1)}, s32[6,4,128]{2,1,0:T(4,128)}, u32[]{:S(2)}) copy-start(s32[6,4,128]{2,1,0:T(4,128)} %pairing_ref.1) | copy-start | bytes 36868
  12.7 1.3 %collective-permute-start.4 = (f32[64,128]{1,0:T(8,128)S(1)}, f32[64,128]{1,0:T(8,128)S(1)}, u32[]{:S(2)}, u32[]{:S(2)}) collective-permute-start(f32[64,128]{1,0:T(8,128)S(1)} %get-tuple-element.19), channel_id=1, source_target_pairs={{0,1},{1,0},{2,3},{3,2},{4,5},{5,4},{6,7},{7,6},{8,9},{9,8},{10,11... | collective-permute-start | bytes 98312 | tf_op jit(solution)/shard_map/ppermute | solution.py:395
  14.0 5.3 %collective-permute-start.5 = (f32[136,128]{1,0:T(8,128)S(1)}, f32[136,128]{1,0:T(8,128)S(1)}, u32[]{:S(2)}, u32[]{:S(2)}) collective-permute-start(f32[136,128]{1,0:T(8,128)S(1)} %pad_maximum_fusion), channel_id=1, source_target_pairs={{0,2},{2,0},{4,6},{6,4},{8,10},{10,8},{12,14},{14,12},{1,3},{3,1},... | collective-permute-start | bytes 208904 | tf_op jit(solution)/shard_map/ppermute | solution.py:399
  19.3 4.4 %collective-permute-start.6 = (f32[136,128]{1,0:T(8,128)S(1)}, f32[136,128]{1,0:T(8,128)S(1)}, u32[]{:S(2)}, u32[]{:S(2)}) collective-permute-start(f32[136,128]{1,0:T(8,128)S(1)} %fusion), channel_id=1, source_target_pairs={{0,4},{2,6},{4,0},{6,2},{8,12},{10,14},{12,8},{14,10},{1,5},{3,7},... | collective-permute-start | bytes 208904 | tf_op jit(solution)/shard_map/ppermute | solution.py:399
  23.7 5.3 %collective-permute-start.7 = (f32[136,128]{1,0:T(8,128)S(1)}, f32[136,128]{1,0:T(8,128)S(1)}, u32[]{:S(2)}, u32[]{:S(2)}) collective-permute-start(f32[136,128]{1,0:T(8,128)S(1)} %add.14), channel_id=1, source_target_pairs={{0,8},{2,10},{4,12},{6,14},{8,0},{10,2},{12,4},{14,6},{1,9},{3,11}... | collective-permute-start | bytes 208904 | tf_op jit(solution)/shard_map/ppermute | solution.py:399
  29.0 1.3 %collective-permute-start.8 = (f32[136,128]{1,0:T(8,128)S(1)}, f32[136,128]{1,0:T(8,128)S(1)}, u32[]{:S(2)}, u32[]{:S(2)}) collective-permute-start(f32[136,128]{1,0:T(8,128)S(1)} %add.15.mine_ref), channel_id=1, source_target_pairs={{0,1},{1,0},{2,3},{3,2},{4,5},{5,4},{6,7},{7,6},{8,9},{9,8},{10,11... | collective-permute-start | bytes 208904 | tf_op jit(solution)/shard_map/ppermute | solution.py:401

commit v6 on v5

--- a/solution.py
+++ b/solution.py
@@ -125,37 +125,45 @@
 
 def halo_kernel(
     place_ref, table_ref, own_ref, halo_ref, mine_ref, theirs_ref, gram_ref, turned_ref,
-    kept_ref, sent_ref, applied_ref,
+    parts_ref, cross_ref, sent_ref, applied_ref,
 ):
     ny, nz, width = own_ref.shape
     mine = quarter_squares(mine_ref[...], table_ref[...])
     theirs = quarter_squares(theirs_ref[...], table_ref[...])
-    after = jnp.where(place_ref[0] == 0, mine, theirs)
-    before = jnp.where(place_ref[0] == 0, theirs, mine)
+    ahead_first = place_ref[0] == place_ref[1] % 2
+    after = jnp.where(ahead_first, mine, theirs)
+    before = jnp.where(ahead_first, theirs, mine)
     after = jnp.where(place_ref[1] < place_ref[2] - 1, after, 0.0)
     before = jnp.where(place_ref[1] > 0, before, 0.0)
+    around = after + before
+    after = 2.0 * after
     for y in range(ny):
-        ahead = after[:, y : y + 1]
-        applied_ref[y * nz : (y + 1) * nz, :] = (ahead + before[:, y : y + 1]) * own_ref[y] - (
-            2.0 * ahead
-        ) * halo_ref[y]
-    gram = gram_ref[...] + jnp.dot(
-        turned_ref[...],
-        laid(split(applied_ref[...], 3), THREE, 1, 0),
-        preferred_element_type=jnp.float32,
-    )
+        applied_ref[y * nz : (y + 1) * nz, :] = (
+            around[:, y : y + 1] * own_ref[y] - after[:, y : y + 1] * halo_ref[y]
+        )
+    parts = laid(split(applied_ref[...], 3), THREE, 1, 0)
+    parts_ref[...] = parts
     half = width // 2
     first = place_ref[0] == 0
-    own = gram[:width]
-    cross = gram[width:]
+    cross = gram_ref[width:, :] + jnp.dot(
+        turned_ref[width:, :], parts, preferred_element_type=jnp.float32
+    )
     cross = 0.5 * jnp.where(first, cross.T, cross)
+    cross_ref[...] = jnp.where(first, cross[:half], cross[half:])
+    sent_ref[...] = jnp.where(first, cross[half:], cross[:half])
+
+
+def own_kernel(gram_ref, turned_ref, parts_ref, packed_ref):
+    width = parts_ref.shape[1]
+    half = width // 2
+    own = gram_ref[:width, :] + jnp.dot(
+        turned_ref[:width, :], parts_ref[...], preferred_element_type=jnp.float32
+    )
     own = 0.5 * (own + own.T)
     row = lax.broadcasted_iota(jnp.int32, (half, width), 0)
     col = lax.broadcasted_iota(jnp.int32, (half, width), 1)
-    kept_ref[:half, :] = jnp.where(
-        (col >= row), own[:half], pltpu.roll(own[half:], half, 1)
-    )
-    kept_ref[half : half + 8, :] = column_sums(
+    packed_ref[:half, :] = jnp.where(col >= row, own[:half], pltpu.roll(own[half:], half, 1))
+    packed_ref[half:, :] = column_sums(
         jnp.where(
             lax.broadcasted_iota(jnp.int32, (width, width), 0)
             == lax.broadcasted_iota(jnp.int32, (width, width), 1),
@@ -163,8 +171,6 @@
             0.0,
         )
     )
-    kept_ref[half + 8 :, :] = jnp.where(first, cross[:half], cross[half:])
-    sent_ref[...] = jnp.where(first, cross[half:], cross[:half])
 
 
 def unpacked(share):
@@ -358,8 +364,8 @@
     beside = lax.ppermute(
         labels,
         ("rows", "cols"),
-        [(2 * (i + 1), 2 * i) for i in range(count - 1)]
-        + [(2 * i + 1, 2 * (i + 1) + 1) for i in range(count - 1)],
+        [(2 * i, 2 * (i ^ 1)) for i in range(count)]
+        + [(2 * i + 1, 2 * (i + (1 if i % 2 else -1)) + 1) for i in range(1, count - 1)],
     )
     gram, turned, own, table = pl.pallas_call(
         local_kernel,
@@ -381,19 +387,27 @@
     )(*[pltpu.with_memory_space_constraint(value, pltpu.HBM) for value in (conductivity, own, labels)], other)
     beside, table = lax.optimization_barrier((beside, table))
     across = lax.ppermute(beside, "cols", swap)
-    kept, sent = pl.pallas_call(
+    parts, cross, sent = pl.pallas_call(
         halo_kernel,
         out_shape=(
-            jax.ShapeDtypeStruct((width + 8, width), jnp.float32),
+            jax.ShapeDtypeStruct((len(THREE) * cells, width), jnp.bfloat16),
+            jax.ShapeDtypeStruct((half, width), jnp.float32),
             jax.ShapeDtypeStruct((half, width), jnp.float32),
         ),
         in_specs=[SMEM] + [VMEM] * 7,
-        out_specs=[VMEM] * 2,
+        out_specs=[VMEM] * 3,
         scratch_shapes=[pltpu.VMEM((cells, width), jnp.float32)],
         compiler_params=PARAMS,
     )(place, table, own, halo, beside, across, gram, turned)
     received = lax.ppermute(sent, "cols", swap)
-    share = jnp.concatenate([kept[: half + 8], kept[half + 8 :] + received], axis=0)
+    packed = pl.pallas_call(
+        own_kernel,
+        out_shape=jax.ShapeDtypeStruct((half + 8, width), jnp.float32),
+        in_specs=[VMEM] * 3,
+        out_specs=VMEM,
+        compiler_params=PARAMS,
+    )(gram, turned, parts)
+    share = jnp.concatenate([packed, cross + received], axis=0)
     apart = 1
     while apart < count:
         share = share + lax.ppermute(share, "rows", [(i, i ^ apart) for i in range(count)])

time: 38.2 us -> 37.5 us (0.982)
  waiting for transfers between devices: 14.2 us -> 11.6 us
  starting transfers between devices: 11 us -> 12.7 us
    ppermute x1, starting transfers between devices: 1.29 us -> 4.42 us  [shards(): lax.ppermute(labels, ('rows', 'cols'), [(2 * i, 2 * (i ^ 1)) for i in ran...]
    ppermute x1, waiting for transfers between devices: 3.05 us -> 0.01 us  [shards(): lax.ppermute(labels, ('rows', 'cols'), [(2 * i, 2 * (i ^ 1)) for i in ran...]
    ppermute x3, starting transfers between devices: 7.4 us -> 6.26 us  [shards(): lax.ppermute(share, 'rows', [(i, i ^ apart) for i in range(count)])]
    ppermute x3, waiting for transfers between devices: 7.55 us -> 8.13 us  [shards(): lax.ppermute(share, 'rows', [(i, i ^ apart) for i in range(count)])]
    ppermute x1, waiting for transfers between devices: 1.18 us -> 0.73 us  [shards(): received = lax.ppermute(sent, 'cols', swap)]
    pallas_call x1 -> x2, Pallas kernels: 1.29 us -> 1.56 us  [the longest x1 1.11 us: shards(): pl.pallas_call(halo_kernel, out_shape=(jax.ShapeDtypeStruct((len(THREE) *...]
  transfers between devices with their start and end apart: 9 -> 9, of which waited for: 7 -> 6; matrix products, arithmetic and copies ran while one was open for 0% -> 0% of each run, Pallas kernels for 8% -> 9%
where the time goes in v6:
time: 37.5 us; the launch traced here: 37.3 us
  starting transfers between devices  12.7 us (34%)
  Pallas kernels  12.2 us (33%)
  waiting for transfers between devices  11.6 us (31%)
  between operations  0.75 us (2%)
    ppermute x3, waiting for transfers between devices, shards(): lax.ppermute(share, 'rows', [(i, i ^ apart) for i in range(count)])  8.13 us
    pallas_call x1, Pallas kernels, shards(): pl.pallas_call(functools.partial(tournament_kernel, pairing.shape[0], pai...  7.69 us
    ppermute x3, starting transfers between devices, shards(): lax.ppermute(share, 'rows', [(i, i ^ apart) for i in range(count)])  6.26 us
    ppermute x1, starting transfers between devices, shards(): lax.ppermute(labels, ('rows', 'cols'), [(2 * i, 2 * (i ^ 1)) for i in ran...  4.42 us
    ppermute x1, waiting for transfers between devices, shards(): halo = lax.ppermute(own, 'rows', [(i + 2, i) for i in range(count - 2)])  2.55 us
    pallas_call x1, Pallas kernels, shards(): pl.pallas_call(local_kernel, out_shape=(jax.ShapeDtypeStruct((2 * width,...  1.88 us
    ppermute x1, starting transfers between devices, shards(): halo = lax.ppermute(own, 'rows', [(i + 2, i) for i in range(count - 2)])  1.28 us
    pallas_call x1, Pallas kernels, shards(): pl.pallas_call(halo_kernel, out_shape=(jax.ShapeDtypeStruct((len(THREE) *...  1.11 us
  transfers between devices with their start and end apart: 9, of which 6 were waited for; matrix products, arithmetic and copies ran while one was open for 0% of the time, Pallas kernels for 9%

profile of v6, /device:TPU:0, one launch (start us, length us, event | category | flops | bytes accessed | tf_op | source)
XLA Modules:
  0.0 37.3 jit_solution(6846066179865620571)
XLA Ops:
  0.6 0.5 %collective-permute-start = (f32[24,16,128]{2,1,0:T(8,128)}, f32[24,16,128]{2,1,0:T(8,128)S(1)}, u32[]{:S(2)}, u32[]{:S(2)}) collective-permute-start(f32[24,16,128]{2,1,0:T(8,128)} %bitcast.8), channel_id=1, source_target_pairs={{0,1},{1,0},{2,3},{3,2},{4,5},{5,4},{6,7},{7,6},{8,9},{9,8},{10,11... | collective-permute-start | bytes 589832 | tf_op jit(solution)/shard_map/ppermute | solution.py:352
  1.1 1.3 %collective-permute-start.2 = (f32[24,16,128]{2,1,0:T(8,128)}, f32[24,16,128]{2,1,0:T(8,128)S(1)}, u32[]{:S(2)}, u32[]{:S(2)}) collective-permute-start(f32[24,16,128]{2,1,0:T(8,128)} %bitcast.9), channel_id=1, source_target_pairs={{4,0},{6,2},{8,4},{10,6},{12,8},{14,10},{5,1},{7,3},{9,5},{11,7},{... | collective-permute-start | bytes 589832 | tf_op jit(solution)/shard_map/ppermute | solution.py:351
  2.4 4.4 %collective-permute-start.1 = (s32[16,24]{1,0:T(8,128)}, s32[16,24]{1,0:T(8,128)S(1)}, u32[]{:S(2)}, u32[]{:S(2)}) collective-permute-start(s32[16,24]{1,0:T(8,128)} %bitcast.11), channel_id=1, source_target_pairs={{0,2},{2,0},{4,6},{6,4},{8,10},{10,8},{12,14},{14,12},{3,5},{5,3},... | collective-permute-start | bytes 4616 | tf_op jit(solution)/shard_map/ppermute | solution.py:364
  6.9 0.0 collective-permute-done.other_ref
  6.9 1.9 %shard_map.59 = (f32[256,128]{1,0:T(8,128)S(1)}, bf16[256,2304]{1,0:T(8,128)(2,1)S(1)}, f32[24,16,128]{2,1,0:T(8,128)S(1)}, f32[8,128]{1,0:T(8,128)S(1)}) custom-call(f32[8]{0:T(128)} %conductivity_ref.1, f32[24,16,128]{2,1,0:T(8,128)} %bitcast.10, s32[16,24]{1,0:T(8,128)} %bitcast.12, f32[24,16,128]{2,1,0:T(8,128)S(1)} %collective-permute-done.other_ref), custom_call_target="tpu_custom_call" | custom-call | tf_op jit(solution)/shard_map/pallas_call | solution.py:370
  8.8 0.0 collective-permute-done.1.mine_ref
  8.8 0.1 collective-permute-start.3
  8.9 0.1 pad_add_fusion.place_ref
  8.9 2.5 %collective-permute-done.2.halo_ref = f32[24,16,128]{2,1,0:T(8,128)S(1)} collective-permute-done((f32[24,16,128]{2,1,0:T(8,128)}, f32[24,16,128]{2,1,0:T(8,128)S(1)}, u32[]{:S(2)}, u32[]{:S(2)}) %collective-permute-start.2) | collective-permute-done | bytes 196640 | tf_op jit(solution)/shard_map/ppermute | solution.py:351
  11.5 1.1 %shard_map.60 = (bf16[2304,128]{1,0:T(8,128)(2,1)S(1)}, f32[64,128]{1,0:T(8,128)S(1)}, f32[64,128]{1,0:T(8,128)S(1)}) custom-call(s32[3]{0:T(128)S(1)} %pad_add_fusion.place_ref, f32[8,128]{1,0:T(8,128)S(1)} %get-tuple-element.16.table_ref, f32[24,16,128]{2,1,0:T(8,128)S(1)} %get-tuple-element.17.own_ref, ...), custom_call_target="tpu_custom_call" | custom-call | tf_op jit(solution)/shard_map/pallas_call | solution.py:390
  12.6 0.1 collective-permute-start.4
  12.7 0.0 copy-start
  12.7 0.4 %shard_map.61 = f32[72,128]{1,0:T(8,128)S(1)} custom-call(f32[256,128]{1,0:T(8,128)S(1)} %get-tuple-element.13.gram_ref, bf16[256,2304]{1,0:T(8,128)(2,1)S(1)} %get-tuple-element.14.turned_ref, bf16[2304,128]{1,0:T(8,128)(2,1)S(1)} %get-tuple-element.19.parts_ref), custom_call_target="tpu_custom_call" | custom-call | tf_op jit(solution)/shard_map/pallas_call | solution.py:403
  13.1 0.7 %collective-permute-done.4 = f32[64,128]{1,0:T(8,128)S(1)} collective-permute-done((f32[64,128]{1,0:T(8,128)S(1)}, f32[64,128]{1,0:T(8,128)S(1)}, u32[]{:S(2)}, u32[]{:S(2)}) %collective-permute-start.4) | collective-permute-done | bytes 32800 | tf_op jit(solution)/shard_map/ppermute | solution.py:402
  13.9 2.1 %collective-permute-start.5 = (f32[136,128]{1,0:T(8,128)S(1)}, f32[136,128]{1,0:T(8,128)S(1)}, u32[]{:S(2)}, u32[]{:S(2)}) collective-permute-start(f32[136,128]{1,0:T(8,128)S(1)} %pad_maximum_fusion), channel_id=1, source_target_pairs={{0,2},{2,0},{4,6},{6,4},{8,10},{10,8},{12,14},{14,12},{1,3},{3,1},... | collective-permute-start | bytes 208904 | tf_op jit(solution)/shard_map/ppermute | solution.py:413
  15.9 2.7 %collective-permute-done.5 = f32[136,128]{1,0:T(8,128)S(1)} collective-permute-done((f32[136,128]{1,0:T(8,128)S(1)}, f32[136,128]{1,0:T(8,128)S(1)}, u32[]{:S(2)}, u32[]{:S(2)}) %collective-permute-start.5) | collective-permute-done | bytes 69664 | tf_op jit(solution)/shard_map/ppermute | solution.py:413
  18.6 1.6 %collective-permute-start.6 = (f32[136,128]{1,0:T(8,128)S(1)}, f32[136,128]{1,0:T(8,128)S(1)}, u32[]{:S(2)}, u32[]{:S(2)}) collective-permute-start(f32[136,128]{1,0:T(8,128)S(1)} %fusion), channel_id=1, source_target_pairs={{0,4},{2,6},{4,0},{6,2},{8,12},{10,14},{12,8},{14,10},{1,5},{3,7},... | collective-permute-start | bytes 208904 | tf_op jit(solution)/shard_map/ppermute | solution.py:413
  20.2 2.8 %collective-permute-done.6 = f32[136,128]{1,0:T(8,128)S(1)} collective-permute-done((f32[136,128]{1,0:T(8,128)S(1)}, f32[136,128]{1,0:T(8,128)S(1)}, u32[]{:S(2)}, u32[]{:S(2)}) %collective-permute-start.6) | collective-permute-done | bytes 69664 | tf_op jit(solution)/shard_map/ppermute | solution.py:413
  23.0 2.6 %collective-permute-start.7 = (f32[136,128]{1,0:T(8,128)S(1)}, f32[136,128]{1,0:T(8,128)S(1)}, u32[]{:S(2)}, u32[]{:S(2)}) collective-permute-start(f32[136,128]{1,0:T(8,128)S(1)} %add.14), channel_id=1, source_target_pairs={{0,8},{2,10},{4,12},{6,14},{8,0},{10,2},{12,4},{14,6},{1,9},{3,11}... | collective-permute-start | bytes 208904 | tf_op jit(solution)/shard_map/ppermute | solution.py:413
  25.6 2.7 %collective-permute-done.7 = f32[136,128]{1,0:T(8,128)S(1)} collective-permute-done((f32[136,128]{1,0:T(8,128)S(1)}, f32[136,128]{1,0:T(8,128)S(1)}, u32[]{:S(2)}, u32[]{:S(2)}) %collective-permute-start.7) | collective-permute-done | bytes 69664 | tf_op jit(solution)/shard_map/ppermute | solution.py:413
  28.3 0.1 collective-permute-start.8
  28.4 1.1 %shard_map.62.code_ref = s32[24,128]{1,0:T(8,128)S(1)} custom-call(s32[6,4,128]{2,1,0:T(4,128)S(1)} %copy-done), custom_call_target="tpu_custom_call" | custom-call | tf_op jit(solution)/shard_map/pallas_call | solution.py:357
  29.5 0.2 collective-permute-done.8.theirs_ref
  29.7 7.7 %shard_map.63 = (f32[24,16,128]{2,1,0:T(8,128)}, f32[1,128]{1,0:T(1,128)}) custom-call(s32[3]{0:T(128)S(1)} %pad_add_fusion.place_ref, f32[136,128]{1,0:T(8,128)S(1)} %add.15.mine_ref, f32[136,128]{1,0:T(8,128)S(1)} %collective-permute-done.8.theirs_ref, s32[24,128]{1,0:T(8,128)S(1)} %shard_map.62.code_ref, f32[24,16,128]{2,1,0:T(8,128)S(1)} %get-tuple-element.17.own_ref, ...), custom_call_target="tpu_custom_call" | custom-call | tf_op jit(solution)/shard_map/pallas_call | solution.py:416
  (7 shorter events, 0.0 us)
Async XLA Ops:
  0.6 6.2 %collective-permute-start = (f32[24,16,128]{2,1,0:T(8,128)}, f32[24,16,128]{2,1,0:T(8,128)S(1)}, u32[]{:S(2)}, u32[]{:S(2)}) collective-permute-start(f32[24,16,128]{2,1,0:T(8,128)} %bitcast.8), channel_id=1, source_target_pairs={{0,1},{1,0},{2,3},{3,2},{4,5},{5,4},{6,7},{7,6},{8,9},{9,8},{10,11... | collective-permute-start | bytes 589832 | tf_op jit(solution)/shard_map/ppermute | solution.py:352
  1.1 10.3 %collective-permute-start.2 = (f32[24,16,128]{2,1,0:T(8,128)}, f32[24,16,128]{2,1,0:T(8,128)S(1)}, u32[]{:S(2)}, u32[]{:S(2)}) collective-permute-start(f32[24,16,128]{2,1,0:T(8,128)} %bitcast.9), channel_id=1, source_target_pairs={{4,0},{6,2},{8,4},{10,6},{12,8},{14,10},{5,1},{7,3},{9,5},{11,7},{... | collective-permute-start | bytes 589832 | tf_op jit(solution)/shard_map/ppermute | solution.py:351
  2.4 6.3 %collective-permute-start.1 = (s32[16,24]{1,0:T(8,128)}, s32[16,24]{1,0:T(8,128)S(1)}, u32[]{:S(2)}, u32[]{:S(2)}) collective-permute-start(s32[16,24]{1,0:T(8,128)} %bitcast.11), channel_id=1, source_target_pairs={{0,2},{2,0},{4,6},{6,4},{8,10},{10,8},{12,14},{14,12},{3,5},{5,3},... | collective-permute-start | bytes 4616 | tf_op jit(solution)/shard_map/ppermute | solution.py:364
  8.8 2.7 %collective-permute-start.3 = (s32[16,24]{1,0:T(8,128)S(1)}, s32[16,24]{1,0:T(8,128)S(1)}, u32[]{:S(2)}, u32[]{:S(2)}) collective-permute-start(s32[16,24]{1,0:T(8,128)S(1)} %collective-permute-done.1.mine_ref), channel_id=1, source_target_pairs={{0,1},{1,0},{2,3},{3,2},{4,5},{5,4},{6,7},{7,6},{8,9},{9,8},{10,11... | collective-permute-start | bytes 4616 | tf_op jit(solution)/shard_map/ppermute | solution.py:389
  12.6 1.3 %collective-permute-start.4 = (f32[64,128]{1,0:T(8,128)S(1)}, f32[64,128]{1,0:T(8,128)S(1)}, u32[]{:S(2)}, u32[]{:S(2)}) collective-permute-start(f32[64,128]{1,0:T(8,128)S(1)} %get-tuple-element.21), channel_id=1, source_target_pairs={{0,1},{1,0},{2,3},{3,2},{4,5},{5,4},{6,7},{7,6},{8,9},{9,8},{10,11... | collective-permute-start | bytes 98312 | tf_op jit(solution)/shard_map/ppermute | solution.py:402
  12.7 15.7 %copy-start = (s32[6,4,128]{2,1,0:T(4,128)S(1)}, s32[6,4,128]{2,1,0:T(4,128)}, u32[]{:S(2)}) copy-start(s32[6,4,128]{2,1,0:T(4,128)} %pairing_ref.1) | copy-start | bytes 36868
  13.9 4.7 %collective-permute-start.5 = (f32[136,128]{1,0:T(8,128)S(1)}, f32[136,128]{1,0:T(8,128)S(1)}, u32[]{:S(2)}, u32[]{:S(2)}) collective-permute-start(f32[136,128]{1,0:T(8,128)S(1)} %pad_maximum_fusion), channel_id=1, source_target_pairs={{0,2},{2,0},{4,6},{6,4},{8,10},{10,8},{12,14},{14,12},{1,3},{3,1},... | collective-permute-start | bytes 208904 | tf_op jit(solution)/shard_map/ppermute | solution.py:413
  18.6 4.4 %collective-permute-start.6 = (f32[136,128]{1,0:T(8,128)S(1)}, f32[136,128]{1,0:T(8,128)S(1)}, u32[]{:S(2)}, u32[]{:S(2)}) collective-permute-start(f32[136,128]{1,0:T(8,128)S(1)} %fusion), channel_id=1, source_target_pairs={{0,4},{2,6},{4,0},{6,2},{8,12},{10,14},{12,8},{14,10},{1,5},{3,7},... | collective-permute-start | bytes 208904 | tf_op jit(solution)/shard_map/ppermute | solution.py:413
  23.0 5.3 %collective-permute-start.7 = (f32[136,128]{1,0:T(8,128)S(1)}, f32[136,128]{1,0:T(8,128)S(1)}, u32[]{:S(2)}, u32[]{:S(2)}) collective-permute-start(f32[136,128]{1,0:T(8,128)S(1)} %add.14), channel_id=1, source_target_pairs={{0,8},{2,10},{4,12},{6,14},{8,0},{10,2},{12,4},{14,6},{1,9},{3,11}... | collective-permute-start | bytes 208904 | tf_op jit(solution)/shard_map/ppermute | solution.py:413
  28.3 1.3 %collective-permute-start.8 = (f32[136,128]{1,0:T(8,128)S(1)}, f32[136,128]{1,0:T(8,128)S(1)}, u32[]{:S(2)}, u32[]{:S(2)}) collective-permute-start(f32[136,128]{1,0:T(8,128)S(1)} %add.15.mine_ref), channel_id=1, source_target_pairs={{0,1},{1,0},{2,3},{3,2},{4,5},{5,4},{6,7},{7,6},{8,9},{9,8},{10,11... | collective-permute-start | bytes 208904 | tf_op jit(solution)/shard_map/ppermute | solution.py:415

commit v7 on v6

--- a/solution.py
+++ b/solution.py
@@ -270,13 +270,6 @@
         factor = [jnp.concatenate(factor[d], axis=0) for d in range(2)]
         if last:
             break
-        if total is None:
-            total = [
-                jnp.concatenate([factor[0], blank], axis=0),
-                jnp.concatenate([blank, factor[1]], axis=0),
-            ]
-        else:
-            total = [long_dot(total[d], factor[d], TWO) for d in range(2)]
         near = [jnp.concatenate(near[d], axis=0) for d in range(2)]
         cross = jnp.concatenate(cross, axis=0)
         top = long_dot(factor[0].T, jnp.concatenate([near[0], cross], axis=1), THREE)
@@ -285,12 +278,12 @@
         g10 = g01.T
         upper, lower = [upper[0], lower[0]], [lower[1], upper[1]]
         meets_next = [frozenset((upper[d], lower[d])) for d in range(2)]
-        if frozenset((slots[0][0], slots[1][1])) not in meets_next:
+        rolled = frozenset((slots[0][0], slots[1][1])) not in meets_next
+        if rolled:
             slots[1] = slots[1][::-1]
             g01, g11 = pltpu.roll(g01, h, 1), pltpu.roll(g11, h, 1)
             g10 = jnp.concatenate([g10[h:], g10[:h]], axis=0)
             g11 = jnp.concatenate([g11[h:], g11[:h]], axis=0)
-            total[1] = pltpu.roll(total[1], h, 1)
             diagonal[1] = pltpu.roll(diagonal[1], h, 1)
         slots = [[slots[0][0], slots[1][1]], [slots[1][0], slots[0][1]]]
 
@@ -309,6 +302,15 @@
             jnp.where(cols < h, diagonal[0], diagonal[1]),
             jnp.where(cols < h, diagonal[1], diagonal[0]),
         ]
+        if total is None:
+            total = [
+                jnp.concatenate([factor[0], blank], axis=0),
+                jnp.concatenate([blank, factor[1]], axis=0),
+            ]
+        else:
+            total = [long_dot(total[d], factor[d], TWO) for d in range(2)]
+        if rolled:
+            total[1] = pltpu.roll(total[1], h, 1)
         total = [jnp.where(low, total[0], total[1]), jnp.where(low, total[1], total[0])]
 
     flat = jnp.concatenate(

time: 37.5 us -> 37.1 us (0.989)
  Pallas kernels: 12.2 us -> 11.8 us
    pallas_call x1, Pallas kernels: 7.69 us -> 7.3 us  [shards(): pl.pallas_call(functools.partial(tournament_kernel, pairing.shape[0], pai...]
where the time goes in v7:
time: 37.1 us; the launch traced here: 37 us
  starting transfers between devices  12.7 us (34%)
  Pallas kernels  11.8 us (32%)
  waiting for transfers between devices  11.6 us (31%)
  between operations  0.75 us (2%)
    ppermute x3, waiting for transfers between devices, shards(): lax.ppermute(share, 'rows', [(i, i ^ apart) for i in range(count)])  8.13 us
    pallas_call x1, Pallas kernels, shards(): pl.pallas_call(functools.partial(tournament_kernel, pairing.shape[0], pai...  7.3 us
    ppermute x3, starting transfers between devices, shards(): lax.ppermute(share, 'rows', [(i, i ^ apart) for i in range(count)])  6.26 us
    ppermute x1, starting transfers between devices, shards(): lax.ppermute(labels, ('rows', 'cols'), [(2 * i, 2 * (i ^ 1)) for i in ran...  4.42 us
    ppermute x1, waiting for transfers between devices, shards(): halo = lax.ppermute(own, 'rows', [(i + 2, i) for i in range(count - 2)])  2.55 us
    pallas_call x1, Pallas kernels, shards(): pl.pallas_call(local_kernel, out_shape=(jax.ShapeDtypeStruct((2 * width,...  1.88 us
    ppermute x1, starting transfers between devices, shards(): halo = lax.ppermute(own, 'rows', [(i + 2, i) for i in range(count - 2)])  1.28 us
    pallas_call x1, Pallas kernels, shards(): pl.pallas_call(halo_kernel, out_shape=(jax.ShapeDtypeStruct((len(THREE) *...  1.11 us
  transfers between devices with their start and end apart: 9, of which 6 were waited for; matrix products, arithmetic and copies ran while one was open for 0% of the time, Pallas kernels for 9%

profile of v7, /device:TPU:0, one launch (start us, length us, event | category | flops | bytes accessed | tf_op | source)
XLA Modules:
  0.0 37.0 jit_solution(8429660388358047365)
XLA Ops:
  0.6 0.5 %collective-permute-start = (f32[24,16,128]{2,1,0:T(8,128)}, f32[24,16,128]{2,1,0:T(8,128)S(1)}, u32[]{:S(2)}, u32[]{:S(2)}) collective-permute-start(f32[24,16,128]{2,1,0:T(8,128)} %bitcast.8), channel_id=1, source_target_pairs={{0,1},{1,0},{2,3},{3,2},{4,5},{5,4},{6,7},{7,6},{8,9},{9,8},{10,11... | collective-permute-start | bytes 589832 | tf_op jit(solution)/shard_map/ppermute | solution.py:354
  1.1 1.3 %collective-permute-start.2 = (f32[24,16,128]{2,1,0:T(8,128)}, f32[24,16,128]{2,1,0:T(8,128)S(1)}, u32[]{:S(2)}, u32[]{:S(2)}) collective-permute-start(f32[24,16,128]{2,1,0:T(8,128)} %bitcast.9), channel_id=1, source_target_pairs={{4,0},{6,2},{8,4},{10,6},{12,8},{14,10},{5,1},{7,3},{9,5},{11,7},{... | collective-permute-start | bytes 589832 | tf_op jit(solution)/shard_map/ppermute | solution.py:353
  2.4 4.4 %collective-permute-start.1 = (s32[16,24]{1,0:T(8,128)}, s32[16,24]{1,0:T(8,128)S(1)}, u32[]{:S(2)}, u32[]{:S(2)}) collective-permute-start(s32[16,24]{1,0:T(8,128)} %bitcast.11), channel_id=1, source_target_pairs={{0,2},{2,0},{4,6},{6,4},{8,10},{10,8},{12,14},{14,12},{3,5},{5,3},... | collective-permute-start | bytes 4616 | tf_op jit(solution)/shard_map/ppermute | solution.py:366
  6.9 0.0 collective-permute-done.other_ref
  6.9 1.9 %shard_map.59 = (f32[256,128]{1,0:T(8,128)S(1)}, bf16[256,2304]{1,0:T(8,128)(2,1)S(1)}, f32[24,16,128]{2,1,0:T(8,128)S(1)}, f32[8,128]{1,0:T(8,128)S(1)}) custom-call(f32[8]{0:T(128)} %conductivity_ref.1, f32[24,16,128]{2,1,0:T(8,128)} %bitcast.10, s32[16,24]{1,0:T(8,128)} %bitcast.12, f32[24,16,128]{2,1,0:T(8,128)S(1)} %collective-permute-done.other_ref), custom_call_target="tpu_custom_call" | custom-call | tf_op jit(solution)/shard_map/pallas_call | solution.py:372
  8.8 0.0 collective-permute-done.1.mine_ref
  8.8 0.1 collective-permute-start.3
  8.9 0.1 pad_add_fusion.place_ref
  8.9 2.5 %collective-permute-done.2.halo_ref = f32[24,16,128]{2,1,0:T(8,128)S(1)} collective-permute-done((f32[24,16,128]{2,1,0:T(8,128)}, f32[24,16,128]{2,1,0:T(8,128)S(1)}, u32[]{:S(2)}, u32[]{:S(2)}) %collective-permute-start.2) | collective-permute-done | bytes 196640 | tf_op jit(solution)/shard_map/ppermute | solution.py:353
  11.5 1.1 %shard_map.60 = (bf16[2304,128]{1,0:T(8,128)(2,1)S(1)}, f32[64,128]{1,0:T(8,128)S(1)}, f32[64,128]{1,0:T(8,128)S(1)}) custom-call(s32[3]{0:T(128)S(1)} %pad_add_fusion.place_ref, f32[8,128]{1,0:T(8,128)S(1)} %get-tuple-element.16.table_ref, f32[24,16,128]{2,1,0:T(8,128)S(1)} %get-tuple-element.17.own_ref, ...), custom_call_target="tpu_custom_call" | custom-call | tf_op jit(solution)/shard_map/pallas_call | solution.py:392
  12.6 0.1 collective-permute-start.4
  12.7 0.0 copy-start
  12.7 0.4 %shard_map.61 = f32[72,128]{1,0:T(8,128)S(1)} custom-call(f32[256,128]{1,0:T(8,128)S(1)} %get-tuple-element.13.gram_ref, bf16[256,2304]{1,0:T(8,128)(2,1)S(1)} %get-tuple-element.14.turned_ref, bf16[2304,128]{1,0:T(8,128)(2,1)S(1)} %get-tuple-element.19.parts_ref), custom_call_target="tpu_custom_call" | custom-call | tf_op jit(solution)/shard_map/pallas_call | solution.py:405
  13.1 0.7 %collective-permute-done.4 = f32[64,128]{1,0:T(8,128)S(1)} collective-permute-done((f32[64,128]{1,0:T(8,128)S(1)}, f32[64,128]{1,0:T(8,128)S(1)}, u32[]{:S(2)}, u32[]{:S(2)}) %collective-permute-start.4) | collective-permute-done | bytes 32800 | tf_op jit(solution)/shard_map/ppermute | solution.py:404
  13.9 2.1 %collective-permute-start.5 = (f32[136,128]{1,0:T(8,128)S(1)}, f32[136,128]{1,0:T(8,128)S(1)}, u32[]{:S(2)}, u32[]{:S(2)}) collective-permute-start(f32[136,128]{1,0:T(8,128)S(1)} %pad_maximum_fusion), channel_id=1, source_target_pairs={{0,2},{2,0},{4,6},{6,4},{8,10},{10,8},{12,14},{14,12},{1,3},{3,1},... | collective-permute-start | bytes 208904 | tf_op jit(solution)/shard_map/ppermute | solution.py:415
  15.9 2.7 %collective-permute-done.5 = f32[136,128]{1,0:T(8,128)S(1)} collective-permute-done((f32[136,128]{1,0:T(8,128)S(1)}, f32[136,128]{1,0:T(8,128)S(1)}, u32[]{:S(2)}, u32[]{:S(2)}) %collective-permute-start.5) | collective-permute-done | bytes 69664 | tf_op jit(solution)/shard_map/ppermute | solution.py:415
  18.6 1.6 %collective-permute-start.6 = (f32[136,128]{1,0:T(8,128)S(1)}, f32[136,128]{1,0:T(8,128)S(1)}, u32[]{:S(2)}, u32[]{:S(2)}) collective-permute-start(f32[136,128]{1,0:T(8,128)S(1)} %fusion), channel_id=1, source_target_pairs={{0,4},{2,6},{4,0},{6,2},{8,12},{10,14},{12,8},{14,10},{1,5},{3,7},... | collective-permute-start | bytes 208904 | tf_op jit(solution)/shard_map/ppermute | solution.py:415
  20.2 2.8 %collective-permute-done.6 = f32[136,128]{1,0:T(8,128)S(1)} collective-permute-done((f32[136,128]{1,0:T(8,128)S(1)}, f32[136,128]{1,0:T(8,128)S(1)}, u32[]{:S(2)}, u32[]{:S(2)}) %collective-permute-start.6) | collective-permute-done | bytes 69664 | tf_op jit(solution)/shard_map/ppermute | solution.py:415
  23.0 2.6 %collective-permute-start.7 = (f32[136,128]{1,0:T(8,128)S(1)}, f32[136,128]{1,0:T(8,128)S(1)}, u32[]{:S(2)}, u32[]{:S(2)}) collective-permute-start(f32[136,128]{1,0:T(8,128)S(1)} %add.14), channel_id=1, source_target_pairs={{0,8},{2,10},{4,12},{6,14},{8,0},{10,2},{12,4},{14,6},{1,9},{3,11}... | collective-permute-start | bytes 208904 | tf_op jit(solution)/shard_map/ppermute | solution.py:415
  25.6 2.7 %collective-permute-done.7 = f32[136,128]{1,0:T(8,128)S(1)} collective-permute-done((f32[136,128]{1,0:T(8,128)S(1)}, f32[136,128]{1,0:T(8,128)S(1)}, u32[]{:S(2)}, u32[]{:S(2)}) %collective-permute-start.7) | collective-permute-done | bytes 69664 | tf_op jit(solution)/shard_map/ppermute | solution.py:415
  28.3 0.1 collective-permute-start.8
  28.4 1.1 %shard_map.62.code_ref = s32[24,128]{1,0:T(8,128)S(1)} custom-call(s32[6,4,128]{2,1,0:T(4,128)S(1)} %copy-done), custom_call_target="tpu_custom_call" | custom-call | tf_op jit(solution)/shard_map/pallas_call | solution.py:359
  29.5 0.2 collective-permute-done.8.theirs_ref
  29.7 7.3 %shard_map.63 = (f32[24,16,128]{2,1,0:T(8,128)}, f32[1,128]{1,0:T(1,128)}) custom-call(s32[3]{0:T(128)S(1)} %pad_add_fusion.place_ref, f32[136,128]{1,0:T(8,128)S(1)} %add.15.mine_ref, f32[136,128]{1,0:T(8,128)S(1)} %collective-permute-done.8.theirs_ref, s32[24,128]{1,0:T(8,128)S(1)} %shard_map.62.code_ref, f32[24,16,128]{2,1,0:T(8,128)S(1)} %get-tuple-element.17.own_ref, ...), custom_call_target="tpu_custom_call" | custom-call | tf_op jit(solution)/shard_map/pallas_call | solution.py:418
  (7 shorter events, 0.0 us)
Async XLA Ops:
  0.6 6.2 %collective-permute-start = (f32[24,16,128]{2,1,0:T(8,128)}, f32[24,16,128]{2,1,0:T(8,128)S(1)}, u32[]{:S(2)}, u32[]{:S(2)}) collective-permute-start(f32[24,16,128]{2,1,0:T(8,128)} %bitcast.8), channel_id=1, source_target_pairs={{0,1},{1,0},{2,3},{3,2},{4,5},{5,4},{6,7},{7,6},{8,9},{9,8},{10,11... | collective-permute-start | bytes 589832 | tf_op jit(solution)/shard_map/ppermute | solution.py:354
  1.1 10.3 %collective-permute-start.2 = (f32[24,16,128]{2,1,0:T(8,128)}, f32[24,16,128]{2,1,0:T(8,128)S(1)}, u32[]{:S(2)}, u32[]{:S(2)}) collective-permute-start(f32[24,16,128]{2,1,0:T(8,128)} %bitcast.9), channel_id=1, source_target_pairs={{4,0},{6,2},{8,4},{10,6},{12,8},{14,10},{5,1},{7,3},{9,5},{11,7},{... | collective-permute-start | bytes 589832 | tf_op jit(solution)/shard_map/ppermute | solution.py:353
  2.4 6.3 %collective-permute-start.1 = (s32[16,24]{1,0:T(8,128)}, s32[16,24]{1,0:T(8,128)S(1)}, u32[]{:S(2)}, u32[]{:S(2)}) collective-permute-start(s32[16,24]{1,0:T(8,128)} %bitcast.11), channel_id=1, source_target_pairs={{0,2},{2,0},{4,6},{6,4},{8,10},{10,8},{12,14},{14,12},{3,5},{5,3},... | collective-permute-start | bytes 4616 | tf_op jit(solution)/shard_map/ppermute | solution.py:366
  8.8 2.7 %collective-permute-start.3 = (s32[16,24]{1,0:T(8,128)S(1)}, s32[16,24]{1,0:T(8,128)S(1)}, u32[]{:S(2)}, u32[]{:S(2)}) collective-permute-start(s32[16,24]{1,0:T(8,128)S(1)} %collective-permute-done.1.mine_ref), channel_id=1, source_target_pairs={{0,1},{1,0},{2,3},{3,2},{4,5},{5,4},{6,7},{7,6},{8,9},{9,8},{10,11... | collective-permute-start | bytes 4616 | tf_op jit(solution)/shard_map/ppermute | solution.py:391
  12.6 1.3 %collective-permute-start.4 = (f32[64,128]{1,0:T(8,128)S(1)}, f32[64,128]{1,0:T(8,128)S(1)}, u32[]{:S(2)}, u32[]{:S(2)}) collective-permute-start(f32[64,128]{1,0:T(8,128)S(1)} %get-tuple-element.21), channel_id=1, source_target_pairs={{0,1},{1,0},{2,3},{3,2},{4,5},{5,4},{6,7},{7,6},{8,9},{9,8},{10,11... | collective-permute-start | bytes 98312 | tf_op jit(solution)/shard_map/ppermute | solution.py:404
  12.7 15.7 %copy-start = (s32[6,4,128]{2,1,0:T(4,128)S(1)}, s32[6,4,128]{2,1,0:T(4,128)}, u32[]{:S(2)}) copy-start(s32[6,4,128]{2,1,0:T(4,128)} %pairing_ref.1) | copy-start | bytes 36868
  13.9 4.7 %collective-permute-start.5 = (f32[136,128]{1,0:T(8,128)S(1)}, f32[136,128]{1,0:T(8,128)S(1)}, u32[]{:S(2)}, u32[]{:S(2)}) collective-permute-start(f32[136,128]{1,0:T(8,128)S(1)} %pad_maximum_fusion), channel_id=1, source_target_pairs={{0,2},{2,0},{4,6},{6,4},{8,10},{10,8},{12,14},{14,12},{1,3},{3,1},... | collective-permute-start | bytes 208904 | tf_op jit(solution)/shard_map/ppermute | solution.py:415
  18.6 4.4 %collective-permute-start.6 = (f32[136,128]{1,0:T(8,128)S(1)}, f32[136,128]{1,0:T(8,128)S(1)}, u32[]{:S(2)}, u32[]{:S(2)}) collective-permute-start(f32[136,128]{1,0:T(8,128)S(1)} %fusion), channel_id=1, source_target_pairs={{0,4},{2,6},{4,0},{6,2},{8,12},{10,14},{12,8},{14,10},{1,5},{3,7},... | collective-permute-start | bytes 208904 | tf_op jit(solution)/shard_map/ppermute | solution.py:415
  23.0 5.3 %collective-permute-start.7 = (f32[136,128]{1,0:T(8,128)S(1)}, f32[136,128]{1,0:T(8,128)S(1)}, u32[]{:S(2)}, u32[]{:S(2)}) collective-permute-start(f32[136,128]{1,0:T(8,128)S(1)} %add.14), channel_id=1, source_target_pairs={{0,8},{2,10},{4,12},{6,14},{8,0},{10,2},{12,4},{14,6},{1,9},{3,11}... | collective-permute-start | bytes 208904 | tf_op jit(solution)/shard_map/ppermute | solution.py:415
  28.3 1.3 %collective-permute-start.8 = (f32[136,128]{1,0:T(8,128)S(1)}, f32[136,128]{1,0:T(8,128)S(1)}, u32[]{:S(2)}, u32[]{:S(2)}) collective-permute-start(f32[136,128]{1,0:T(8,128)S(1)} %add.15.mine_ref), channel_id=1, source_target_pairs={{0,1},{1,0},{2,3},{3,2},{4,5},{5,4},{6,7},{7,6},{8,9},{9,8},{10,11... | collective-permute-start | bytes 208904 | tf_op jit(solution)/shard_map/ppermute | solution.py:417

commit v8 on v7

--- a/solution.py
+++ b/solution.py
@@ -124,17 +124,18 @@
 
 
 def halo_kernel(
-    place_ref, table_ref, own_ref, halo_ref, mine_ref, theirs_ref, gram_ref, turned_ref,
-    parts_ref, cross_ref, sent_ref, applied_ref,
+    count, table_ref, own_ref, halo_ref, mine_ref, theirs_ref, gram_ref, turned_ref,
+    applied_ref, cross_ref, sent_ref,
 ):
     ny, nz, width = own_ref.shape
     mine = quarter_squares(mine_ref[...], table_ref[...])
     theirs = quarter_squares(theirs_ref[...], table_ref[...])
-    ahead_first = place_ref[0] == place_ref[1] % 2
+    row = lax.axis_index("rows")
+    ahead_first = lax.axis_index("cols") == row % 2
     after = jnp.where(ahead_first, mine, theirs)
     before = jnp.where(ahead_first, theirs, mine)
-    after = jnp.where(place_ref[1] < place_ref[2] - 1, after, 0.0)
-    before = jnp.where(place_ref[1] > 0, before, 0.0)
+    after = jnp.where(row < count - 1, after, 0.0)
+    before = jnp.where(row > 0, before, 0.0)
     around = after + before
     after = 2.0 * after
     for y in range(ny):
@@ -142,9 +143,8 @@
             around[:, y : y + 1] * own_ref[y] - after[:, y : y + 1] * halo_ref[y]
         )
     parts = laid(split(applied_ref[...], 3), THREE, 1, 0)
-    parts_ref[...] = parts
     half = width // 2
-    first = place_ref[0] == 0
+    first = lax.axis_index("cols") == 0
     cross = gram_ref[width:, :] + jnp.dot(
         turned_ref[width:, :], parts, preferred_element_type=jnp.float32
     )
@@ -153,11 +153,13 @@
     sent_ref[...] = jnp.where(first, cross[half:], cross[:half])
 
 
-def own_kernel(gram_ref, turned_ref, parts_ref, packed_ref):
-    width = parts_ref.shape[1]
+def own_kernel(gram_ref, turned_ref, applied_ref, packed_ref):
+    width = applied_ref.shape[1]
     half = width // 2
     own = gram_ref[:width, :] + jnp.dot(
-        turned_ref[:width, :], parts_ref[...], preferred_element_type=jnp.float32
+        turned_ref[:width, :],
+        laid(split(applied_ref[...], 3), THREE, 1, 0),
+        preferred_element_type=jnp.float32,
     )
     own = 0.5 * (own + own.T)
     row = lax.broadcasted_iota(jnp.int32, (half, width), 0)
@@ -203,11 +205,11 @@
 
 
 def tournament_kernel(
-    meets, turns, place_ref, mine_ref, theirs_ref, code_ref, own_ref, other_ref, rotated_ref, sigma_ref
+    meets, turns, mine_ref, theirs_ref, code_ref, own_ref, other_ref, rotated_ref, sigma_ref
 ):
     n = own_ref.shape[2]
     h = n // 2
-    side = place_ref[0] == 0
+    side = lax.axis_index("cols") == 0
     mine, theirs = mine_ref[...], theirs_ref[...]
     zero_side = jnp.where(side, mine, theirs)
     one_side = jnp.where(side, theirs, mine)
@@ -352,10 +354,6 @@
     labels = labels[0].T
     halo = lax.ppermute(own, "rows", [(i + 2, i) for i in range(count - 2)])
     other = lax.ppermute(own, "cols", swap)
-    place = jnp.stack(
-        [lax.axis_index("cols"), lax.axis_index("rows"), jnp.asarray(count, jnp.int32)]
-    ).astype(jnp.int32)
-
     code = pl.pallas_call(
         code_kernel,
         out_shape=jax.ShapeDtypeStruct((pairing.shape[0] * pairing.shape[1], width), jnp.int32),
@@ -389,18 +387,17 @@
     )(*[pltpu.with_memory_space_constraint(value, pltpu.HBM) for value in (conductivity, own, labels)], other)
     beside, table = lax.optimization_barrier((beside, table))
     across = lax.ppermute(beside, "cols", swap)
-    parts, cross, sent = pl.pallas_call(
-        halo_kernel,
+    applied, cross, sent = pl.pallas_call(
+        functools.partial(halo_kernel, count),
         out_shape=(
-            jax.ShapeDtypeStruct((len(THREE) * cells, width), jnp.bfloat16),
+            jax.ShapeDtypeStruct((cells, width), jnp.float32),
             jax.ShapeDtypeStruct((half, width), jnp.float32),
             jax.ShapeDtypeStruct((half, width), jnp.float32),
         ),
-        in_specs=[SMEM] + [VMEM] * 7,
+        in_specs=[VMEM] * 7,
         out_specs=[VMEM] * 3,
-        scratch_shapes=[pltpu.VMEM((cells, width), jnp.float32)],
         compiler_params=PARAMS,
-    )(place, table, own, halo, beside, across, gram, turned)
+    )(table, own, halo, beside, across, gram, turned)
     received = lax.ppermute(sent, "cols", swap)
     packed = pl.pallas_call(
         own_kernel,
@@ -408,7 +405,7 @@
         in_specs=[VMEM] * 3,
         out_specs=VMEM,
         compiler_params=PARAMS,
-    )(gram, turned, parts)
+    )(gram, turned, applied)
     share = jnp.concatenate([packed, cross + received], axis=0)
     apart = 1
     while apart < count:
@@ -421,10 +418,10 @@
             jax.ShapeDtypeStruct((ny, nz, width), jnp.float32),
             jax.ShapeDtypeStruct((1, width), jnp.float32),
         ),
-        in_specs=[SMEM] + [VMEM] * 5,
+        in_specs=[VMEM] * 5,
         out_specs=[VMEM] * 2,
         compiler_params=PARAMS,
-    )(place, share, theirs, code, own, other)
+    )(share, theirs, code, own, other)
     return rotated.reshape(snapshots.shape), sigma.reshape(width)
 
 

time: 37.1 us -> 36.1 us (0.973)
  Pallas kernels: 11.8 us -> 10.7 us
    pallas_call x1, Pallas kernels: 7.3 us -> 6.76 us  [shards(): pl.pallas_call(functools.partial(tournament_kernel, pairing.shape[0], pai...]
    pallas_call x1, Pallas kernels: 1.11 us -> 0.58 us  [shards(): pl.pallas_call(functools.partial(halo_kernel, count), out_shape=(jax.Shap...]
where the time goes in v8:
time: 36.1 us; the launch traced here: 35.9 us
  starting transfers between devices  12.7 us (35%)
  waiting for transfers between devices  11.7 us (32%)
  Pallas kernels  10.7 us (30%)
  between operations  0.74 us (2%)
    ppermute x3, waiting for transfers between devices, shards(): lax.ppermute(share, 'rows', [(i, i ^ apart) for i in range(count)])  8.13 us
    pallas_call x1, Pallas kernels, shards(): pl.pallas_call(functools.partial(tournament_kernel, pairing.shape[0], pai...  6.76 us
    ppermute x3, starting transfers between devices, shards(): lax.ppermute(share, 'rows', [(i, i ^ apart) for i in range(count)])  6.26 us
    ppermute x1, starting transfers between devices, shards(): lax.ppermute(labels, ('rows', 'cols'), [(2 * i, 2 * (i ^ 1)) for i in ran...  4.42 us
    ppermute x1, waiting for transfers between devices, shards(): halo = lax.ppermute(own, 'rows', [(i + 2, i) for i in range(count - 2)])  2.64 us
    pallas_call x1, Pallas kernels, shards(): pl.pallas_call(local_kernel, out_shape=(jax.ShapeDtypeStruct((2 * width,...  1.87 us
    ppermute x1, starting transfers between devices, shards(): halo = lax.ppermute(own, 'rows', [(i + 2, i) for i in range(count - 2)])  1.28 us
    pallas_call x1, Pallas kernels, shards(): pl.pallas_call(code_kernel, out_shape=jax.ShapeDtypeStruct((pairing.shape...  1.07 us
  transfers between devices with their start and end apart: 9, of which 6 were waited for; matrix products, arithmetic and copies ran while one was open for 0% of the time, Pallas kernels for 9%

profile of v8, /device:TPU:0, one launch (start us, length us, event | category | flops | bytes accessed | tf_op | source)
XLA Modules:
  0.0 35.9 jit_solution(7692135876920870781)
XLA Ops:
  0.6 0.5 %collective-permute-start = (f32[24,16,128]{2,1,0:T(8,128)}, f32[24,16,128]{2,1,0:T(8,128)S(1)}, u32[]{:S(2)}, u32[]{:S(2)}) collective-permute-start(f32[24,16,128]{2,1,0:T(8,128)} %bitcast.6), channel_id=1, source_target_pairs={{0,1},{1,0},{2,3},{3,2},{4,5},{5,4},{6,7},{7,6},{8,9},{9,8},{10,11... | collective-permute-start | bytes 589832 | tf_op jit(solution)/shard_map/ppermute | solution.py:356
  1.1 1.3 %collective-permute-start.2 = (f32[24,16,128]{2,1,0:T(8,128)}, f32[24,16,128]{2,1,0:T(8,128)S(1)}, u32[]{:S(2)}, u32[]{:S(2)}) collective-permute-start(f32[24,16,128]{2,1,0:T(8,128)} %bitcast.7), channel_id=1, source_target_pairs={{4,0},{6,2},{8,4},{10,6},{12,8},{14,10},{5,1},{7,3},{9,5},{11,7},{... | collective-permute-start | bytes 589832 | tf_op jit(solution)/shard_map/ppermute | solution.py:355
  2.4 4.4 %collective-permute-start.1 = (s32[16,24]{1,0:T(8,128)}, s32[16,24]{1,0:T(8,128)S(1)}, u32[]{:S(2)}, u32[]{:S(2)}) collective-permute-start(s32[16,24]{1,0:T(8,128)} %bitcast.9), channel_id=1, source_target_pairs={{0,2},{2,0},{4,6},{6,4},{8,10},{10,8},{12,14},{14,12},{3,5},{5,3},... | collective-permute-start | bytes 4616 | tf_op jit(solution)/shard_map/ppermute | solution.py:364
  6.9 0.0 collective-permute-done.other_ref
  6.9 1.9 %shard_map.59 = (f32[256,128]{1,0:T(8,128)S(1)}, bf16[256,2304]{1,0:T(8,128)(2,1)S(1)}, f32[24,16,128]{2,1,0:T(8,128)S(1)}, f32[8,128]{1,0:T(8,128)S(1)}) custom-call(f32[8]{0:T(128)} %conductivity_ref.1, f32[24,16,128]{2,1,0:T(8,128)} %bitcast.8, s32[16,24]{1,0:T(8,128)} %bitcast.10, f32[24,16,128]{2,1,0:T(8,128)S(1)} %collective-permute-done.other_ref), custom_call_target="tpu_custom_call" | custom-call | tf_op jit(solution)/shard_map/pallas_call | solution.py:370
  8.7 0.0 collective-permute-done.1.mine_ref
  8.8 0.1 collective-permute-start.3
  8.8 2.6 %collective-permute-done.2.halo_ref = f32[24,16,128]{2,1,0:T(8,128)S(1)} collective-permute-done((f32[24,16,128]{2,1,0:T(8,128)}, f32[24,16,128]{2,1,0:T(8,128)S(1)}, u32[]{:S(2)}, u32[]{:S(2)}) %collective-permute-start.2) | collective-permute-done | bytes 196640 | tf_op jit(solution)/shard_map/ppermute | solution.py:355
  11.5 0.0 collective-permute-done.3.theirs_ref
  11.5 0.6 %shard_map.60 = (f32[384,128]{1,0:T(8,128)S(1)}, f32[64,128]{1,0:T(8,128)S(1)}, f32[64,128]{1,0:T(8,128)S(1)}) custom-call(f32[8,128]{1,0:T(8,128)S(1)} %get-tuple-element.16.table_ref, f32[24,16,128]{2,1,0:T(8,128)S(1)} %get-tuple-element.17.own_ref, f32[24,16,128]{2,1,0:T(8,128)S(1)} %collective-permute-done.2.halo_ref, ...), custom_call_target="tpu_custom_call" | custom-call | tf_op jit(solution)/shard_map/pallas_call | solution.py:390
  12.1 0.1 collective-permute-start.4
  12.1 0.0 copy-start
  12.2 0.5 %shard_map.61 = f32[72,128]{1,0:T(8,128)S(1)} custom-call(f32[256,128]{1,0:T(8,128)S(1)} %get-tuple-element.13.gram_ref, bf16[256,2304]{1,0:T(8,128)(2,1)S(1)} %get-tuple-element.14.turned_ref, f32[384,128]{1,0:T(8,128)S(1)} %get-tuple-element.19.applied_ref), custom_call_target="tpu_custom_call" | custom-call | tf_op jit(solution)/shard_map/pallas_call | solution.py:402
  12.6 0.7 %collective-permute-done.4 = f32[64,128]{1,0:T(8,128)S(1)} collective-permute-done((f32[64,128]{1,0:T(8,128)S(1)}, f32[64,128]{1,0:T(8,128)S(1)}, u32[]{:S(2)}, u32[]{:S(2)}) %collective-permute-start.4) | collective-permute-done | bytes 32800 | tf_op jit(solution)/shard_map/ppermute | solution.py:401
  13.4 2.1 %collective-permute-start.5 = (f32[136,128]{1,0:T(8,128)S(1)}, f32[136,128]{1,0:T(8,128)S(1)}, u32[]{:S(2)}, u32[]{:S(2)}) collective-permute-start(f32[136,128]{1,0:T(8,128)S(1)} %pad_maximum_fusion), channel_id=1, source_target_pairs={{0,2},{2,0},{4,6},{6,4},{8,10},{10,8},{12,14},{14,12},{1,3},{3,1},... | collective-permute-start | bytes 208904 | tf_op jit(solution)/shard_map/ppermute | solution.py:412
  15.4 2.7 %collective-permute-done.5 = f32[136,128]{1,0:T(8,128)S(1)} collective-permute-done((f32[136,128]{1,0:T(8,128)S(1)}, f32[136,128]{1,0:T(8,128)S(1)}, u32[]{:S(2)}, u32[]{:S(2)}) %collective-permute-start.5) | collective-permute-done | bytes 69664 | tf_op jit(solution)/shard_map/ppermute | solution.py:412
  18.1 1.6 %collective-permute-start.6 = (f32[136,128]{1,0:T(8,128)S(1)}, f32[136,128]{1,0:T(8,128)S(1)}, u32[]{:S(2)}, u32[]{:S(2)}) collective-permute-start(f32[136,128]{1,0:T(8,128)S(1)} %fusion), channel_id=1, source_target_pairs={{0,4},{2,6},{4,0},{6,2},{8,12},{10,14},{12,8},{14,10},{1,5},{3,7},... | collective-permute-start | bytes 208904 | tf_op jit(solution)/shard_map/ppermute | solution.py:412
  19.7 2.8 %collective-permute-done.6 = f32[136,128]{1,0:T(8,128)S(1)} collective-permute-done((f32[136,128]{1,0:T(8,128)S(1)}, f32[136,128]{1,0:T(8,128)S(1)}, u32[]{:S(2)}, u32[]{:S(2)}) %collective-permute-start.6) | collective-permute-done | bytes 69664 | tf_op jit(solution)/shard_map/ppermute | solution.py:412
  22.5 2.6 %collective-permute-start.7 = (f32[136,128]{1,0:T(8,128)S(1)}, f32[136,128]{1,0:T(8,128)S(1)}, u32[]{:S(2)}, u32[]{:S(2)}) collective-permute-start(f32[136,128]{1,0:T(8,128)S(1)} %add.14), channel_id=1, source_target_pairs={{0,8},{2,10},{4,12},{6,14},{8,0},{10,2},{12,4},{14,6},{1,9},{3,11}... | collective-permute-start | bytes 208904 | tf_op jit(solution)/shard_map/ppermute | solution.py:412
  25.1 2.7 %collective-permute-done.7 = f32[136,128]{1,0:T(8,128)S(1)} collective-permute-done((f32[136,128]{1,0:T(8,128)S(1)}, f32[136,128]{1,0:T(8,128)S(1)}, u32[]{:S(2)}, u32[]{:S(2)}) %collective-permute-start.7) | collective-permute-done | bytes 69664 | tf_op jit(solution)/shard_map/ppermute | solution.py:412
  27.8 0.1 collective-permute-start.8
  27.9 1.1 %shard_map.62.code_ref = s32[24,128]{1,0:T(8,128)S(1)} custom-call(s32[6,4,128]{2,1,0:T(4,128)S(1)} %copy-done), custom_call_target="tpu_custom_call" | custom-call | tf_op jit(solution)/shard_map/pallas_call | solution.py:357
  28.9 0.2 collective-permute-done.8.theirs_ref
  29.1 6.8 %shard_map.63 = (f32[24,16,128]{2,1,0:T(8,128)}, f32[1,128]{1,0:T(1,128)}) custom-call(f32[136,128]{1,0:T(8,128)S(1)} %add.15.mine_ref, f32[136,128]{1,0:T(8,128)S(1)} %collective-permute-done.8.theirs_ref, s32[24,128]{1,0:T(8,128)S(1)} %shard_map.62.code_ref, f32[24,16,128]{2,1,0:T(8,128)S(1)} %get-tuple-element.17.own_ref, ...), custom_call_target="tpu_custom_call" | custom-call | tf_op jit(solution)/shard_map/pallas_call | solution.py:415
  (6 shorter events, 0.0 us)
Async XLA Ops:
  0.6 6.2 %collective-permute-start = (f32[24,16,128]{2,1,0:T(8,128)}, f32[24,16,128]{2,1,0:T(8,128)S(1)}, u32[]{:S(2)}, u32[]{:S(2)}) collective-permute-start(f32[24,16,128]{2,1,0:T(8,128)} %bitcast.6), channel_id=1, source_target_pairs={{0,1},{1,0},{2,3},{3,2},{4,5},{5,4},{6,7},{7,6},{8,9},{9,8},{10,11... | collective-permute-start | bytes 589832 | tf_op jit(solution)/shard_map/ppermute | solution.py:356
  1.1 10.3 %collective-permute-start.2 = (f32[24,16,128]{2,1,0:T(8,128)}, f32[24,16,128]{2,1,0:T(8,128)S(1)}, u32[]{:S(2)}, u32[]{:S(2)}) collective-permute-start(f32[24,16,128]{2,1,0:T(8,128)} %bitcast.7), channel_id=1, source_target_pairs={{4,0},{6,2},{8,4},{10,6},{12,8},{14,10},{5,1},{7,3},{9,5},{11,7},{... | collective-permute-start | bytes 589832 | tf_op jit(solution)/shard_map/ppermute | solution.py:355
  2.4 6.3 %collective-permute-start.1 = (s32[16,24]{1,0:T(8,128)}, s32[16,24]{1,0:T(8,128)S(1)}, u32[]{:S(2)}, u32[]{:S(2)}) collective-permute-start(s32[16,24]{1,0:T(8,128)} %bitcast.9), channel_id=1, source_target_pairs={{0,2},{2,0},{4,6},{6,4},{8,10},{10,8},{12,14},{14,12},{3,5},{5,3},... | collective-permute-start | bytes 4616 | tf_op jit(solution)/shard_map/ppermute | solution.py:364
  8.8 2.7 %collective-permute-start.3 = (s32[16,24]{1,0:T(8,128)S(1)}, s32[16,24]{1,0:T(8,128)S(1)}, u32[]{:S(2)}, u32[]{:S(2)}) collective-permute-start(s32[16,24]{1,0:T(8,128)S(1)} %collective-permute-done.1.mine_ref), channel_id=1, source_target_pairs={{0,1},{1,0},{2,3},{3,2},{4,5},{5,4},{6,7},{7,6},{8,9},{9,8},{10,11... | collective-permute-start | bytes 4616 | tf_op jit(solution)/shard_map/ppermute | solution.py:389
  12.1 1.3 %collective-permute-start.4 = (f32[64,128]{1,0:T(8,128)S(1)}, f32[64,128]{1,0:T(8,128)S(1)}, u32[]{:S(2)}, u32[]{:S(2)}) collective-permute-start(f32[64,128]{1,0:T(8,128)S(1)} %get-tuple-element.21), channel_id=1, source_target_pairs={{0,1},{1,0},{2,3},{3,2},{4,5},{5,4},{6,7},{7,6},{8,9},{9,8},{10,11... | collective-permute-start | bytes 98312 | tf_op jit(solution)/shard_map/ppermute | solution.py:401
  12.1 15.7 %copy-start = (s32[6,4,128]{2,1,0:T(4,128)S(1)}, s32[6,4,128]{2,1,0:T(4,128)}, u32[]{:S(2)}) copy-start(s32[6,4,128]{2,1,0:T(4,128)} %pairing_ref.1) | copy-start | bytes 36868
  13.4 4.7 %collective-permute-start.5 = (f32[136,128]{1,0:T(8,128)S(1)}, f32[136,128]{1,0:T(8,128)S(1)}, u32[]{:S(2)}, u32[]{:S(2)}) collective-permute-start(f32[136,128]{1,0:T(8,128)S(1)} %pad_maximum_fusion), channel_id=1, source_target_pairs={{0,2},{2,0},{4,6},{6,4},{8,10},{10,8},{12,14},{14,12},{1,3},{3,1},... | collective-permute-start | bytes 208904 | tf_op jit(solution)/shard_map/ppermute | solution.py:412
  18.1 4.4 %collective-permute-start.6 = (f32[136,128]{1,0:T(8,128)S(1)}, f32[136,128]{1,0:T(8,128)S(1)}, u32[]{:S(2)}, u32[]{:S(2)}) collective-permute-start(f32[136,128]{1,0:T(8,128)S(1)} %fusion), channel_id=1, source_target_pairs={{0,4},{2,6},{4,0},{6,2},{8,12},{10,14},{12,8},{14,10},{1,5},{3,7},... | collective-permute-start | bytes 208904 | tf_op jit(solution)/shard_map/ppermute | solution.py:412
  22.5 5.3 %collective-permute-start.7 = (f32[136,128]{1,0:T(8,128)S(1)}, f32[136,128]{1,0:T(8,128)S(1)}, u32[]{:S(2)}, u32[]{:S(2)}) collective-permute-start(f32[136,128]{1,0:T(8,128)S(1)} %add.14), channel_id=1, source_target_pairs={{0,8},{2,10},{4,12},{6,14},{8,0},{10,2},{12,4},{14,6},{1,9},{3,11}... | collective-permute-start | bytes 208904 | tf_op jit(solution)/shard_map/ppermute | solution.py:412
  27.8 1.3 %collective-permute-start.8 = (f32[136,128]{1,0:T(8,128)S(1)}, f32[136,128]{1,0:T(8,128)S(1)}, u32[]{:S(2)}, u32[]{:S(2)}) collective-permute-start(f32[136,128]{1,0:T(8,128)S(1)} %add.15.mine_ref), channel_id=1, source_target_pairs={{0,1},{1,0},{2,3},{3,2},{4,5},{5,4},{6,7},{7,6},{8,9},{9,8},{10,11... | collective-permute-start | bytes 208904 | tf_op jit(solution)/shard_map/ppermute | solution.py:414

commit v9 on v8

--- a/solution.py
+++ b/solution.py
@@ -239,7 +239,7 @@
             told = jnp.broadcast_to(code_ref[index : index + 1, :], (8, n))
             other_way = pltpu.roll(told, h, 1)
             for d in range(2):
-                partner = (other_way % n) ^ h if swapped[d] else told % n
+                partner = (other_way & (n - 1)) ^ h if swapped[d] else told & (n - 1)
                 first = (other_way if swapped[d] else told) >= n
                 if turn == 0:
                     coupling = [
@@ -407,10 +407,9 @@
         compiler_params=PARAMS,
     )(gram, turned, applied)
     share = jnp.concatenate([packed, cross + received], axis=0)
-    apart = 1
-    while apart < count:
+    steps = [2**k for k in range(count.bit_length() - 1)]
+    for apart in steps[:2][::-1] + steps[2:]:
         share = share + lax.ppermute(share, "rows", [(i, i ^ apart) for i in range(count)])
-        apart *= 2
     theirs = lax.ppermute(share, "cols", swap)
     rotated, sigma = pl.pallas_call(
         functools.partial(tournament_kernel, pairing.shape[0], pairing.shape[1]),

time: 36.1 us -> 35.8 us (level)
  waiting for transfers between devices: 11.7 us -> 11 us
  starting transfers between devices: 12.7 us -> 13.1 us
    ppermute x3, waiting for transfers between devices: 8.13 us -> 7.41 us  [shards(): lax.ppermute(share, 'rows', [(i, i ^ apart) for i in range(count)])]
    ppermute x3, starting transfers between devices: 6.26 us -> 6.7 us  [shards(): lax.ppermute(share, 'rows', [(i, i ^ apart) for i in range(count)])]
  transfers between devices with their start and end apart: 9 -> 9, of which waited for: 6 -> 6; matrix products, arithmetic and copies ran while one was open for 0% -> 0% of each run, Pallas kernels for 9% -> 10%
where the time goes in v9:
time: 35.8 us; the launch traced here: 35.6 us
  starting transfers between devices  13.1 us (37%)
  waiting for transfers between devices  11 us (31%)
  Pallas kernels  10.7 us (30%)
  between operations  0.74 us (2%)
    ppermute x3, waiting for transfers between devices, shards(): lax.ppermute(share, 'rows', [(i, i ^ apart) for i in range(count)])  7.41 us
    pallas_call x1, Pallas kernels, shards(): pl.pallas_call(functools.partial(tournament_kernel, pairing.shape[0], pai...  6.76 us
    ppermute x3, starting transfers between devices, shards(): lax.ppermute(share, 'rows', [(i, i ^ apart) for i in range(count)])  6.7 us
    ppermute x1, starting transfers between devices, shards(): lax.ppermute(labels, ('rows', 'cols'), [(2 * i, 2 * (i ^ 1)) for i in ran...  4.42 us
    ppermute x1, waiting for transfers between devices, shards(): halo = lax.ppermute(own, 'rows', [(i + 2, i) for i in range(count - 2)])  2.64 us
    pallas_call x1, Pallas kernels, shards(): pl.pallas_call(local_kernel, out_shape=(jax.ShapeDtypeStruct((2 * width,...  1.87 us
    ppermute x1, starting transfers between devices, shards(): halo = lax.ppermute(own, 'rows', [(i + 2, i) for i in range(count - 2)])  1.28 us
    pallas_call x1, Pallas kernels, shards(): pl.pallas_call(code_kernel, out_shape=jax.ShapeDtypeStruct((pairing.shape...  1.07 us
  transfers between devices with their start and end apart: 9, of which 6 were waited for; matrix products, arithmetic and copies ran while one was open for 0% of the time, Pallas kernels for 10%

profile of v9, /device:TPU:0, one launch (start us, length us, event | category | flops | bytes accessed | tf_op | source)
XLA Modules:
  0.0 35.6 jit_solution(1551722291500595237)
XLA Ops:
  0.6 0.5 %collective-permute-start = (f32[24,16,128]{2,1,0:T(8,128)}, f32[24,16,128]{2,1,0:T(8,128)S(1)}, u32[]{:S(2)}, u32[]{:S(2)}) collective-permute-start(f32[24,16,128]{2,1,0:T(8,128)} %bitcast.6), channel_id=1, source_target_pairs={{0,1},{1,0},{2,3},{3,2},{4,5},{5,4},{6,7},{7,6},{8,9},{9,8},{10,11... | collective-permute-start | bytes 589832 | tf_op jit(solution)/shard_map/ppermute | solution.py:356
  1.1 1.3 %collective-permute-start.2 = (f32[24,16,128]{2,1,0:T(8,128)}, f32[24,16,128]{2,1,0:T(8,128)S(1)}, u32[]{:S(2)}, u32[]{:S(2)}) collective-permute-start(f32[24,16,128]{2,1,0:T(8,128)} %bitcast.7), channel_id=1, source_target_pairs={{4,0},{6,2},{8,4},{10,6},{12,8},{14,10},{5,1},{7,3},{9,5},{11,7},{... | collective-permute-start | bytes 589832 | tf_op jit(solution)/shard_map/ppermute | solution.py:355
  2.4 4.4 %collective-permute-start.1 = (s32[16,24]{1,0:T(8,128)}, s32[16,24]{1,0:T(8,128)S(1)}, u32[]{:S(2)}, u32[]{:S(2)}) collective-permute-start(s32[16,24]{1,0:T(8,128)} %bitcast.9), channel_id=1, source_target_pairs={{0,2},{2,0},{4,6},{6,4},{8,10},{10,8},{12,14},{14,12},{3,5},{5,3},... | collective-permute-start | bytes 4616 | tf_op jit(solution)/shard_map/ppermute | solution.py:364
  6.9 0.0 collective-permute-done.other_ref
  6.9 1.9 %shard_map.59 = (f32[256,128]{1,0:T(8,128)S(1)}, bf16[256,2304]{1,0:T(8,128)(2,1)S(1)}, f32[24,16,128]{2,1,0:T(8,128)S(1)}, f32[8,128]{1,0:T(8,128)S(1)}) custom-call(f32[8]{0:T(128)} %conductivity_ref.1, f32[24,16,128]{2,1,0:T(8,128)} %bitcast.8, s32[16,24]{1,0:T(8,128)} %bitcast.10, f32[24,16,128]{2,1,0:T(8,128)S(1)} %collective-permute-done.other_ref), custom_call_target="tpu_custom_call" | custom-call | tf_op jit(solution)/shard_map/pallas_call | solution.py:370
  8.7 0.0 collective-permute-done.1.mine_ref
  8.8 0.1 collective-permute-start.3
  8.8 2.6 %collective-permute-done.2.halo_ref = f32[24,16,128]{2,1,0:T(8,128)S(1)} collective-permute-done((f32[24,16,128]{2,1,0:T(8,128)}, f32[24,16,128]{2,1,0:T(8,128)S(1)}, u32[]{:S(2)}, u32[]{:S(2)}) %collective-permute-start.2) | collective-permute-done | bytes 196640 | tf_op jit(solution)/shard_map/ppermute | solution.py:355
  11.5 0.0 collective-permute-done.3.theirs_ref
  11.5 0.6 %shard_map.60 = (f32[384,128]{1,0:T(8,128)S(1)}, f32[64,128]{1,0:T(8,128)S(1)}, f32[64,128]{1,0:T(8,128)S(1)}) custom-call(f32[8,128]{1,0:T(8,128)S(1)} %get-tuple-element.16.table_ref, f32[24,16,128]{2,1,0:T(8,128)S(1)} %get-tuple-element.17.own_ref, f32[24,16,128]{2,1,0:T(8,128)S(1)} %collective-permute-done.2.halo_ref, ...), custom_call_target="tpu_custom_call" | custom-call | tf_op jit(solution)/shard_map/pallas_call | solution.py:390
  12.1 0.1 collective-permute-start.4
  12.1 0.0 copy-start
  12.2 0.5 %shard_map.61 = f32[72,128]{1,0:T(8,128)S(1)} custom-call(f32[256,128]{1,0:T(8,128)S(1)} %get-tuple-element.13.gram_ref, bf16[256,2304]{1,0:T(8,128)(2,1)S(1)} %get-tuple-element.14.turned_ref, f32[384,128]{1,0:T(8,128)S(1)} %get-tuple-element.19.applied_ref), custom_call_target="tpu_custom_call" | custom-call | tf_op jit(solution)/shard_map/pallas_call | solution.py:402
  12.6 0.7 %collective-permute-done.4 = f32[64,128]{1,0:T(8,128)S(1)} collective-permute-done((f32[64,128]{1,0:T(8,128)S(1)}, f32[64,128]{1,0:T(8,128)S(1)}, u32[]{:S(2)}, u32[]{:S(2)}) %collective-permute-start.4) | collective-permute-done | bytes 32800 | tf_op jit(solution)/shard_map/ppermute | solution.py:401
  13.4 1.8 %collective-permute-start.5 = (f32[136,128]{1,0:T(8,128)S(1)}, f32[136,128]{1,0:T(8,128)S(1)}, u32[]{:S(2)}, u32[]{:S(2)}) collective-permute-start(f32[136,128]{1,0:T(8,128)S(1)} %pad_maximum_fusion), channel_id=1, source_target_pairs={{0,4},{2,6},{4,0},{6,2},{8,12},{10,14},{12,8},{14,10},{1,5},{3,7},... | collective-permute-start | bytes 208904 | tf_op jit(solution)/shard_map/ppermute | solution.py:412
  15.2 2.6 %collective-permute-done.5 = f32[136,128]{1,0:T(8,128)S(1)} collective-permute-done((f32[136,128]{1,0:T(8,128)S(1)}, f32[136,128]{1,0:T(8,128)S(1)}, u32[]{:S(2)}, u32[]{:S(2)}) %collective-permute-start.5) | collective-permute-done | bytes 69664 | tf_op jit(solution)/shard_map/ppermute | solution.py:412
  17.7 2.2 %collective-permute-start.6 = (f32[136,128]{1,0:T(8,128)S(1)}, f32[136,128]{1,0:T(8,128)S(1)}, u32[]{:S(2)}, u32[]{:S(2)}) collective-permute-start(f32[136,128]{1,0:T(8,128)S(1)} %fusion), channel_id=1, source_target_pairs={{0,2},{2,0},{4,6},{6,4},{8,10},{10,8},{12,14},{14,12},{1,3},{3,1},... | collective-permute-start | bytes 208904 | tf_op jit(solution)/shard_map/ppermute | solution.py:412
  19.9 2.3 %collective-permute-done.6 = f32[136,128]{1,0:T(8,128)S(1)} collective-permute-done((f32[136,128]{1,0:T(8,128)S(1)}, f32[136,128]{1,0:T(8,128)S(1)}, u32[]{:S(2)}, u32[]{:S(2)}) %collective-permute-start.6) | collective-permute-done | bytes 69664 | tf_op jit(solution)/shard_map/ppermute | solution.py:412
  22.2 2.7 %collective-permute-start.7 = (f32[136,128]{1,0:T(8,128)S(1)}, f32[136,128]{1,0:T(8,128)S(1)}, u32[]{:S(2)}, u32[]{:S(2)}) collective-permute-start(f32[136,128]{1,0:T(8,128)S(1)} %add.14), channel_id=1, source_target_pairs={{0,8},{2,10},{4,12},{6,14},{8,0},{10,2},{12,4},{14,6},{1,9},{3,11}... | collective-permute-start | bytes 208904 | tf_op jit(solution)/shard_map/ppermute | solution.py:412
  24.9 2.5 %collective-permute-done.7 = f32[136,128]{1,0:T(8,128)S(1)} collective-permute-done((f32[136,128]{1,0:T(8,128)S(1)}, f32[136,128]{1,0:T(8,128)S(1)}, u32[]{:S(2)}, u32[]{:S(2)}) %collective-permute-start.7) | collective-permute-done | bytes 69664 | tf_op jit(solution)/shard_map/ppermute | solution.py:412
  27.5 0.1 collective-permute-start.8
  27.6 1.1 %shard_map.62.code_ref = s32[24,128]{1,0:T(8,128)S(1)} custom-call(s32[6,4,128]{2,1,0:T(4,128)S(1)} %copy-done), custom_call_target="tpu_custom_call" | custom-call | tf_op jit(solution)/shard_map/pallas_call | solution.py:357
  28.7 0.2 collective-permute-done.8.theirs_ref
  28.8 6.8 %shard_map.63 = (f32[24,16,128]{2,1,0:T(8,128)}, f32[1,128]{1,0:T(1,128)}) custom-call(f32[136,128]{1,0:T(8,128)S(1)} %add.15.mine_ref, f32[136,128]{1,0:T(8,128)S(1)} %collective-permute-done.8.theirs_ref, s32[24,128]{1,0:T(8,128)S(1)} %shard_map.62.code_ref, f32[24,16,128]{2,1,0:T(8,128)S(1)} %get-tuple-element.17.own_ref, ...), custom_call_target="tpu_custom_call" | custom-call | tf_op jit(solution)/shard_map/pallas_call | solution.py:414
  (6 shorter events, 0.0 us)
Async XLA Ops:
  0.6 6.2 %collective-permute-start = (f32[24,16,128]{2,1,0:T(8,128)}, f32[24,16,128]{2,1,0:T(8,128)S(1)}, u32[]{:S(2)}, u32[]{:S(2)}) collective-permute-start(f32[24,16,128]{2,1,0:T(8,128)} %bitcast.6), channel_id=1, source_target_pairs={{0,1},{1,0},{2,3},{3,2},{4,5},{5,4},{6,7},{7,6},{8,9},{9,8},{10,11... | collective-permute-start | bytes 589832 | tf_op jit(solution)/shard_map/ppermute | solution.py:356
  1.1 10.3 %collective-permute-start.2 = (f32[24,16,128]{2,1,0:T(8,128)}, f32[24,16,128]{2,1,0:T(8,128)S(1)}, u32[]{:S(2)}, u32[]{:S(2)}) collective-permute-start(f32[24,16,128]{2,1,0:T(8,128)} %bitcast.7), channel_id=1, source_target_pairs={{4,0},{6,2},{8,4},{10,6},{12,8},{14,10},{5,1},{7,3},{9,5},{11,7},{... | collective-permute-start | bytes 589832 | tf_op jit(solution)/shard_map/ppermute | solution.py:355
  2.4 6.3 %collective-permute-start.1 = (s32[16,24]{1,0:T(8,128)}, s32[16,24]{1,0:T(8,128)S(1)}, u32[]{:S(2)}, u32[]{:S(2)}) collective-permute-start(s32[16,24]{1,0:T(8,128)} %bitcast.9), channel_id=1, source_target_pairs={{0,2},{2,0},{4,6},{6,4},{8,10},{10,8},{12,14},{14,12},{3,5},{5,3},... | collective-permute-start | bytes 4616 | tf_op jit(solution)/shard_map/ppermute | solution.py:364
  8.8 2.7 %collective-permute-start.3 = (s32[16,24]{1,0:T(8,128)S(1)}, s32[16,24]{1,0:T(8,128)S(1)}, u32[]{:S(2)}, u32[]{:S(2)}) collective-permute-start(s32[16,24]{1,0:T(8,128)S(1)} %collective-permute-done.1.mine_ref), channel_id=1, source_target_pairs={{0,1},{1,0},{2,3},{3,2},{4,5},{5,4},{6,7},{7,6},{8,9},{9,8},{10,11... | collective-permute-start | bytes 4616 | tf_op jit(solution)/shard_map/ppermute | solution.py:389
  12.1 1.3 %collective-permute-start.4 = (f32[64,128]{1,0:T(8,128)S(1)}, f32[64,128]{1,0:T(8,128)S(1)}, u32[]{:S(2)}, u32[]{:S(2)}) collective-permute-start(f32[64,128]{1,0:T(8,128)S(1)} %get-tuple-element.21), channel_id=1, source_target_pairs={{0,1},{1,0},{2,3},{3,2},{4,5},{5,4},{6,7},{7,6},{8,9},{9,8},{10,11... | collective-permute-start | bytes 98312 | tf_op jit(solution)/shard_map/ppermute | solution.py:401
  12.1 15.4 %copy-start = (s32[6,4,128]{2,1,0:T(4,128)S(1)}, s32[6,4,128]{2,1,0:T(4,128)}, u32[]{:S(2)}) copy-start(s32[6,4,128]{2,1,0:T(4,128)} %pairing_ref.1) | copy-start | bytes 36868
  13.4 4.4 %collective-permute-start.5 = (f32[136,128]{1,0:T(8,128)S(1)}, f32[136,128]{1,0:T(8,128)S(1)}, u32[]{:S(2)}, u32[]{:S(2)}) collective-permute-start(f32[136,128]{1,0:T(8,128)S(1)} %pad_maximum_fusion), channel_id=1, source_target_pairs={{0,4},{2,6},{4,0},{6,2},{8,12},{10,14},{12,8},{14,10},{1,5},{3,7},... | collective-permute-start | bytes 208904 | tf_op jit(solution)/shard_map/ppermute | solution.py:412
  17.7 4.5 %collective-permute-start.6 = (f32[136,128]{1,0:T(8,128)S(1)}, f32[136,128]{1,0:T(8,128)S(1)}, u32[]{:S(2)}, u32[]{:S(2)}) collective-permute-start(f32[136,128]{1,0:T(8,128)S(1)} %fusion), channel_id=1, source_target_pairs={{0,2},{2,0},{4,6},{6,4},{8,10},{10,8},{12,14},{14,12},{1,3},{3,1},... | collective-permute-start | bytes 208904 | tf_op jit(solution)/shard_map/ppermute | solution.py:412
  22.2 5.3 %collective-permute-start.7 = (f32[136,128]{1,0:T(8,128)S(1)}, f32[136,128]{1,0:T(8,128)S(1)}, u32[]{:S(2)}, u32[]{:S(2)}) collective-permute-start(f32[136,128]{1,0:T(8,128)S(1)} %add.14), channel_id=1, source_target_pairs={{0,8},{2,10},{4,12},{6,14},{8,0},{10,2},{12,4},{14,6},{1,9},{3,11}... | collective-permute-start | bytes 208904 | tf_op jit(solution)/shard_map/ppermute | solution.py:412
  27.5 1.3 %collective-permute-start.8 = (f32[136,128]{1,0:T(8,128)S(1)}, f32[136,128]{1,0:T(8,128)S(1)}, u32[]{:S(2)}, u32[]{:S(2)}) collective-permute-start(f32[136,128]{1,0:T(8,128)S(1)} %add.15.mine_ref), channel_id=1, source_target_pairs={{0,1},{1,0},{2,3},{3,2},{4,5},{5,4},{6,7},{7,6},{8,9},{9,8},{10,11... | collective-permute-start | bytes 208904 | tf_op jit(solution)/shard_map/ppermute | solution.py:413
